TPU v7x, 512 devices: a whole 4x8x8 slice. The times are simulated.
512 devices in a mesh: dp: 32 (over y_lo, z), mp: 16 (over x, y_hi, core).
Axes of the slice: x: 4, y: 8 (y_hi: 2, y_lo: 4; y = y_hi * 4 + y_lo), z: 8, core: 2. Of those that a mesh axis runs over, the one named last changes fastest.
Arguments:
- tokens: bfloat16 [11776, 2048], P('dp', 'mp'), may hold values from -21 to 21, as said below
- cotangent: bfloat16 [11776, 5120], P('dp', 'mp'), may hold values from -8.7576054 to 8.7576054, as said below
- weights: float32 [2, 2048, 5120], P(None, 'dp', 'mp'), may hold values from -14 to 14, as said below
- row_moments: float32 [2, 2048], P(None, 'dp'), may hold values from 0.05 to 2
- col_moments: float32 [2, 5120], P(None, 'mp'), may hold values from 0.05 to 2
Outputs:
- input_grad: bfloat16 [11776, 2048], P('dp', 'mp')
- weight_step: float32 [2, 2048, 5120], P(None, 'dp', 'mp')
- new_rows: float32 [2, 2048], P(None, 'dp')
- new_cols: float32 [2, 5120], P(None, 'mp')
Inputs may be any that keep to these rules, and one draw needn't show every extreme that they name: `tokens`: activations with a different scale for each feature. `cotangent`: gradients with a different scale for each hidden unit. weights of order one with a different scale for each row.
All inputs are finite; a program needn't handle non-finite values.
Results may differ from a plain program's by a relative error of at most 0.029.
Values may be sent and summed in bfloat16 or wider, within the bound.
No kernel may reach another device: no remote copies, remote signals or barrier semaphores. Data moves between devices by JAX's collectives and lax.ppermute only.
A program may use at most 64 MiB of HBM per device.

v0:
```python
import jax
import jax.numpy as jnp
from jax import lax
from jax.sharding import PartitionSpec as P

D = 2048
FF = 5120


def gelu_parts(values):
    cubed_values = values * values * values
    argument = 0.7978845608 * (values + 0.044715 * cubed_values)
    tangent = jnp.tanh(argument)
    gelu_value = 0.5 * values * (1.0 + tangent)
    gelu_slope = 0.5 * (1.0 + tangent) + 0.5 * values * (1.0 - tangent * tangent) * 0.7978845608 * (
        1.0 + 3.0 * 0.044715 * values * values
    )
    return (gelu_value, gelu_slope)


def grad_rows(features_full, hidden_grads, scaling, row_count):
    product = jnp.einsum(
        "td,ktf->dkf", features_full, hidden_grads, preferred_element_type=jnp.float32
    )
    return (product * scaling).reshape(row_count, -1)


def shards(tokens, cotangent, weights, row_moments, col_moments):
    scaling = D ** (-0.5)
    local_rows = weights.shape[1]
    local_cols = weights.shape[2]
    mp_index = lax.axis_index("mp")
    features_full = lax.all_gather(tokens, "mp", axis=1, tiled=True)
    weights_half = weights.astype(jnp.bfloat16)
    weight_full = lax.all_gather(weights_half, "dp", axis=1, tiled=True)
    preact = (
        jnp.einsum("td,kdf->ktf", features_full, weight_full, preferred_element_type=jnp.float32)
        * scaling
    )
    gelu_value, gelu_slope = gelu_parts(preact[0])
    grad_gate = (cotangent * preact[1] * gelu_slope).astype(jnp.bfloat16)
    grad_up = (cotangent * gelu_value).astype(jnp.bfloat16)
    hidden_grads = jnp.stack([grad_gate, grad_up])
    input_term = (
        jnp.einsum("ktf,kdf->td", hidden_grads, weight_full, preferred_element_type=jnp.float32)
        * scaling
    )
    input_grad = lax.psum_scatter(
        input_term.astype(jnp.bfloat16), "mp", scatter_dimension=1, tiled=True
    )
    scattered = lax.psum_scatter(
        grad_rows(features_full, hidden_grads, scaling, local_rows * lax.axis_size("dp")).astype(
            jnp.bfloat16
        ),
        "dp",
        scatter_dimension=0,
        tiled=True,
    ).astype(jnp.float32)
    own_grads = scattered.reshape(local_rows, 2, local_cols).transpose(1, 0, 2)
    col_part = jnp.sum(own_grads * own_grads + 1e-30, axis=1)
    squares = own_grads * own_grads + 1e-30
    row_part = jnp.sum(squares, axis=2)
    weight_squares = jnp.sum(weights * weights, axis=(1, 2))
    row_sum = lax.psum(row_part, "mp")
    col_sum = lax.psum(col_part, "dp")
    new_rows = 0.5 * row_moments + 0.5 * (row_sum / FF)
    new_cols = 0.5 * col_moments + 0.5 * (col_sum / D)
    rows_total = jnp.where(mp_index == 0, jnp.sum(new_rows, axis=1), 0.0)
    rows_summed, weight_total = lax.psum((rows_total, weight_squares), ("dp", "mp"))
    row_level = rows_summed / D
    estimate = new_rows[:, :, None] * new_cols[:, None, :] / row_level[:, None, None]
    update = own_grads * lax.rsqrt(estimate)
    step_scale = jnp.sqrt(weight_total / (D * FF))
    weight_step = step_scale[:, None, None] * update
    return (input_grad, weight_step, new_rows, new_cols)


def solution(mesh):
    return jax.shard_map(
        shards,
        mesh=mesh,
        in_specs=(P("dp", "mp"), P("dp", "mp"), P(None, "dp", "mp"), P(None, "dp"), P(None, "mp")),
        out_specs=(P("dp", "mp"), P(None, "dp", "mp"), P(None, "dp"), P(None, "mp")),
        check_vma=False,
    )
```

profile of v0, /device:TPU:1, one launch (start us, length us, event | category | flops | bytes accessed | tf_op | source)
XLA Modules:
  0.0 717.3 jit_solution(11477825741014486872)
XLA Ops:
  7.2 0.0 all-gather.5.cloned.1.call-start
  7.2 0.7 all-gather.5.cloned.1.call-update
  7.9 0.0 all-gather.3.cloned.1.call-start
  7.9 1.7 multiply_reduce_fusion
  9.7 0.0 all-gather.3.cloned.1.call-update
  9.7 0.0 copy-start
  9.7 0.0 reduce-scatter.7.cloned.1.call-start
  9.8 70.2 %all-gather.5.cloned.1.call-done = bf16[368,2048]{1,0:T(8,128)(2,1)} async-done(((bf16[368,128]{1,0:T(8,128)(2,1)}), bf16[368,2048]{1,0:T(8,128)(2,1)}) %all-gather.5.cloned.1.call-update) | async-done | bytes 1507344 | tf_op jit(solution)/shard_map/all_gather | solution.py:33
  80.0 137.2 %all-gather.3.cloned.1.call-done = bf16[2,2048,320]{2,1,0:T(8,128)(2,1)} async-done(((bf16[2,64,320]{2,1,0:T(8,128)(2,1)}), bf16[2,2048,320]{2,1,0:T(8,128)(2,1)}) %all-gather.3.cloned.1.call-update) | async-done | bytes 2621456 | tf_op jit(solution)/shard_map/all_gather | solution.py:35
  217.2 0.0 copy-start.5
  217.2 4.3 fusion.7
  221.5 0.0 copy-done
  221.5 0.4 fusion.21
  221.9 0.0 copy-done.5
  221.9 1.5 fusion
  223.4 1.6 copy.21
  225.0 0.0 reduce-scatter.7.cloned.1.call-update
  225.0 0.0 reduce-scatter.5.cloned.1.call-start
  225.0 2.9 multiply_convert_fusion
  228.0 0.0 copy-start.4
  228.0 2.6 copy.17
  230.6 0.0 copy-start.3
  230.6 0.0 reduce-scatter.5.cloned.1.call-update
  230.6 99.6 %reduce-scatter.7.cloned.1.call-done = bf16[128,368]{1,0:T(8,128)(2,1)} async-done(((bf16[2048,368]{1,0:T(8,128)(2,1)}), bf16[128,368]{1,0:T(8,128)(2,1)}) %reduce-scatter.7.cloned.1.call-update) | async-done | bytes 94224
  330.2 1.6 copy.22
  331.9 141.3 %reduce-scatter.5.cloned.1.call-done = bf16[64,640]{1,0:T(8,128)(2,1)} async-done(((bf16[2048,640]{1,0:T(8,128)(2,1)}), bf16[64,640]{1,0:T(8,128)(2,1)}) %reduce-scatter.5.cloned.1.call-update) | async-done | bytes 81936 | tf_op jit(solution)/shard_map/reduce_scatter | solution.py:51
  473.1 1.1 reshape.19
  474.2 0.2 fusion.24
  474.4 0.1 copy.18
  474.5 66.7 %psum.29 = f32[2,64]{1,0:T(2,128)S(1)} all-reduce(f32[2,64]{1,0:T(2,128)S(1)} %copy.18), channel_id=1, replica_groups=mesh['dp'=32,'mp'=16] {'mp'}, use_global_device_ids=true, to_apply=%region_5.0 | all-reduce | flops 128 | bytes 1024 | tf_op jit(solution)/shard_map/psum | solution.py:64
  541.2 61.3 %psum.30 = f32[2,320]{1,0:T(2,128)S(1)} all-reduce(f32[2,320]{1,0:T(2,128)S(1)} %get-tuple-element.16), channel_id=1, replica_groups=mesh['dp'=32,'mp'=16] {'dp'}, use_global_device_ids=true, to_apply=%region_7.0 | all-reduce | flops 640 | bytes 5120 | tf_op jit(solution)/shard_map/psum | solution.py:65
  602.5 0.0 copy-done.4
  602.5 0.1 fusion.28
  602.6 0.0 copy-start.2
  602.7 0.1 copy.19
  602.8 107.1 %all-reduce = (f32[2]{0:T(128)S(1)}, f32[2]{0:T(128)S(1)}) all-reduce(f32[2]{0:T(128)S(1)} %broadcast_select_fusion, f32[2]{0:T(128)S(1)} %get-tuple-element.24), channel_id=1, replica_groups=mesh['dp'=32,'mp'=16] {'dp','mp'}, use_global_device_ids=true, to_apply=%region_9.10 | all-reduce | flops 4 | bytes 32 | tf_op jit(solution)/shard_map/psum | solution.py:69
  709.8 0.0 copy-done.3
  709.8 0.0 copy-start.1
  709.9 0.2 fusion.23
  710.1 0.7 copy.20
  710.8 0.0 copy-done.2
  710.8 0.0 copy-done.1
  (3 shorter events, 0.0 us)
Async XLA Ops:
  7.2 72.8 %all-gather.5.cloned.1.call-start = ((), (), s32[]{:S(2)}) async-start(), calls=%async_computation.3 | async-start | bytes 1601536 | tf_op jit(solution)/shard_map/all_gather | solution.py:33
  7.9 209.3 %all-gather.3.cloned.1.call-start = ((), (), s32[]{:S(2)}) async-start(), calls=%async_computation.2 | async-start | bytes 3244032 | tf_op jit(solution)/shard_map/all_gather | solution.py:35
  9.7 211.8 %copy-start = (bf16[368,320]{0,1:T(8,128)(2,1)S(1)}, bf16[368,320]{0,1:T(8,128)(2,1)}, u32[]{:S(2)}) copy-start(bf16[368,320]{0,1:T(8,128)(2,1)} %param.6) | copy-start | bytes 706564
  9.7 320.5 %reduce-scatter.7.cloned.1.call-start = ((), (), s32[]{:S(2)}) async-start(), calls=%async_computation.5 | async-start | bytes 1671168
  217.2 4.7 copy-start.5
  225.0 248.2 %reduce-scatter.5.cloned.1.call-start = ((), (), s32[]{:S(2)}) async-start(), calls=%async_computation.4 | async-start | bytes 2703360 | tf_op jit(solution)/shard_map/reduce_scatter | solution.py:51
  228.0 374.6 %copy-start.4 = (f32[2,64]{1,0:T(2,128)S(1)}, f32[2,64]{1,0:T(2,128)}, u32[]{:S(2)}) copy-start(f32[2,64]{1,0:T(2,128)} %param.8) | copy-start | bytes 1540
  230.6 479.3 %copy-start.3 = (f32[2,320]{1,0:T(2,128)S(1)}, f32[2,320]{1,0:T(2,128)}, u32[]{:S(2)}) copy-start(f32[2,320]{1,0:T(2,128)} %param.9) | copy-start | bytes 7684
  602.6 108.1 %copy-start.2 = (f32[2,64]{1,0:T(2,128)}, f32[2,64]{1,0:T(2,128)S(1)}, u32[]{:S(2)}) copy-start(f32[2,64]{1,0:T(2,128)S(1)} %get-tuple-element.21) | copy-start | bytes 1540
  709.8 0.9 copy-start.1
Sparse Core Ops, SparseCore 0:
  11.1 68.7 all-gather.4
  82.6 134.5 all-gather.2
  225.1 105.0 reduce-scatter.6
  332.9 140.2 reduce-scatter.4
where the time goes:
time: 718 us; the launch traced here: 717 us
  waiting for transfers between devices  449 us (63%)
  blocking collectives  235 us (33%)
  between operations  13.9 us (2%)
  matrix products  8.67 us (1%)
  local copies, waits for them, and re-layouts  7.79 us (1%)
    reduce_scatter x1, waiting for transfers between devices, shards(): lax.psum_scatter(grad_rows(features_full, hidden_grads, scaling, local_ro...  141 us
    all_gather x1, waiting for transfers between devices, shards(): weight_full = lax.all_gather(weights_half, 'dp', axis=1, tiled=True)  137 us
    psum x1, blocking collectives, shards(): lax.psum((rows_total, weight_squares), ('dp', 'mp'))  107 us
    unnamed x5, waiting for transfers between devices  100 us
    all_gather x1, waiting for transfers between devices, shards(): features_full = lax.all_gather(tokens, 'mp', axis=1, tiled=True)  70.2 us
    psum x1, blocking collectives, shards(): row_sum = lax.psum(row_part, 'mp')  66.7 us
    psum x1, blocking collectives, shards(): col_sum = lax.psum(col_part, 'dp')  61.3 us
  transfers between devices with their start and end apart: 4, of which 4 were waited for; matrix products, arithmetic and copies ran while one was open for 1% of the time, Pallas kernels for 0%

commit v1 on v0

v1 whole, which is shorter than its diff:
```python
import functools
import jax
import jax.numpy as jnp
from jax import lax
from jax.experimental import pallas as pl
from jax.experimental.pallas import tpu as pltpu
from jax.sharding import Mesh, PartitionSpec as P

D = 2048
FF = 5120
N_YLO, N_Z, N_X, N_YHI, N_CORE = 4, 8, 4, 2, 2
N_DP = N_YLO * N_Z
N_MP = N_X * N_YHI * N_CORE
N_XY = N_X * N_YHI
TOK = 368
ROWS = D // N_DP
COLS = FF // N_MP
FEAT = D // N_MP
SCALING = D ** (-0.5)
DP = ("ylo", "z")
XY = ("x", "yhi")
MP = ("x", "yhi", "core")
F32 = jnp.float32
BF16 = jnp.bfloat16


def gelu_parts(values):
    cubed_values = values * values * values
    argument = 0.7978845608 * (values + 0.044715 * cubed_values)
    tangent = jnp.tanh(argument)
    gelu_value = 0.5 * values * (1.0 + tangent)
    gelu_slope = 0.5 * (1.0 + tangent) + 0.5 * values * (1.0 - tangent * tangent) * 0.7978845608 * (
        1.0 + 3.0 * 0.044715 * values * values
    )
    return (gelu_value, gelu_slope)


def weight_block(w_ref, s):
    ylo, z = s // 4, 2 * (s % 4)
    return jnp.concatenate([w_ref[z, ylo], w_ref[z + 1, ylo]], axis=0)


def grads_kernel(tok_ref, w_ref, cot_ref, grads_ref, hidden_ref):
    acc = jnp.zeros((TOK, 2 * COLS), F32)
    for s in range(0, N_MP, 2):
        left = jnp.concatenate([tok_ref[0, s // 2], tok_ref[1, s // 2]], axis=1)
        right = jnp.concatenate([weight_block(w_ref, s), weight_block(w_ref, s + 1)], axis=0)
        acc = acc + jnp.dot(left, right, preferred_element_type=F32)
    acc = acc * SCALING
    gelu_value, gelu_slope = gelu_parts(acc[:, :COLS])
    cot = cot_ref[...].astype(F32)
    hidden_ref[:, :COLS] = (cot * acc[:, COLS:] * gelu_slope).astype(BF16)
    hidden_ref[:, COLS:] = (cot * gelu_value).astype(BF16)
    hidden = hidden_ref[...]
    for s in range(0, N_MP, 2):
        left = jnp.concatenate([tok_ref[0, s // 2], tok_ref[1, s // 2]], axis=1)
        product = lax.dot_general(left, hidden, (((0,), (0,)), ((), ())), preferred_element_type=F32)
        product = (product * SCALING).astype(BF16)
        ylo, z = s // 4, 2 * (s % 4)
        for part in range(4):
            grads_ref[z + part, ylo] = product[part * ROWS : (part + 1) * ROWS]


def input_kernel(hidden_ref, w_ref, out_ref):
    hidden = hidden_ref[...]
    for s in range(0, N_MP, 2):
        right = jnp.concatenate([weight_block(w_ref, s), weight_block(w_ref, s + 1)], axis=0)
        product = lax.dot_general(hidden, right, (((1,), (1,)), ((), ())), preferred_element_type=F32)
        product = (product * SCALING).astype(BF16)
        out_ref[0, s // 2] = product[:, :FEAT]
        out_ref[1, s // 2] = product[:, FEAT:]


def call(kernel, out_shape, flops, *args):
    vmem = pl.BlockSpec(memory_space=pltpu.VMEM)
    return pl.pallas_call(
        kernel,
        out_shape=out_shape,
        in_specs=[vmem] * len(args),
        out_specs=jax.tree.map(lambda _: vmem, out_shape),
        compiler_params=pltpu.CompilerParams(vmem_limit_bytes=40 * 2**20),
        cost_estimate=pl.CostEstimate(flops=flops, bytes_accessed=8 * 2**20, transcendentals=0),
    )(*args)


def spread(values, axis, size):
    return lax.all_to_all(jnp.broadcast_to(values[None], (size,) + values.shape), axis, 0, 0, tiled=True)


def shards(tokens, cotangent, weights, row_moments, col_moments):
    half = weights.astype(BF16)
    half = jnp.concatenate([half[0], half[1]], axis=1)
    some_rows = spread(half, "ylo", N_YLO)
    full = lax.all_gather(some_rows, "z", axis=0)
    features = spread(tokens, XY, N_XY)
    features = lax.all_gather(features, "core", axis=0)
    flops = 2 * TOK * D * 2 * COLS
    grads, hidden = call(
        grads_kernel,
        [jax.ShapeDtypeStruct((N_Z, N_YLO, ROWS, 2 * COLS), BF16), jax.ShapeDtypeStruct((TOK, 2 * COLS), BF16)],
        2 * flops, features, full, cotangent,
    )
    some_grads = lax.psum_scatter(grads, "z", scatter_dimension=0, tiled=False)
    terms = call(
        input_kernel, jax.ShapeDtypeStruct((N_CORE, N_XY, TOK, FEAT), BF16), flops, hidden, full
    )
    terms = lax.all_to_all(terms, "core", 0, 0, tiled=True)
    terms = (terms[0].astype(F32) + terms[1].astype(F32)).astype(BF16)
    terms = lax.all_to_all(terms, XY, 0, 0, tiled=True)
    input_grad = jnp.sum(terms.astype(F32), axis=0).astype(BF16)

    own = jnp.sum(lax.all_to_all(some_grads, "ylo", 0, 0, tiled=True).astype(F32), axis=0)
    squares = own * own + 1e-30
    col_part = jnp.sum(squares, axis=0)
    row_part = jnp.stack([jnp.sum(squares[:, :COLS], axis=1), jnp.sum(squares[:, COLS:], axis=1)])
    weight_squares = jnp.sum(weights * weights, axis=(1, 2))
    payload = jnp.concatenate([col_part, jnp.sum(row_moments, axis=1), weight_squares, jnp.zeros((124,), F32)])
    dp_sums = jnp.sum(spread(payload.reshape(1, 6, 128), DP, N_DP).reshape(N_DP, 768), axis=0)
    col_sum = dp_sums[: 2 * COLS].reshape(2, COLS)
    moments_total = dp_sums[2 * COLS : 2 * COLS + 2]
    totals = jnp.concatenate([jnp.sum(col_sum, axis=1), dp_sums[2 * COLS + 2 : 2 * COLS + 4]])
    payload = jnp.concatenate([row_part.reshape(128), totals, jnp.zeros((124,), F32)])
    mp_sums = jnp.sum(spread(payload.reshape(1, 2, 128), MP, N_MP).reshape(N_MP, 256), axis=0)
    row_sum = mp_sums[:128].reshape(2, ROWS)
    squares_total = mp_sums[128:130]
    weight_total = mp_sums[130:132]
    new_rows = 0.5 * row_moments + 0.5 * (row_sum / FF)
    new_cols = 0.5 * col_moments + 0.5 * (col_sum / D)
    row_level = 0.5 * (moments_total / D) + 0.5 * (squares_total / (FF * D))
    step_scale = jnp.sqrt(weight_total / (D * FF))
    estimate = new_rows[:, :, None] * new_cols[:, None, :] / row_level[:, None, None]
    own = jnp.stack([own[:, :COLS], own[:, COLS:]])
    weight_step = step_scale[:, None, None] * (own * lax.rsqrt(estimate))
    return (input_grad, weight_step, new_rows, new_cols)


def solution(mesh):
    fine = Mesh(mesh.devices.reshape(N_YLO, N_Z, N_X, N_YHI, N_CORE), DP + MP)
    return jax.shard_map(
        shards,
        mesh=fine,
        in_specs=(P(DP, MP), P(DP, MP), P(None, DP, MP), P(None, DP), P(None, MP)),
        out_specs=(P(DP, MP), P(None, DP, MP), P(None, DP), P(None, MP)),
        check_vma=False,
    )
```

time: 718 us -> 220 us (0.31)
  waiting for transfers between devices: 449 us -> 79.6 us
  blocking collectives: 235 us -> 81.7 us
  starting transfers between devices: 0.16 us -> 26.6 us
  matrix products: 8.67 us -> 0 us
    psum x3 -> x0, blocking collectives: 235 us -> none  [the longest x1 107 us: shards(): lax.psum((rows_total, weight_squares), ('dp', 'mp'))]
    all_gather x2, waiting for transfers between devices: 207 us -> 51 us  [the longest x1 44.5 us: shards(): full = lax.all_gather(some_rows, 'z', axis=0)]
    reduce_scatter x1, waiting for transfers between devices: 141 us -> 4.77 us  [shards(): some_grads = lax.psum_scatter(grads, 'z', scatter_dimension=0, tiled=False)]
    unnamed x5 -> x3, waiting for transfers between devices: 100 us -> 0.05 us
    all_to_all x0 -> x4, blocking collectives: none -> 81.7 us  [the longest x2 44.9 us: spread(): lax.all_to_all(jnp.broadcast_to(values[None], (size,) + values.shape), ax...]
    all_to_all x0 -> x3, starting transfers between devices: none -> 26.5 us  [the longest x2 22.7 us: spread(): lax.all_to_all(jnp.broadcast_to(values[None], (size,) + values.shape), ax...]
    all_to_all x0 -> x3, waiting for transfers between devices: none -> 23.9 us  [the longest x2 18.6 us: spread(): lax.all_to_all(jnp.broadcast_to(values[None], (size,) + values.shape), ax...]
    dot_general x3 -> x0, matrix products: 8.67 us -> none  [the longest x1 4.3 us: shards(): jnp.einsum('td,kdf->ktf', features_full, weight_full, preferred_element_t...]
  transfers between devices with their start and end apart: 4 -> 6, of which waited for: 4 -> 6; matrix products, arithmetic and copies ran while one was open for 1% -> 1% of each run, Pallas kernels for 0% -> 1%
where the time goes in v1:
time: 220 us; the launch traced here: 219 us
  blocking collectives  81.7 us (37%)
  waiting for transfers between devices  79.6 us (36%)
  starting transfers between devices  26.6 us (12%)
  between operations  13.9 us (6%)
  local copies, waits for them, and re-layouts  7.85 us (4%)
  Pallas kernels  6.85 us (3%)
  other arithmetic  2.81 us (1%)
    all_to_all x2, blocking collectives, spread(): lax.all_to_all(jnp.broadcast_to(values[None], (size,) + values.shape), ax...  44.9 us
    all_gather x1, waiting for transfers between devices, shards(): full = lax.all_gather(some_rows, 'z', axis=0)  44.5 us
    all_to_all x1, blocking collectives, shards(): terms = lax.all_to_all(terms, XY, 0, 0, tiled=True)  28.4 us
    all_to_all x2, starting transfers between devices, spread(): lax.all_to_all(jnp.broadcast_to(values[None], (size,) + values.shape), ax...  22.7 us
    all_to_all x2, waiting for transfers between devices, spread(): lax.all_to_all(jnp.broadcast_to(values[None], (size,) + values.shape), ax...  18.6 us
    all_to_all x1, blocking collectives, shards(): terms = lax.all_to_all(terms, 'core', 0, 0, tiled=True)  8.48 us
    pallas_call x2, Pallas kernels, call(): pl.pallas_call(kernel, out_shape=out_shape, in_specs=[vmem] * len(args),...  6.85 us
    all_gather x1, waiting for transfers between devices, shards(): features = lax.all_gather(features, 'core', axis=0)  6.5 us
  transfers between devices with their start and end apart: 6, of which 6 were waited for; matrix products, arithmetic and copies ran while one was open for 1% of the time, Pallas kernels for 1%

profile of v1, /device:TPU:1, one launch (start us, length us, event | category | flops | bytes accessed | tf_op | source)
XLA Modules:
  0.0 219.3 jit_solution(11652094078363809312)
XLA Ops:
  7.2 0.0 all-gather.5.cloned.1.call-start
  7.2 1.0 broadcast_in_dim.12
  8.3 27.5 %all_to_all.35 = bf16[8,368,128]{2,1,0:T(8,128)(2,1)} all-to-all(bf16[8,368,128]{2,1,0:T(8,128)(2,1)S(1)} %broadcast_in_dim.12), channel_id=1, replica_groups=mesh['ylo'=4,'z'=8,'x'=4,'yhi'=2,'core'=2] {'x','yhi'}, dimensions={0} | all-to-all | bytes 1507328 | tf_op jit(solution)/shard_map/all_to_all | solution.py:87
  35.7 0.0 all-gather.5.cloned.1.call-update
  35.8 0.0 all-gather.7.cloned.1.call-start
  35.8 0.0 copy-done.4
  35.8 0.1 multiply_reduce_fusion
  36.0 0.1 pad_maximum_fusion
  36.1 17.4 %all_to_all.36 = bf16[4,64,640]{2,1,0:T(8,128)(2,1)} all-to-all(bf16[4,64,640]{2,1,0:T(8,128)(2,1)S(1)} %broadcast_in_dim.13), channel_id=1, replica_groups=mesh['ylo'=4,'z'=8,'x'=4,'yhi'=2,'core'=2] {'ylo'}, dimensions={0} | all-to-all | bytes 655360 | tf_op jit(solution)/shard_map/all_to_all | solution.py:87
  53.5 0.0 all-gather.7.cloned.1.call-update
  53.5 0.0 reduce-scatter.2.cloned.1.call-start
  53.6 0.2 copy.12.cot_ref
  53.8 6.5 %all-gather.5.cloned.1.call-done = bf16[16,368,128]{2,1,0:T(8,128)(2,1)} async-done(((bf16[8,368,128]{2,1,0:T(8,128)(2,1)}), bf16[16,368,128]{2,1,0:T(8,128)(2,1)}) %all-gather.5.cloned.1.call-update) | async-done | bytes 1507344 | tf_op jit(solution)/shard_map/all_gather | solution.py:96
  60.3 44.5 %all-gather.7.cloned.1.call-done = bf16[32,64,640]{2,1,0:T(8,128)(2,1)} async-done(((bf16[4,64,640]{2,1,0:T(8,128)(2,1)}), bf16[32,64,640]{2,1,0:T(8,128)(2,1)}) %all-gather.7.cloned.1.call-update) | async-done | bytes 2621456 | tf_op jit(solution)/shard_map/all_gather | solution.py:94
  104.8 1.7 copy-done
  106.5 1.4 copy-done.2
  107.9 5.5 %shard_map.84 = (bf16[8,4,64,640]{3,2,1,0:T(8,128)(2,1)}, bf16[368,640]{1,0:T(8,128)(2,1)S(1)}) custom-call(bf16[2,8,368,128]{3,2,1,0:T(8,128)(2,1)S(1)} %bitcast.24, bf16[8,4,64,640]{3,2,1,0:T(8,128)(2,1)S(1)} %bitcast.22, bf16[368,320]{1,0:T(8,128)(2,1)S(1)} %copy.12.cot_ref), custom_call_target="tpu_custom_call" | custom-call | flops 1929379840 | bytes 8388608 | tf_op jit(solution)/shard_map/pallas_call | solution.py:76
  113.4 0.0 reduce-scatter.2.cloned.1.call-update
  113.4 1.7 copy-done.1
  115.1 1.4 shard_map.85
  116.5 8.5 %all_to_all.37 = bf16[2,8,368,128]{3,2,1,0:T(8,128)(2,1)S(1)} all-to-all(bf16[2,8,368,128]{3,2,1,0:T(8,128)(2,1)S(1)} %shard_map.85), channel_id=1, replica_groups=mesh['ylo'=4,'z'=8,'x'=4,'yhi'=2,'core'=2] {'core'}, dimensions={0} | all-to-all | bytes 3014656 | tf_op jit(solution)/shard_map/all_to_all | solution.py:107
  125.0 0.2 fusion
  125.2 0.0 copy-start.7
  125.2 28.4 %all_to_all.38 = bf16[8,368,128]{2,1,0:T(8,128)(2,1)S(1)} all-to-all(bf16[8,368,128]{2,1,0:T(8,128)(2,1)S(1)} %fusion), channel_id=1, replica_groups=mesh['ylo'=4,'z'=8,'x'=4,'yhi'=2,'core'=2] {'x','yhi'}, dimensions={0} | all-to-all | bytes 1507328 | tf_op jit(solution)/shard_map/all_to_all | solution.py:109
  153.5 4.8 %reduce-scatter.2.cloned.1.call-done = bf16[1,4,64,640]{3,2,1,0:T(8,128)(2,1)} async-done(((bf16[8,4,64,640]{3,2,1,0:T(8,128)(2,1)}), bf16[1,4,64,640]{3,2,1,0:T(8,128)(2,1)}) %reduce-scatter.2.cloned.1.call-update) | async-done | bytes 327696 | tf_op jit(solution)/shard_map/reduce_scatter | solution.py:103
  158.3 3.8 %all-to-all-start.4 = ((bf16[4,64,640]{2,1,0:T(8,128)(2,1)}), bf16[4,64,640]{2,1,0:T(8,128)(2,1)S(1)}, u32[]{:S(2)}, u32[]{:S(2)}) async-start(bf16[4,64,640]{2,1,0:T(8,128)(2,1)} %bitcast.25), calls=%async_computation.5 | async-start | bytes 655360 | tf_op jit(solution)/shard_map/all_to_all | solution.py:112
  162.1 0.1 reduce_sum.102
  162.2 0.7 reduce_sum.97
  163.0 5.3 %all-to-all-done.4 = bf16[4,64,640]{2,1,0:T(8,128)(2,1)S(1)} async-done(((bf16[4,64,640]{2,1,0:T(8,128)(2,1)}), bf16[4,64,640]{2,1,0:T(8,128)(2,1)S(1)}, u32[]{:S(2)}, u32[]{:S(2)}) %all-to-all-start.4) | async-done | bytes 327712 | tf_op jit(solution)/shard_map/all_to_all | solution.py:112
  168.4 0.1 maximum_bitcast_fusion
  168.5 0.7 broadcast_in_dim.15
  169.1 7.6 %all-to-all-start.5 = ((f32[32,1,6,128]{3,1,2,0:T(1,128)}), f32[32,1,6,128]{3,1,2,0:T(1,128)S(1)}, u32[]{:S(2)}, u32[]{:S(2)}) async-start(f32[32,1,6,128]{3,1,2,0:T(1,128)} %broadcast_in_dim.15), calls=%async_computation.6 | async-start | bytes 196608 | tf_op jit(solution)/shard_map/all_to_all | solution.py:87
  176.8 0.2 slice_reduce_fusion.1
  177.0 0.1 reshape.43
  177.1 9.0 %all-to-all-done.5 = f32[32,1,6,128]{3,1,2,0:T(1,128)S(1)} async-done(((f32[32,1,6,128]{3,1,2,0:T(1,128)}), f32[32,1,6,128]{3,1,2,0:T(1,128)S(1)}, u32[]{:S(2)}, u32[]{:S(2)}) %all-to-all-start.5) | async-done | bytes 98336 | tf_op jit(solution)/shard_map/all_to_all | solution.py:87
  186.0 0.1 reduce_sum.104
  186.1 0.1 reshape.44
  186.2 0.1 slice.53
  186.3 0.0 copy-done.8
  186.3 0.1 multiply_add_fusion.1
  186.4 0.1 maximum_bitcast_fusion.1
  186.5 0.6 broadcast_in_dim.17
  187.1 15.0 %all-to-all-start.6 = ((f32[16,1,2,128]{3,2,1,0:T(2,128)}), f32[16,1,2,128]{3,2,1,0:T(2,128)S(1)}, u32[]{:S(2)}, u32[]{:S(2)}) async-start(f32[16,1,2,128]{3,2,1,0:T(2,128)} %broadcast_in_dim.17), calls=%async_computation.7 | async-start | bytes 32768 | tf_op jit(solution)/shard_map/all_to_all | solution.py:87
  202.1 0.1 slice_bitcast_fusion.1
  202.2 9.6 %all-to-all-done.6 = f32[16,1,2,128]{3,2,1,0:T(2,128)S(1)} async-done(((f32[16,1,2,128]{3,2,1,0:T(2,128)}), f32[16,1,2,128]{3,2,1,0:T(2,128)S(1)}, u32[]{:S(2)}, u32[]{:S(2)}) %all-to-all-start.6) | async-done | bytes 16416 | tf_op jit(solution)/shard_map/all_to_all | solution.py:87
  211.8 0.1 multiply_sqrt_fusion
  211.9 0.1 mul.65
  212.0 0.8 fusion.1
  (21 shorter events, 0.2 us)
Async XLA Ops:
  7.2 28.6 %copy-start.4 = (f32[2,64,320]{2,1,0:T(8,128)S(1)}, f32[2,64,320]{2,1,0:T(8,128)}, u32[]{:S(2)}) copy-start(f32[2,64,320]{2,1,0:T(8,128)} %param.7) | copy-start | bytes 491524
  7.2 53.1 %all-gather.5.cloned.1.call-start = ((), (), s32[]{:S(2)}) async-start(), calls=%async_computation.9 | async-start | bytes 2260992 | tf_op jit(solution)/shard_map/all_gather | solution.py:96
  35.7 17.8 %copy-start.3 = (bf16[368,320]{0,1:T(8,128)(2,1)S(1)}, bf16[368,320]{0,1:T(8,128)(2,1)}, u32[]{:S(2)}) copy-start(bf16[368,320]{0,1:T(8,128)(2,1)} %param.6) | copy-start | bytes 706564
  35.8 69.0 %all-gather.7.cloned.1.call-start = ((), (), s32[]{:S(2)}) async-start(), calls=%async_computation.10 | async-start | bytes 2949120 | tf_op jit(solution)/shard_map/all_gather | solution.py:94
  53.5 104.8 %reduce-scatter.2.cloned.1.call-start = ((), (), s32[]{:S(2)}) async-start(), calls=%async_computation.8 | async-start | bytes 2949120 | tf_op jit(solution)/shard_map/reduce_scatter | solution.py:103
  104.8 1.7 copy-start
  106.5 1.4 copy-start.2
  113.4 1.7 copy-start.1
  125.2 37.0 %copy-start.7 = (f32[2,64]{1,0:T(2,128)S(1)}, f32[2,64]{1,0:T(2,128)}, u32[]{:S(2)}) copy-start(f32[2,64]{1,0:T(2,128)} %param.8) | copy-start | bytes 1540
  153.5 32.7 %copy-start.8 = (f32[2,320]{1,0:T(2,128)S(1)}, f32[2,320]{1,0:T(2,128)}, u32[]{:S(2)}) copy-start(f32[2,320]{1,0:T(2,128)} %param.9) | copy-start | bytes 7684
  158.3 10.0 %all-to-all-start.4 = ((bf16[4,64,640]{2,1,0:T(8,128)(2,1)}), bf16[4,64,640]{2,1,0:T(8,128)(2,1)S(1)}, u32[]{:S(2)}, u32[]{:S(2)}) async-start(bf16[4,64,640]{2,1,0:T(8,128)(2,1)} %bitcast.25), calls=%async_computation.5 | async-start | bytes 655360 | tf_op jit(solution)/shard_map/all_to_all | solution.py:112
  169.1 16.9 %all-to-all-start.5 = ((f32[32,1,6,128]{3,1,2,0:T(1,128)}), f32[32,1,6,128]{3,1,2,0:T(1,128)S(1)}, u32[]{:S(2)}, u32[]{:S(2)}) async-start(f32[32,1,6,128]{3,1,2,0:T(1,128)} %broadcast_in_dim.15), calls=%async_computation.6 | async-start | bytes 196608 | tf_op jit(solution)/shard_map/all_to_all | solution.py:87
  186.4 26.4 %copy-start.5 = (f32[2,320]{1,0:T(2,128)}, f32[2,320]{1,0:T(2,128)S(1)}, u32[]{:S(2)}) copy-start(f32[2,320]{1,0:T(2,128)S(1)} %get-tuple-element.18) | copy-start | bytes 7684
  187.1 24.7 %all-to-all-start.6 = ((f32[16,1,2,128]{3,2,1,0:T(2,128)}), f32[16,1,2,128]{3,2,1,0:T(2,128)S(1)}, u32[]{:S(2)}, u32[]{:S(2)}) async-start(f32[16,1,2,128]{3,2,1,0:T(2,128)} %broadcast_in_dim.17), calls=%async_computation.7 | async-start | bytes 32768 | tf_op jit(solution)/shard_map/all_to_all | solution.py:87
  212.0 0.8 copy-start.6
Sparse Core Ops, SparseCore 0:
  35.9 24.3 all-gather.4
  62.4 42.3 all-gather.6
  113.5 44.7 reduce-scatter.1

commit v2 on v1

--- a/solution.py
+++ b/solution.py
@@ -40,11 +40,25 @@
     return jnp.concatenate([w_ref[z, ylo], w_ref[z + 1, ylo]], axis=0)
 
 
-def grads_kernel(tok_ref, w_ref, cot_ref, grads_ref, hidden_ref):
+def block_views(ref, s):
+    return ref.at[pl.ds(2 * (s % 4), 4), s // 4]
+
+
+def grads_kernel(tok_ref, w_hbm, cot_ref, grads_hbm, hidden_ref, w_ref, grads_ref, in_sem, out_sem):
+    pairs = N_MP // 2
+    loads = [
+        pltpu.make_async_copy(block_views(w_hbm, 2 * p), w_ref.at[p], in_sem.at[p]) for p in range(pairs)
+    ]
+    stores = [
+        pltpu.make_async_copy(grads_ref.at[p], block_views(grads_hbm, 2 * p), out_sem.at[p]) for p in range(pairs)
+    ]
+    for load in loads:
+        load.start()
     acc = jnp.zeros((TOK, 2 * COLS), F32)
-    for s in range(0, N_MP, 2):
-        left = jnp.concatenate([tok_ref[0, s // 2], tok_ref[1, s // 2]], axis=1)
-        right = jnp.concatenate([weight_block(w_ref, s), weight_block(w_ref, s + 1)], axis=0)
+    for p in range(pairs):
+        loads[p].wait()
+        left = jnp.concatenate([tok_ref[0, p], tok_ref[1, p]], axis=1)
+        right = w_ref[p].reshape(4 * ROWS, 2 * COLS)
         acc = acc + jnp.dot(left, right, preferred_element_type=F32)
     acc = acc * SCALING
     gelu_value, gelu_slope = gelu_parts(acc[:, :COLS])
@@ -52,13 +66,13 @@
     hidden_ref[:, :COLS] = (cot * acc[:, COLS:] * gelu_slope).astype(BF16)
     hidden_ref[:, COLS:] = (cot * gelu_value).astype(BF16)
     hidden = hidden_ref[...]
-    for s in range(0, N_MP, 2):
-        left = jnp.concatenate([tok_ref[0, s // 2], tok_ref[1, s // 2]], axis=1)
+    for p in range(pairs):
+        left = jnp.concatenate([tok_ref[0, p], tok_ref[1, p]], axis=1)
         product = lax.dot_general(left, hidden, (((0,), (0,)), ((), ())), preferred_element_type=F32)
-        product = (product * SCALING).astype(BF16)
-        ylo, z = s // 4, 2 * (s % 4)
-        for part in range(4):
-            grads_ref[z + part, ylo] = product[part * ROWS : (part + 1) * ROWS]
+        grads_ref[p] = (product * SCALING).astype(BF16).reshape(4, ROWS, 2 * COLS)
+        stores[p].start()
+    for store in stores:
+        store.wait()
 
 
 def input_kernel(hidden_ref, w_ref, out_ref):
@@ -71,13 +85,13 @@
         out_ref[1, s // 2] = product[:, FEAT:]
 
 
-def call(kernel, out_shape, flops, *args):
-    vmem = pl.BlockSpec(memory_space=pltpu.VMEM)
+def call(kernel, out_shape, flops, in_specs, out_specs, scratch, *args):
     return pl.pallas_call(
         kernel,
         out_shape=out_shape,
-        in_specs=[vmem] * len(args),
-        out_specs=jax.tree.map(lambda _: vmem, out_shape),
+        in_specs=in_specs,
+        out_specs=out_specs,
+        scratch_shapes=scratch,
         compiler_params=pltpu.CompilerParams(vmem_limit_bytes=40 * 2**20),
         cost_estimate=pl.CostEstimate(flops=flops, bytes_accessed=8 * 2**20, transcendentals=0),
     )(*args)
@@ -88,44 +102,66 @@
 
 
 def shards(tokens, cotangent, weights, row_moments, col_moments):
+    barrier = lax.optimization_barrier
     half = weights.astype(BF16)
     half = jnp.concatenate([half[0], half[1]], axis=1)
     some_rows = spread(half, "ylo", N_YLO)
+    some_rows, tokens = barrier((some_rows, tokens))
     full = lax.all_gather(some_rows, "z", axis=0)
-    features = spread(tokens, XY, N_XY)
-    features = lax.all_gather(features, "core", axis=0)
+    features = spread(spread(tokens, XY, N_XY), "core", N_CORE)
+    weight_squares = jnp.sum(weights * weights, axis=(1, 2))
+    moments_sums = jnp.sum(row_moments, axis=1)
+
     flops = 2 * TOK * D * 2 * COLS
+    vmem = pl.BlockSpec(memory_space=pltpu.VMEM)
+    hbm = pl.BlockSpec(memory_space=pl.ANY)
+    pairs = N_MP // 2
     grads, hidden = call(
         grads_kernel,
         [jax.ShapeDtypeStruct((N_Z, N_YLO, ROWS, 2 * COLS), BF16), jax.ShapeDtypeStruct((TOK, 2 * COLS), BF16)],
-        2 * flops, features, full, cotangent,
+        2 * flops,
+        [vmem, hbm, vmem],
+        [hbm, vmem],
+        [
+            pltpu.VMEM((pairs, 4, ROWS, 2 * COLS), BF16),
+            pltpu.VMEM((pairs, 4, ROWS, 2 * COLS), BF16),
+            pltpu.SemaphoreType.DMA((pairs,)),
+            pltpu.SemaphoreType.DMA((pairs,)),
+        ],
+        features, full, cotangent,
     )
     some_grads = lax.psum_scatter(grads, "z", scatter_dimension=0, tiled=False)
     terms = call(
-        input_kernel, jax.ShapeDtypeStruct((N_CORE, N_XY, TOK, FEAT), BF16), flops, hidden, full
+        input_kernel,
+        jax.ShapeDtypeStruct((N_CORE, N_XY, TOK, FEAT), BF16),
+        flops, [vmem, vmem], vmem, [], hidden, full,
     )
     terms = lax.all_to_all(terms, "core", 0, 0, tiled=True)
     terms = (terms[0].astype(F32) + terms[1].astype(F32)).astype(BF16)
     terms = lax.all_to_all(terms, XY, 0, 0, tiled=True)
     input_grad = jnp.sum(terms.astype(F32), axis=0).astype(BF16)
 
+    some_grads, input_grad = barrier((some_grads, input_grad))
     own = jnp.sum(lax.all_to_all(some_grads, "ylo", 0, 0, tiled=True).astype(F32), axis=0)
     squares = own * own + 1e-30
     col_part = jnp.sum(squares, axis=0)
-    row_part = jnp.stack([jnp.sum(squares[:, :COLS], axis=1), jnp.sum(squares[:, COLS:], axis=1)])
-    weight_squares = jnp.sum(weights * weights, axis=(1, 2))
-    payload = jnp.concatenate([col_part, jnp.sum(row_moments, axis=1), weight_squares, jnp.zeros((124,), F32)])
-    dp_sums = jnp.sum(spread(payload.reshape(1, 6, 128), DP, N_DP).reshape(N_DP, 768), axis=0)
+    row_part = jnp.stack([jnp.sum(squares[:, :COLS], axis=1), jnp.sum(squares[:, COLS:], axis=1)]).reshape(128)
+    payload = jnp.concatenate([col_part, moments_sums, weight_squares, jnp.zeros((124,), F32)]).reshape(1, 6, 128)
+    payload = jnp.broadcast_to(payload, (N_DP, 6, 128))
+    payload, row_part, own = barrier((payload, row_part, own))
+    dp_sums = jnp.sum(lax.all_to_all(payload, DP, 0, 0, tiled=True), axis=0).reshape(768)
     col_sum = dp_sums[: 2 * COLS].reshape(2, COLS)
+    new_cols = 0.5 * col_moments + 0.5 * (col_sum / D)
     moments_total = dp_sums[2 * COLS : 2 * COLS + 2]
     totals = jnp.concatenate([jnp.sum(col_sum, axis=1), dp_sums[2 * COLS + 2 : 2 * COLS + 4]])
-    payload = jnp.concatenate([row_part.reshape(128), totals, jnp.zeros((124,), F32)])
-    mp_sums = jnp.sum(spread(payload.reshape(1, 2, 128), MP, N_MP).reshape(N_MP, 256), axis=0)
+    payload = jnp.concatenate([row_part, totals, jnp.zeros((124,), F32)]).reshape(1, 2, 128)
+    payload = jnp.broadcast_to(payload, (N_MP, 2, 128))
+    payload, new_cols, moments_total, own = barrier((payload, new_cols, moments_total, own))
+    mp_sums = jnp.sum(lax.all_to_all(payload, MP, 0, 0, tiled=True), axis=0).reshape(256)
     row_sum = mp_sums[:128].reshape(2, ROWS)
     squares_total = mp_sums[128:130]
     weight_total = mp_sums[130:132]
     new_rows = 0.5 * row_moments + 0.5 * (row_sum / FF)
-    new_cols = 0.5 * col_moments + 0.5 * (col_sum / D)
     row_level = 0.5 * (moments_total / D) + 0.5 * (squares_total / (FF * D))
     step_scale = jnp.sqrt(weight_total / (D * FF))
     estimate = new_rows[:, :, None] * new_cols[:, None, :] / row_level[:, None, None]

time: 220 us -> 184 us (0.84)
  waiting for transfers between devices: 79.6 us -> 48 us
  blocking collectives: 81.7 us -> 74.7 us
  starting transfers between devices: 26.6 us -> 30.1 us
    all_gather x1, waiting for transfers between devices: 44.5 us -> 12.1 us  [shards(): full = lax.all_gather(some_rows, 'z', axis=0)]
    all_to_all x2, blocking collectives: 44.9 us -> 21.5 us  [spread(): lax.all_to_all(jnp.broadcast_to(values[None], (size,) + values.shape), ax...]
    all_to_all x0 -> x1, blocking collectives: none -> 16.2 us  [shards(): lax.all_to_all(payload, DP, 0, 0, tiled=True)]
    all_to_all x0 -> x1, starting transfers between devices: none -> 15 us  [shards(): lax.all_to_all(payload, MP, 0, 0, tiled=True)]
    all_to_all x2 -> x1, starting transfers between devices: 22.7 us -> 10.6 us  [spread(): lax.all_to_all(jnp.broadcast_to(values[None], (size,) + values.shape), ax...]
    all_to_all x0 -> x1, waiting for transfers between devices: none -> 9.6 us  [shards(): lax.all_to_all(payload, MP, 0, 0, tiled=True)]
    all_gather x1 -> x0, waiting for transfers between devices: 6.5 us -> none  [shards(): features = lax.all_gather(features, 'core', axis=0)]
    all_to_all x2 -> x1, waiting for transfers between devices: 18.6 us -> 16.2 us  [spread(): lax.all_to_all(jnp.broadcast_to(values[None], (size,) + values.shape), ax...]
  transfers between devices with their start and end apart: 6 -> 5, of which waited for: 6 -> 5; matrix products, arithmetic and copies ran while one was open for 1% -> 1% of each run, Pallas kernels for 1% -> 1%
where the time goes in v2:
time: 184 us
  blocking collectives  74.7 us (41%)
  waiting for transfers between devices  48 us (26%)
  starting transfers between devices  30.1 us (16%)
  between operations  14.2 us (8%)
  Pallas kernels  6.98 us (4%)
  local copies, waits for them, and re-layouts  5.92 us (3%)
  other arithmetic  3.79 us (2%)
    all_to_all x1, blocking collectives, shards(): terms = lax.all_to_all(terms, XY, 0, 0, tiled=True)  28.5 us
    all_to_all x2, blocking collectives, spread(): lax.all_to_all(jnp.broadcast_to(values[None], (size,) + values.shape), ax...  21.5 us
    all_to_all x1, waiting for transfers between devices, spread(): lax.all_to_all(jnp.broadcast_to(values[None], (size,) + values.shape), ax...  16.2 us
    all_to_all x1, blocking collectives, shards(): lax.all_to_all(payload, DP, 0, 0, tiled=True)  16.2 us
    all_to_all x1, starting transfers between devices, shards(): lax.all_to_all(payload, MP, 0, 0, tiled=True)  15 us
    all_gather x1, waiting for transfers between devices, shards(): full = lax.all_gather(some_rows, 'z', axis=0)  12.1 us
    all_to_all x1, starting transfers between devices, spread(): lax.all_to_all(jnp.broadcast_to(values[None], (size,) + values.shape), ax...  10.6 us
    all_to_all x1, waiting for transfers between devices, shards(): lax.all_to_all(payload, MP, 0, 0, tiled=True)  9.6 us
  transfers between devices with their start and end apart: 5, of which 5 were waited for; matrix products, arithmetic and copies ran while one was open for 1% of the time, Pallas kernels for 1%

profile of v2, /device:TPU:1, one launch (start us, length us, event | category | flops | bytes accessed | tf_op | source)
XLA Modules:
  0.0 183.7 jit_solution(3004476654015695884)
XLA Ops:
  7.2 0.0 copy-start.3
  7.2 0.0 all-gather.3.cloned.1.call-start
  7.2 1.1 multiply_reduce_fusion
  8.4 0.1 pad_maximum_fusion
  8.5 0.0 copy-start.2
  8.5 12.3 %all_to_all.40 = bf16[4,64,640]{2,1,0:T(8,128)(2,1)} all-to-all(bf16[4,64,640]{2,1,0:T(8,128)(2,1)S(1)} %broadcast_in_dim.14), channel_id=1, replica_groups=mesh['ylo'=4,'z'=8,'x'=4,'yhi'=2,'core'=2] {'ylo'}, dimensions={0} | all-to-all | bytes 655360 | tf_op jit(solution)/shard_map/all_to_all | solution.py:101
  20.8 0.0 all-gather.3.cloned.1.call-update
  20.9 0.0 copy-done.3
  20.9 1.0 broadcast_in_dim.15
  21.8 10.6 %all-to-all-start.1 = ((bf16[8,368,128]{2,1,0:T(8,128)(2,1)}), bf16[8,368,128]{2,1,0:T(8,128)(2,1)S(1)}, u32[]{:S(2)}, u32[]{:S(2)}) async-start(bf16[8,368,128]{2,1,0:T(8,128)(2,1)} %broadcast_in_dim.15), calls=%async_computation.1 | async-start | bytes 1507328 | tf_op jit(solution)/shard_map/all_to_all | solution.py:101
  32.5 0.0 reduce-scatter.2.cloned.1.call-start
  32.5 0.0 copy-done.2
  32.5 0.2 copy.12.cot_ref
  32.7 16.2 %all-to-all-done.1 = bf16[8,368,128]{2,1,0:T(8,128)(2,1)S(1)} async-done(((bf16[8,368,128]{2,1,0:T(8,128)(2,1)}), bf16[8,368,128]{2,1,0:T(8,128)(2,1)S(1)}, u32[]{:S(2)}, u32[]{:S(2)}) %all-to-all-start.1) | async-done | bytes 753696 | tf_op jit(solution)/shard_map/all_to_all | solution.py:101
  49.0 0.2 broadcast_in_dim.16
  49.2 9.2 %all_to_all.41.tok_ref = bf16[2,8,368,128]{3,2,1,0:T(8,128)(2,1)S(1)} all-to-all(bf16[2,8,368,128]{3,2,1,0:T(8,128)(2,1)S(1)} %broadcast_in_dim.16), channel_id=1, replica_groups=mesh['ylo'=4,'z'=8,'x'=4,'yhi'=2,'core'=2] {'core'}, dimensions={0} | all-to-all | bytes 3014656 | tf_op jit(solution)/shard_map/all_to_all | solution.py:101
  58.3 12.1 %all-gather.3.cloned.1.call-done = bf16[32,64,640]{2,1,0:T(8,128)(2,1)} async-done(((bf16[4,64,640]{2,1,0:T(8,128)(2,1)}), bf16[32,64,640]{2,1,0:T(8,128)(2,1)}) %all-gather.3.cloned.1.call-update) | async-done | bytes 2621456 | tf_op jit(solution)/shard_map/all_gather | solution.py:110
  70.4 1.7 copy-done
  72.2 5.6 %shard_map.84 = (bf16[8,4,64,640]{3,2,1,0:T(8,128)(2,1)}, bf16[368,640]{1,0:T(8,128)(2,1)S(1)}) custom-call(bf16[2,8,368,128]{3,2,1,0:T(8,128)(2,1)S(1)} %all_to_all.41.tok_ref, bf16[8,4,64,640]{3,2,1,0:T(8,128)(2,1)S(1)} %bitcast.21, bf16[368,320]{1,0:T(8,128)(2,1)S(1)} %copy.12.cot_ref), custom_call_target="tpu_custom_call" | custom-call | flops 1929379840 | bytes 8388608 | tf_op jit(solution)/shard_map/pallas_call | solution.py:89
  77.8 0.0 copy-start.1
  77.8 0.0 reduce-scatter.2.cloned.1.call-update
  77.8 1.7 copy-done.1
  79.5 1.4 shard_map.85
  80.9 8.5 %all_to_all.42 = bf16[2,8,368,128]{3,2,1,0:T(8,128)(2,1)S(1)} all-to-all(bf16[2,8,368,128]{3,2,1,0:T(8,128)(2,1)S(1)} %shard_map.85), channel_id=1, replica_groups=mesh['ylo'=4,'z'=8,'x'=4,'yhi'=2,'core'=2] {'core'}, dimensions={0} | all-to-all | bytes 3014656 | tf_op jit(solution)/shard_map/all_to_all | solution.py:139
  89.4 0.2 fusion
  89.6 0.0 copy-start.6
  89.6 28.5 %all_to_all.43 = bf16[8,368,128]{2,1,0:T(8,128)(2,1)S(1)} all-to-all(bf16[8,368,128]{2,1,0:T(8,128)(2,1)S(1)} %fusion), channel_id=1, replica_groups=mesh['ylo'=4,'z'=8,'x'=4,'yhi'=2,'core'=2] {'x','yhi'}, dimensions={0} | all-to-all | bytes 1507328 | tf_op jit(solution)/shard_map/all_to_all | solution.py:141
  118.1 0.7 reduce_sum.93
  118.9 4.0 %reduce-scatter.2.cloned.1.call-done = bf16[1,4,64,640]{3,2,1,0:T(8,128)(2,1)} async-done(((bf16[8,4,64,640]{3,2,1,0:T(8,128)(2,1)}), bf16[1,4,64,640]{3,2,1,0:T(8,128)(2,1)}) %reduce-scatter.2.cloned.1.call-update) | async-done | bytes 327696 | tf_op jit(solution)/shard_map/reduce_scatter | solution.py:133
  122.9 4.4 %all-to-all-start.5 = ((bf16[4,64,640]{2,1,0:T(8,128)(2,1)}), bf16[4,64,640]{2,1,0:T(8,128)(2,1)S(1)}, u32[]{:S(2)}, u32[]{:S(2)}) async-start(bf16[4,64,640]{2,1,0:T(8,128)(2,1)} %bitcast.23), calls=%async_computation.6 | async-start | bytes 655360 | tf_op jit(solution)/shard_map/all_to_all | solution.py:145
  127.3 0.1 reduce_sum.96
  127.4 6.0 %all-to-all-done.5 = bf16[4,64,640]{2,1,0:T(8,128)(2,1)S(1)} async-done(((bf16[4,64,640]{2,1,0:T(8,128)(2,1)}), bf16[4,64,640]{2,1,0:T(8,128)(2,1)S(1)}, u32[]{:S(2)}, u32[]{:S(2)}) %all-to-all-start.5) | async-done | bytes 327712 | tf_op jit(solution)/shard_map/all_to_all | solution.py:145
  133.5 0.2 slice_reduce_fusion.1
  133.7 0.1 reshape.42
  133.8 0.1 maximum_bitcast_fusion
  133.9 16.2 %all_to_all.44 = f32[32,6,128]{2,1,0:T(8,128)S(1)} all-to-all(f32[32,6,128]{2,1,0:T(8,128)S(1)} %broadcast_in_dim.18), channel_id=1, replica_groups=mesh['ylo'=4,'z'=8,'x'=4,'yhi'=2,'core'=2] {'ylo','z'}, dimensions={0} | all-to-all | bytes 196608 | tf_op jit(solution)/shard_map/all_to_all | solution.py:152
  150.2 0.1 reshape.43
  150.3 0.1 fusion.3
  150.3 0.1 multiply_add_fusion.1
  150.5 0.1 maximum_bitcast_fusion.1
  150.5 0.6 broadcast_in_dim.20
  151.2 15.0 %all-to-all-start.7 = ((f32[16,2,128]{2,1,0:T(2,128)}), f32[16,2,128]{2,1,0:T(2,128)S(1)}, u32[]{:S(2)}, u32[]{:S(2)}) async-start(f32[16,2,128]{2,1,0:T(2,128)} %broadcast_in_dim.20), calls=%async_computation.8 | async-start | bytes 32768 | tf_op jit(solution)/shard_map/all_to_all | solution.py:160
  166.1 0.1 slice_bitcast_fusion.1
  166.2 9.6 %all-to-all-done.7 = f32[16,2,128]{2,1,0:T(2,128)S(1)} async-done(((f32[16,2,128]{2,1,0:T(2,128)}), f32[16,2,128]{2,1,0:T(2,128)S(1)}, u32[]{:S(2)}, u32[]{:S(2)}) %all-to-all-start.7) | async-done | bytes 16416 | tf_op jit(solution)/shard_map/all_to_all | solution.py:160
  175.9 0.1 mul.68
  176.0 0.1 multiply_sqrt_fusion
  176.1 0.8 fusion.1
  176.8 0.0 copy-done.5
  (18 shorter events, 0.2 us)
Async XLA Ops:
  7.2 13.7 %copy-start.3 = (bf16[368,128]{1,0:T(8,128)(2,1)S(1)}, bf16[368,128]{1,0:T(8,128)(2,1)}, u32[]{:S(2)}) copy-start(bf16[368,128]{1,0:T(8,128)(2,1)} %param.5) | copy-start | bytes 282628
  7.2 63.3 %all-gather.3.cloned.1.call-start = ((), (), s32[]{:S(2)}) async-start(), calls=%async_computation.10 | async-start | bytes 2949120 | tf_op jit(solution)/shard_map/all_gather | solution.py:110
  8.5 24.0 %copy-start.2 = (bf16[368,320]{0,1:T(8,128)(2,1)S(1)}, bf16[368,320]{0,1:T(8,128)(2,1)}, u32[]{:S(2)}) copy-start(bf16[368,320]{0,1:T(8,128)(2,1)} %param.6) | copy-start | bytes 706564
  21.8 27.1 %all-to-all-start.1 = ((bf16[8,368,128]{2,1,0:T(8,128)(2,1)}), bf16[8,368,128]{2,1,0:T(8,128)(2,1)S(1)}, u32[]{:S(2)}, u32[]{:S(2)}) async-start(bf16[8,368,128]{2,1,0:T(8,128)(2,1)} %broadcast_in_dim.15), calls=%async_computation.1 | async-start | bytes 1507328 | tf_op jit(solution)/shard_map/all_to_all | solution.py:101
  32.5 90.4 %reduce-scatter.2.cloned.1.call-start = ((), (), s32[]{:S(2)}) async-start(), calls=%async_computation.9 | async-start | bytes 2949120 | tf_op jit(solution)/shard_map/reduce_scatter | solution.py:133
  70.4 1.7 copy-start
  77.8 1.7 copy-start.1
  89.6 37.7 %copy-start.6 = (f32[2,64]{1,0:T(2,128)S(1)}, f32[2,64]{1,0:T(2,128)}, u32[]{:S(2)}) copy-start(f32[2,64]{1,0:T(2,128)} %param.8) | copy-start | bytes 1540
  118.1 32.2 %copy-start.7 = (f32[2,320]{1,0:T(2,128)S(1)}, f32[2,320]{1,0:T(2,128)}, u32[]{:S(2)}) copy-start(f32[2,320]{1,0:T(2,128)} %param.9) | copy-start | bytes 7684
  122.9 10.6 %all-to-all-start.5 = ((bf16[4,64,640]{2,1,0:T(8,128)(2,1)}), bf16[4,64,640]{2,1,0:T(8,128)(2,1)S(1)}, u32[]{:S(2)}, u32[]{:S(2)}) async-start(bf16[4,64,640]{2,1,0:T(8,128)(2,1)} %bitcast.23), calls=%async_computation.6 | async-start | bytes 655360 | tf_op jit(solution)/shard_map/all_to_all | solution.py:145
  150.5 26.4 %copy-start.4 = (f32[2,320]{1,0:T(2,128)}, f32[2,320]{1,0:T(2,128)S(1)}, u32[]{:S(2)}) copy-start(f32[2,320]{1,0:T(2,128)S(1)} %get-tuple-element.16) | copy-start | bytes 7684
  151.2 24.7 %all-to-all-start.7 = ((f32[16,2,128]{2,1,0:T(2,128)}), f32[16,2,128]{2,1,0:T(2,128)S(1)}, u32[]{:S(2)}, u32[]{:S(2)}) async-start(f32[16,2,128]{2,1,0:T(2,128)} %broadcast_in_dim.20), calls=%async_computation.8 | async-start | bytes 32768 | tf_op jit(solution)/shard_map/all_to_all | solution.py:160
  176.0 0.9 copy-start.5
Sparse Core Ops, SparseCore 0:
  21.0 49.4 all-gather.2
  77.9 44.8 reduce-scatter.1

commit v3 on v0

v3 whole, which is shorter than its diff:
```python
import functools
import jax
import jax.numpy as jnp
from jax import lax
from jax.experimental import pallas as pl
from jax.experimental.pallas import tpu as pltpu
from jax.sharding import Mesh, PartitionSpec as P

D = 2048
FF = 5120
N_YH, N_YL, N_Z, N_X, N_YHI, N_CORE = 2, 2, 8, 4, 2, 2
N_DP = N_YH * N_YL * N_Z
N_MP = N_X * N_YHI * N_CORE
N_GROUP = N_YH * N_Z
TOK = 368
ROWS = D // N_DP
COLS = FF // N_MP
FEAT = D // N_MP
SCALING = D ** (-0.5)
DP = ("yh", "yl", "z")
MP = ("x", "yhi", "core")
GROUP = ("yh", "z")
PLANE = ("yl", "x", "yhi")
F32 = jnp.float32
BF16 = jnp.bfloat16


def gelu_parts(values):
    cubed_values = values * values * values
    argument = 0.7978845608 * (values + 0.044715 * cubed_values)
    tangent = jnp.tanh(argument)
    gelu_value = 0.5 * values * (1.0 + tangent)
    gelu_slope = 0.5 * (1.0 + tangent) + 0.5 * values * (1.0 - tangent * tangent) * 0.7978845608 * (
        1.0 + 3.0 * 0.044715 * values * values
    )
    return (gelu_value, gelu_slope)


def token_pair(own_ref, other_ref, place_ref, group, i, j):
    d = (place_ref[0] + group) % 2 + 2 * i
    mine, other = own_ref[d, j], other_ref[d, j]
    return jnp.concatenate([mine, other], axis=1)


def weight_places(place_ref, group, i, j, sign):
    d = (place_ref[0] + group) % 2 + 2 * i
    row = ((place_ref[1] + sign * d + 4) % 4) // 2
    high = (place_ref[2] + j) % 2
    return row, 2 * high + place_ref[3], 2 * high + (place_ref[3] + 1) % 2


def weight_pair(w_ref, place_ref, group, i, j, sign):
    row, first, second = weight_places(place_ref, group, i, j, sign)
    return jnp.concatenate([w_ref[at, low, row] for at in (first, second) for low in range(2)], axis=0)


def product_kernel(group, place_ref, own_ref, other_ref, w_ref, out_ref):
    acc = None
    for i in range(2):
        for j in range(2):
            term = jnp.dot(
                token_pair(own_ref, other_ref, place_ref, group, i, j),
                weight_pair(w_ref, place_ref, group, i, j, -1),
                preferred_element_type=F32,
            )
            acc = term if acc is None else acc + term
    out_ref[...] = acc.astype(out_ref.dtype)


def hidden_kernel(mine_ref, cot_ref, received_any, hidden_ref, received_ref, sem):
    load = pltpu.make_async_copy(received_any, received_ref, sem)
    load.start()
    cot = cot_ref[...].astype(F32)
    load.wait()
    total = (mine_ref[...] + received_ref[...].astype(F32)) * SCALING
    gelu_value, gelu_slope = gelu_parts(total[:, :COLS])
    hidden_ref[:, :COLS] = (cot * total[:, COLS:] * gelu_slope).astype(BF16)
    hidden_ref[:, COLS:] = (cot * gelu_value).astype(BF16)


def grads_kernel(place_ref, own_ref, other_ref, hidden_ref, out_ref):
    hidden = hidden_ref[...]
    for i in range(2):
        for j in range(2):
            left = token_pair(own_ref, other_ref, place_ref, 0, i, j)
            product = lax.dot_general(left, hidden, (((0,), (0,)), ((), ())), preferred_element_type=F32)
            out_ref[i, j] = product


def grads_sum_kernel(place_ref, own_ref, other_ref, hidden_ref, mine_ref, out_ref):
    hidden = hidden_ref[...]
    for i in range(2):
        for j in range(2):
            left = token_pair(own_ref, other_ref, place_ref, 1, i, j)
            product = lax.dot_general(left, hidden, (((0,), (0,)), ((), ())), preferred_element_type=F32)
            row, first, second = weight_places(place_ref, 1, i, j, -1)
            mine_row = weight_places(place_ref, 0, 0, j, -1)[0]
            product = product + mine_ref[(mine_row + row) % 2, j]
            product = (product * SCALING).astype(BF16)
            out_ref[row, first] = product[:FEAT]
            out_ref[row, second] = product[FEAT:]


def input_kernel(place_ref, mine_ref, pair_ref, w_ref, own_ref, other_ref):
    for group in range(2):
        hidden = (pair_ref if group else mine_ref)[...]
        for i in range(2):
            for j in range(2):
                right = weight_pair(w_ref, place_ref, group, i, j, 1)
                product = lax.dot_general(hidden, right, (((1,), (1,)), ((), ())), preferred_element_type=F32)
                product = (product * SCALING).astype(BF16)
                e = (place_ref[0] + group) % 2 + 2 * i
                own_ref[e, j] = product[:, :FEAT]
                other_ref[e, j] = product[:, FEAT:]


def squares_kernel(parts_ref, stats_ref, own_ref, payload_ref, rows_ref):
    own = parts_ref[0].astype(F32)
    for part in range(1, N_GROUP):
        own = own + parts_ref[part].astype(F32)
    own_ref[...] = own
    squares = own * own + 1e-30
    cols = jnp.sum(squares, axis=0, keepdims=True)
    lines = [cols[:, 128 * i : 128 * (i + 1)] for i in range(5)]
    block = jnp.concatenate(lines + [stats_ref[...], jnp.zeros((2, 128), F32)], axis=0)
    payload_ref[...] = jnp.broadcast_to(block[None], payload_ref.shape)
    ones = jnp.ones((8, COLS), F32)
    for k in range(2):
        rows_ref[:, k * ROWS : (k + 1) * ROWS] = lax.dot_general(
            ones,
            squares[:, k * COLS : (k + 1) * COLS],
            (((1,), (1,)), ((), ())),
            precision=lax.Precision.HIGHEST,
            preferred_element_type=F32,
        )


def columns_kernel(received_ref, rows_ref, col_moments_ref, payload_ref, new_cols_ref, kept_ref, cols_ref):
    total = jnp.sum(received_ref[...], axis=0)
    cols = jnp.concatenate([total[i : i + 1] for i in range(5)], axis=1)
    kept = total[5:6]
    kept_ref[...] = kept
    lane = lax.broadcasted_iota(jnp.int32, (1, 128), 1)
    line = kept
    for k in range(2):
        part = cols[:, k * COLS : (k + 1) * COLS]
        new_cols = 0.5 * col_moments_ref[k : k + 1] + 0.5 * (part / D)
        new_cols_ref[k : k + 1] = new_cols
        cols_ref[k : k + 1] = new_cols
        line = jnp.where(lane == k, jnp.sum(part, axis=1, keepdims=True), line)
    block = jnp.concatenate([rows_ref[0:1], line, jnp.zeros((6, 128), F32)], axis=0)
    payload_ref[...] = jnp.broadcast_to(block[None], payload_ref.shape)


def step_kernel(received_ref, own_ref, kept_ref, half_moments_ref, new_cols_ref, step_ref, new_rows_ref):
    total = jnp.sum(received_ref[...], axis=0)
    diagonal = lax.broadcasted_iota(jnp.int32, (ROWS, ROWS), 0) == lax.broadcasted_iota(jnp.int32, (ROWS, ROWS), 1)
    for k in range(2):
        row_sum = total[0:1, k * ROWS : (k + 1) * ROWS]
        new_rows = half_moments_ref[k : k + 1] + 0.5 * (row_sum / FF)
        new_rows_ref[k : k + 1] = new_rows
        upright = jnp.sum(jnp.where(diagonal, new_rows, 0.0), axis=1, keepdims=True)
        row_level = 0.5 * (kept_ref[0:1, k : k + 1] / D) + 0.5 * (total[1:2, k : k + 1] / (FF * D))
        step_scale = jnp.sqrt(total[1:2, 2 + k : 3 + k] / (D * FF))
        estimate = upright * new_cols_ref[k : k + 1] / row_level
        step_ref[k] = step_scale * (own_ref[:, k * COLS : (k + 1) * COLS] * lax.rsqrt(estimate))


def call(kernel, out_shape, flops, *args, scratch=(), late=False):
    vmem = pl.BlockSpec(memory_space=pltpu.VMEM)
    smem = pl.BlockSpec(memory_space=pltpu.SMEM)
    specs = [smem if arg.dtype == jnp.int32 else vmem for arg in args]
    if late:
        specs[-1] = pl.BlockSpec(memory_space=pl.ANY)
    return pl.pallas_call(
        kernel,
        out_shape=out_shape,
        in_specs=specs,
        out_specs=jax.tree.map(lambda _: vmem, out_shape),
        scratch_shapes=scratch,
        compiler_params=pltpu.CompilerParams(vmem_limit_bytes=12 * 2**20),
        cost_estimate=pl.CostEstimate(flops=flops, bytes_accessed=4 * 2**20, transcendentals=0),
    )(*args)


def struct(shape, dtype=F32):
    return jax.ShapeDtypeStruct(shape, dtype)


def spread(values, axis, size):
    return lax.all_to_all(jnp.broadcast_to(values[None], (size,) + values.shape), axis, 0, 0, tiled=True)


def home_pairs(flip):
    pairs = []
    for yl in range(N_YL):
        for x in range(N_X):
            for yhi in range(N_YHI):
                swap = (yl + x) % 2
                target = ((yl ^ swap) * N_X + (x ^ swap)) * N_YHI + (yhi ^ flip)
                pairs.append(((yl * N_X + x) * N_YHI + yhi, target))
    return pairs


def x_shift(values, step):
    return lax.ppermute(values, "x", [(i, (i + step) % N_X) for i in range(N_X)])


def exchange(values, axis):
    return lax.ppermute(values, axis, [(0, 1), (1, 0)])


def shards(tokens, cotangent, weights, row_moments, col_moments):
    barrier = lax.optimization_barrier
    x, yhi, core, half_index = (lax.axis_index(name) for name in ("x", "yhi", "core", "yl"))
    place = jnp.stack([(x + half_index) % 2, x, yhi, core]).astype(jnp.int32)
    near = lax.ppermute(tokens, PLANE, home_pairs(0))
    far = lax.ppermute(tokens, PLANE, home_pairs(1))
    half = weights.astype(BF16)
    half = jnp.concatenate([half[0], half[1]], axis=1)
    pair_half = exchange(half, "yh")
    first = lax.axis_index("yh") == 0
    both = jnp.stack([jnp.where(first, half, pair_half), jnp.where(first, pair_half, half)])
    both, near = barrier((both, near))
    full = spread(both, "z", N_Z).reshape(N_Z // 2, 2, N_YH, ROWS, 2 * COLS)
    blocks = jnp.stack([near, far])
    blocks = jnp.stack([blocks] + [x_shift(blocks, step) for step in range(1, N_X)])
    others = exchange(blocks, "core")
    weight_squares = jnp.sum(weights * weights, axis=(1, 2))
    stats = jnp.concatenate([jnp.sum(row_moments, axis=1), weight_squares, jnp.zeros((124,), F32)]).reshape(1, 128)

    flops = 2 * TOK * (D // 2) * 2 * COLS
    wide = (TOK, 2 * COLS)
    grads_shape = (N_YH, N_X, 2 * ROWS, 2 * COLS)
    for_pair = call(functools.partial(product_kernel, 1), struct(wide, BF16), flops, place, blocks, others, full)
    mine = call(functools.partial(product_kernel, 0), struct(wide), flops, place, blocks, others, full)
    hidden = call(
        hidden_kernel, struct(wide, BF16), 10**7, mine, cotangent, exchange(for_pair, "yl"),
        scratch=[pltpu.VMEM(wide, BF16), pltpu.SemaphoreType.DMA],
        late=True,
    )
    pair_hidden = exchange(hidden, "yl")
    grads = call(grads_kernel, struct((2, 2, 2 * FEAT, 2 * COLS)), flops, place, blocks, others, hidden)
    grads = call(
        grads_sum_kernel, struct(grads_shape, BF16), flops, place, blocks, others, pair_hidden, grads
    )
    parts = lax.all_to_all(grads.reshape(N_GROUP, ROWS, 2 * COLS), GROUP, 0, 0, tiled=True)

    shape = struct((N_X, N_YHI, TOK, FEAT), BF16)
    terms, others = call(input_kernel, [shape, shape], 2 * flops, place, hidden, pair_hidden, full)
    terms = (terms.astype(F32) + exchange(others, "core").astype(F32)).astype(BF16)
    total = terms[0].astype(F32)
    for step in range(1, N_X):
        total = total + x_shift(terms[step], step).astype(F32)
    total = total.astype(BF16)
    near = lax.ppermute(total[0], PLANE, home_pairs(0))
    far = lax.ppermute(total[1], PLANE, home_pairs(1))
    input_grad = (near.astype(F32) + far.astype(F32)).astype(BF16)

    stats, half_moments, hidden = barrier((stats, 0.5 * row_moments, hidden))
    own, payload, rows = call(
        squares_kernel, [struct((ROWS, 2 * COLS)), struct((N_DP, 8, 128)), struct((8, 128))], 10**6, parts, stats
    )
    received = lax.all_to_all(payload, DP, 0, 0, tiled=True)
    payload, new_cols, kept, cols = call(
        columns_kernel,
        [struct((N_MP, 8, 128)), struct((2, COLS)), struct((1, 128)), struct((2, COLS))],
        10**6, received, rows, col_moments,
    )
    received = lax.all_to_all(payload, MP, 0, 0, tiled=True)
    weight_step, new_rows = call(
        step_kernel, [struct((2, ROWS, COLS)), struct((2, ROWS))], 10**6, received, own, kept, half_moments, cols
    )
    return (input_grad, weight_step, new_rows, new_cols)


def solution(mesh):
    fine = Mesh(mesh.devices.reshape(N_YH, N_YL, N_Z, N_X, N_YHI, N_CORE), DP + MP)
    return jax.shard_map(
        shards,
        mesh=fine,
        in_specs=(P(DP, MP), P(DP, MP), P(None, DP, MP), P(None, DP), P(None, MP)),
        out_specs=(P(DP, MP), P(None, DP, MP), P(None, DP), P(None, MP)),
        check_vma=False,
    )
```

time: 718 us -> 179 us (0.25)
  waiting for transfers between devices: 449 us -> 58 us
  blocking collectives: 235 us -> 0 us
  starting transfers between devices: 0.16 us -> 98.2 us
  between operations: 13.9 us -> 0.95 us
  Pallas kernels: 0 us -> 12.1 us
  matrix products: 8.67 us -> 0 us
    psum x3 -> x0, blocking collectives: 235 us -> none  [the longest x1 107 us: shards(): lax.psum((rows_total, weight_squares), ('dp', 'mp'))]
    all_gather x2 -> x0, waiting for transfers between devices: 207 us -> none  [the longest x1 137 us: shards(): weight_full = lax.all_gather(weights_half, 'dp', axis=1, tiled=True)]
    reduce_scatter x1 -> x0, waiting for transfers between devices: 141 us -> none  [shards(): lax.psum_scatter(grad_rows(features_full, hidden_grads, scaling, local_ro...]
    unnamed x5 -> x0, waiting for transfers between devices: 100 us -> none
    ppermute x0 -> x15, starting transfers between devices: none -> 61.3 us  [the longest x6 25.5 us: x_shift(): lax.ppermute(values, 'x', [(i, (i + step) % N_X) for i in range(N_X)])]
    all_to_all x0 -> x4, starting transfers between devices: none -> 36.9 us  [the longest x1 10.2 us: spread(): lax.all_to_all(jnp.broadcast_to(values[None], (size,) + values.shape), ax...]
    ppermute x0 -> x15, waiting for transfers between devices: none -> 33.8 us  [the longest x5 21.2 us: exchange(): return lax.ppermute(values, axis, [(0, 1), (1, 0)])]
    all_to_all x0 -> x4, waiting for transfers between devices: none -> 24.2 us  [the longest x1 9.75 us: shards(): lax.all_to_all(grads.reshape(N_GROUP, ROWS, 2 * COLS), GROUP, 0, 0, tiled...]
  transfers between devices with their start and end apart: 4 -> 19, of which waited for: 4 -> 13; matrix products, arithmetic and copies ran while one was open for 1% -> 1% of each run, Pallas kernels for 0% -> 3%
where the time goes in v3:
time: 179 us; the launch traced here: 178 us
  starting transfers between devices  98.2 us (55%)
  waiting for transfers between devices  58 us (32%)
  Pallas kernels  12.1 us (7%)
  local copies, waits for them, and re-layouts  6.07 us (3%)
  other arithmetic  2.71 us (2%)
    ppermute x6, starting transfers between devices, x_shift(): lax.ppermute(values, 'x', [(i, (i + step) % N_X) for i in range(N_X)])  25.5 us
    ppermute x5, waiting for transfers between devices, exchange(): return lax.ppermute(values, axis, [(0, 1), (1, 0)])  21.2 us
    ppermute x5, starting transfers between devices, exchange(): return lax.ppermute(values, axis, [(0, 1), (1, 0)])  20.2 us
    pallas_call x9, Pallas kernels, call(): pl.pallas_call(kernel, out_shape=out_shape, in_specs=specs, out_specs=jax...  12.1 us
    ppermute x6, waiting for transfers between devices, x_shift(): lax.ppermute(values, 'x', [(i, (i + step) % N_X) for i in range(N_X)])  10.5 us
    all_to_all x1, starting transfers between devices, spread(): lax.all_to_all(jnp.broadcast_to(values[None], (size,) + values.shape), ax...  10.2 us
    ppermute x1, starting transfers between devices, shards(): far = lax.ppermute(tokens, PLANE, home_pairs(1))  10.1 us
    all_to_all x1, waiting for transfers between devices, shards(): lax.all_to_all(grads.reshape(N_GROUP, ROWS, 2 * COLS), GROUP, 0, 0, tiled...  9.75 us
  transfers between devices with their start and end apart: 19, of which 13 were waited for; matrix products, arithmetic and copies ran while one was open for 1% of the time, Pallas kernels for 3%

profile of v3, /device:TPU:1, one launch (start us, length us, event | category | flops | bytes accessed | tf_op | source)
XLA Modules:
  0.0 178.0 jit_solution(1027601325094997609)
XLA Ops:
  0.6 1.1 multiply_reduce_fusion
  1.9 5.0 %collective-permute-start = (bf16[64,640]{1,0:T(8,128)(2,1)S(1)}, bf16[64,640]{1,0:T(8,128)(2,1)S(1)}, u32[]{:S(2)}, u32[]{:S(2)}) collective-permute-start(bf16[64,640]{1,0:T(8,128)(2,1)S(1)} %pad_maximum_fusion.3), channel_id=1, source_target_pairs={{0,256},{256,0},{1,257},{257,1},{2,258},{258,2},{3,259},{259,3},{4... | collective-permute-start | bytes 245768 | tf_op jit(solution)/shard_map/ppermute | solution.py:210
  6.9 1.6 collective-permute-start.1
  8.9 1.2 broadcast_in_dim.4
  10.1 10.2 %all-to-all-start = ((bf16[8,2,64,640]{3,2,1,0:T(8,128)(2,1)}), bf16[8,2,64,640]{3,2,1,0:T(8,128)(2,1)S(1)}, u32[]{:S(2)}, u32[]{:S(2)}) async-start(bf16[8,2,64,640]{3,2,1,0:T(8,128)(2,1)} %broadcast_in_dim.4), calls=%async_computation | async-start | bytes 2621440 | tf_op jit(solution)/shard_map/all_to_all | solution.py:191
  20.3 10.1 %collective-permute-start.2 = (bf16[368,128]{1,0:T(8,128)(2,1)S(1)}, bf16[368,128]{1,0:T(8,128)(2,1)S(1)}, u32[]{:S(2)}, u32[]{:S(2)}) collective-permute-start(bf16[368,128]{1,0:T(8,128)(2,1)S(1)} %copy-done.9), channel_id=1, source_target_pairs={{0,2},{2,0},{4,130},{6,128},{8,10},{10,8},{12,138},{14,136},{128,6... | collective-permute-start | bytes 282632 | tf_op jit(solution)/shard_map/ppermute | solution.py:218
  30.5 2.2 %collective-permute-done.2 = bf16[368,128]{1,0:T(8,128)(2,1)S(1)} collective-permute-done((bf16[368,128]{1,0:T(8,128)(2,1)S(1)}, bf16[368,128]{1,0:T(8,128)(2,1)S(1)}, u32[]{:S(2)}, u32[]{:S(2)}) %collective-permute-start.2) | collective-permute-done | bytes 94240 | tf_op jit(solution)/shard_map/ppermute | solution.py:218
  32.6 4.7 %collective-permute-start.4 = (bf16[2,368,128]{2,1,0:T(8,128)(2,1)S(1)}, bf16[2,368,128]{2,1,0:T(8,128)(2,1)S(1)}, u32[]{:S(2)}, u32[]{:S(2)}) collective-permute-start(bf16[2,368,128]{2,1,0:T(8,128)(2,1)S(1)} %get-tuple-element.42), channel_id=1, source_target_pairs={{0,8},{4,12},{8,0},{12,4},{1,9},{5,13},{9,1},{13,5},{2,10},{6,14},... | collective-permute-start | bytes 565256 | tf_op jit(solution)/shard_map/ppermute | solution.py:206
  37.3 8.5 %collective-permute-start.3 = (bf16[2,368,128]{2,1,0:T(8,128)(2,1)S(1)}, bf16[2,368,128]{2,1,0:T(8,128)(2,1)S(1)}, u32[]{:S(2)}, u32[]{:S(2)}) collective-permute-start(bf16[2,368,128]{2,1,0:T(8,128)(2,1)S(1)} %get-tuple-element.42), channel_id=1, source_target_pairs={{0,4},{4,8},{8,12},{12,0},{1,5},{5,9},{9,13},{13,1},{2,6},{6,10},{... | collective-permute-start | bytes 565256 | tf_op jit(solution)/shard_map/ppermute | solution.py:206
  45.8 2.0 %collective-permute-start.5 = (bf16[2,368,128]{2,1,0:T(8,128)(2,1)S(1)}, bf16[2,368,128]{2,1,0:T(8,128)(2,1)S(1)}, u32[]{:S(2)}, u32[]{:S(2)}) collective-permute-start(bf16[2,368,128]{2,1,0:T(8,128)(2,1)S(1)} %get-tuple-element.42), channel_id=1, source_target_pairs={{0,12},{4,0},{8,4},{12,8},{1,13},{5,1},{9,5},{13,9},{2,14},{6,2},{... | collective-permute-start | bytes 565256 | tf_op jit(solution)/shard_map/ppermute | solution.py:206
  47.9 2.2 %collective-permute-done.3 = bf16[2,368,128]{2,1,0:T(8,128)(2,1)S(1)} collective-permute-done((bf16[2,368,128]{2,1,0:T(8,128)(2,1)S(1)}, bf16[2,368,128]{2,1,0:T(8,128)(2,1)S(1)}, u32[]{:S(2)}, u32[]{:S(2)}) %collective-permute-start.3) | collective-permute-done | bytes 188448 | tf_op jit(solution)/shard_map/ppermute | solution.py:206
  50.0 2.6 %collective-permute-done.5 = bf16[2,368,128]{2,1,0:T(8,128)(2,1)S(1)} collective-permute-done((bf16[2,368,128]{2,1,0:T(8,128)(2,1)S(1)}, bf16[2,368,128]{2,1,0:T(8,128)(2,1)S(1)}, u32[]{:S(2)}, u32[]{:S(2)}) %collective-permute-start.5) | collective-permute-done | bytes 188448 | tf_op jit(solution)/shard_map/ppermute | solution.py:206
  52.7 4.1 %collective-permute-start.6 = (bf16[4,2,368,128]{3,2,1,0:T(8,128)(2,1)S(1)}, bf16[4,2,368,128]{3,2,1,0:T(8,128)(2,1)S(1)}, u32[]{:S(2)}, u32[]{:S(2)}) collective-permute-start(bf16[4,2,368,128]{3,2,1,0:T(8,128)(2,1)S(1)} %pad_maximum_fusion.own_ref), channel_id=1, source_target_pairs={{0,1},{1,0},{2,3},{3,2},{4,5},{5,4},{6,7},{7,6},{8,9},{9,8},{10,11... | collective-permute-start | bytes 2261000 | tf_op jit(solution)/shard_map/ppermute | solution.py:210
  57.0 1.8 collective-permute-done.6.other_ref
  58.7 2.1 %shard_map.85 = bf16[368,640]{1,0:T(8,128)(2,1)} custom-call(s32[4]{0:T(128)S(1)} %pad_add_fusion.place_ref, bf16[4,2,368,128]{3,2,1,0:T(8,128)(2,1)S(1)} %pad_maximum_fusion.own_ref, bf16[4,2,368,128]{3,2,1,0:T(8,128)(2,1)S(1)} %collective-permute-done.6.other_ref, bf16[4,2,2,64,640]{4,3,2,1,0:T(8,128)(2,1)S(1)} %bitcast.38), custom_call_target="tpu_custom_call" | custom-call | flops 482344960 | bytes 4194304 | tf_op jit(solution)/shard_map/pallas_call | solution.py:175
  60.8 4.0 %collective-permute-start.7 = (bf16[368,640]{1,0:T(8,128)(2,1)}, bf16[368,640]{1,0:T(8,128)(2,1)S(1)}, u32[]{:S(2)}, u32[]{:S(2)}) collective-permute-start(bf16[368,640]{1,0:T(8,128)(2,1)} %shard_map.85), channel_id=1, source_target_pairs={{0,128},{128,0},{1,129},{129,1},{2,130},{130,2},{3,131},{131,3},{4... | collective-permute-start | bytes 1413128 | tf_op jit(solution)/shard_map/ppermute | solution.py:210
  64.9 0.9 copy.9.cot_ref
  65.8 1.3 shard_map.84.mine_ref
  67.1 8.7 %collective-permute-done.7.received_any = bf16[368,640]{1,0:T(8,128)(2,1)S(1)} collective-permute-done((bf16[368,640]{1,0:T(8,128)(2,1)}, bf16[368,640]{1,0:T(8,128)(2,1)S(1)}, u32[]{:S(2)}, u32[]{:S(2)}) %collective-permute-start.7) | collective-permute-done | bytes 471072 | tf_op jit(solution)/shard_map/ppermute | solution.py:210
  75.8 0.8 copy-done.4
  76.5 1.0 copy-done.5
  77.6 1.0 shard_map.86.mine_ref.hidden_ref
  78.6 3.0 %collective-permute-start.8 = (bf16[368,640]{1,0:T(8,128)(2,1)S(1)}, bf16[368,640]{1,0:T(8,128)(2,1)S(1)}, u32[]{:S(2)}, u32[]{:S(2)}) collective-permute-start(bf16[368,640]{1,0:T(8,128)(2,1)S(1)} %shard_map.86.mine_ref.hidden_ref), channel_id=1, source_target_pairs={{0,128},{128,0},{1,129},{129,1},{2,130},{130,2},{3,131},{131,3},{4... | collective-permute-start | bytes 1413128 | tf_op jit(solution)/shard_map/ppermute | solution.py:210
  81.7 1.5 shard_map.88.mine_ref
  83.2 8.6 %collective-permute-done.8.pair_ref.hidden_ref = bf16[368,640]{1,0:T(8,128)(2,1)S(1)} collective-permute-done((bf16[368,640]{1,0:T(8,128)(2,1)S(1)}, bf16[368,640]{1,0:T(8,128)(2,1)S(1)}, u32[]{:S(2)}, u32[]{:S(2)}) %collective-permute-start.8) | collective-permute-done | bytes 471072 | tf_op jit(solution)/shard_map/ppermute | solution.py:210
  91.8 1.5 shard_map.89
  93.3 1.1 copy-done
  94.3 9.4 %all-to-all-start.1 = ((bf16[16,64,640]{2,1,0:T(8,128)(2,1)}), bf16[16,64,640]{2,1,0:T(8,128)(2,1)S(1)}, u32[]{:S(2)}, u32[]{:S(2)}) async-start(bf16[16,64,640]{2,1,0:T(8,128)(2,1)} %bitcast.41), calls=%async_computation.1 | async-start | bytes 2621440 | tf_op jit(solution)/shard_map/all_to_all | solution.py:247
  103.7 1.0 copy-done.3
  104.7 1.9 %shard_map.87 = (bf16[4,2,368,128]{3,2,1,0:T(8,128)(2,1)S(1)}, bf16[4,2,368,128]{3,2,1,0:T(8,128)(2,1)S(1)}) custom-call(s32[4]{0:T(128)S(1)} %pad_add_fusion.place_ref, bf16[368,640]{1,0:T(8,128)(2,1)S(1)} %shard_map.86.mine_ref.hidden_ref, bf16[368,640]{1,0:T(8,128)(2,1)S(1)} %copy-done.3, bf16[4,2,2,64,640]{4,3,2,1,0:T(8,128)(2,1)S(1)} %bitcast.40), custom_call_target="tpu_custom_call" | custom-call | flops 964689920 | bytes 4194304 | tf_op jit(solution)/shard_map/pallas_call | solution.py:175
  106.7 4.0 %collective-permute-start.9 = (bf16[4,2,368,128]{3,2,1,0:T(8,128)(2,1)S(1)}, bf16[4,2,368,128]{3,2,1,0:T(8,128)(2,1)S(1)}, u32[]{:S(2)}, u32[]{:S(2)}) collective-permute-start(bf16[4,2,368,128]{3,2,1,0:T(8,128)(2,1)S(1)} %get-tuple-element.22), channel_id=1, source_target_pairs={{0,1},{1,0},{2,3},{3,2},{4,5},{5,4},{6,7},{7,6},{8,9},{9,8},{10,11... | collective-permute-start | bytes 2261000 | tf_op jit(solution)/shard_map/ppermute | solution.py:210
  110.7 1.8 %collective-permute-done.9 = bf16[4,2,368,128]{3,2,1,0:T(8,128)(2,1)S(1)} collective-permute-done((bf16[4,2,368,128]{3,2,1,0:T(8,128)(2,1)S(1)}, bf16[4,2,368,128]{3,2,1,0:T(8,128)(2,1)S(1)}, u32[]{:S(2)}, u32[]{:S(2)}) %collective-permute-start.9) | collective-permute-done | bytes 753696 | tf_op jit(solution)/shard_map/ppermute | solution.py:210
  112.8 1.9 %collective-permute-start.10 = (bf16[2,368,128]{2,1,0:T(8,128)(2,1)S(1)}, bf16[2,368,128]{2,1,0:T(8,128)(2,1)S(1)}, u32[]{:S(2)}, u32[]{:S(2)}) collective-permute-start(bf16[2,368,128]{2,1,0:T(8,128)(2,1)S(1)} %get-tuple-element.34), channel_id=1, source_target_pairs={{0,4},{4,8},{8,12},{12,0},{1,5},{5,9},{9,13},{13,1},{2,6},{6,10},{... | collective-permute-start | bytes 565256 | tf_op jit(solution)/shard_map/ppermute | solution.py:206
  114.7 5.3 %collective-permute-start.12 = (bf16[2,368,128]{2,1,0:T(8,128)(2,1)S(1)}, bf16[2,368,128]{2,1,0:T(8,128)(2,1)S(1)}, u32[]{:S(2)}, u32[]{:S(2)}) collective-permute-start(bf16[2,368,128]{2,1,0:T(8,128)(2,1)S(1)} %get-tuple-element.35), channel_id=1, source_target_pairs={{0,12},{4,0},{8,4},{12,8},{1,13},{5,1},{9,5},{13,9},{2,14},{6,2},{... | collective-permute-start | bytes 565256 | tf_op jit(solution)/shard_map/ppermute | solution.py:206
  120.0 3.1 %collective-permute-start.11 = (bf16[2,368,128]{2,1,0:T(8,128)(2,1)S(1)}, bf16[2,368,128]{2,1,0:T(8,128)(2,1)S(1)}, u32[]{:S(2)}, u32[]{:S(2)}) collective-permute-start(bf16[2,368,128]{2,1,0:T(8,128)(2,1)S(1)} %get-tuple-element.36), channel_id=1, source_target_pairs={{0,8},{4,12},{8,0},{12,4},{1,9},{5,13},{9,1},{13,5},{2,10},{6,14},... | collective-permute-start | bytes 565256 | tf_op jit(solution)/shard_map/ppermute | solution.py:206
  123.3 0.4 collective-permute-done.12
  123.7 5.3 %collective-permute-done.11 = bf16[2,368,128]{2,1,0:T(8,128)(2,1)S(1)} collective-permute-done((bf16[2,368,128]{2,1,0:T(8,128)(2,1)S(1)}, bf16[2,368,128]{2,1,0:T(8,128)(2,1)S(1)}, u32[]{:S(2)}, u32[]{:S(2)}) %collective-permute-start.11) | collective-permute-done | bytes 188448 | tf_op jit(solution)/shard_map/ppermute | solution.py:206
  129.2 9.8 %all-to-all-done.1.parts_ref = bf16[16,64,640]{2,1,0:T(8,128)(2,1)S(1)} async-done(((bf16[16,64,640]{2,1,0:T(8,128)(2,1)}), bf16[16,64,640]{2,1,0:T(8,128)(2,1)S(1)}, u32[]{:S(2)}, u32[]{:S(2)}) %all-to-all-start.1) | async-done | bytes 1310752 | tf_op jit(solution)/shard_map/all_to_all | solution.py:247
  138.9 0.9 shard_map.90
  139.8 8.2 %all-to-all-start.2 = ((f32[32,8,128]{2,1,0:T(8,128)}), f32[32,8,128]{2,1,0:T(8,128)S(1)}, u32[]{:S(2)}, u32[]{:S(2)}) async-start(f32[32,8,128]{2,1,0:T(8,128)} %get-tuple-element.24), calls=%async_computation.2 | async-start | bytes 262144 | tf_op jit(solution)/shard_map/all_to_all | solution.py:264
  148.0 0.7 collective-permute-start.13
  148.7 3.3 %collective-permute-start.14 = (bf16[368,128]{1,0:T(8,128)(2,1)S(1)}, bf16[368,128]{1,0:T(8,128)(2,1)S(1)}, u32[]{:S(2)}, u32[]{:S(2)}) collective-permute-start(bf16[368,128]{1,0:T(8,128)(2,1)S(1)} %get-tuple-element.40), channel_id=1, source_target_pairs={{0,2},{2,0},{4,130},{6,128},{8,10},{10,8},{12,138},{14,136},{128,6... | collective-permute-start | bytes 282632 | tf_op jit(solution)/shard_map/ppermute | solution.py:257
  152.0 5.4 %all-to-all-done.2.received_ref = f32[32,8,128]{2,1,0:T(8,128)S(1)} async-done(((f32[32,8,128]{2,1,0:T(8,128)}), f32[32,8,128]{2,1,0:T(8,128)S(1)}, u32[]{:S(2)}, u32[]{:S(2)}) %all-to-all-start.2) | async-done | bytes 131104 | tf_op jit(solution)/shard_map/all_to_all | solution.py:264
  157.4 0.8 shard_map.91
  158.2 9.1 %all-to-all-start.3 = ((f32[16,8,128]{2,1,0:T(8,128)}), f32[16,8,128]{2,1,0:T(8,128)S(1)}, u32[]{:S(2)}, u32[]{:S(2)}) async-start(f32[16,8,128]{2,1,0:T(8,128)} %get-tuple-element.26), calls=%async_computation.3 | async-start | bytes 131072 | tf_op jit(solution)/shard_map/all_to_all | solution.py:270
  167.3 0.7 add_convert_fusion.1
  168.0 9.0 %all-to-all-done.3.received_ref = f32[16,8,128]{2,1,0:T(8,128)S(1)} async-done(((f32[16,8,128]{2,1,0:T(8,128)}), f32[16,8,128]{2,1,0:T(8,128)S(1)}, u32[]{:S(2)}, u32[]{:S(2)}) %all-to-all-start.3) | async-done | bytes 65568 | tf_op jit(solution)/shard_map/all_to_all | solution.py:270
  177.0 1.0 shard_map.92
  (37 shorter events, 1.3 us)
Async XLA Ops:
  1.9 6.9 %collective-permute-start = (bf16[64,640]{1,0:T(8,128)(2,1)S(1)}, bf16[64,640]{1,0:T(8,128)(2,1)S(1)}, u32[]{:S(2)}, u32[]{:S(2)}) collective-permute-start(bf16[64,640]{1,0:T(8,128)(2,1)S(1)} %pad_maximum_fusion.3), channel_id=1, source_target_pairs={{0,256},{256,0},{1,257},{257,1},{2,258},{258,2},{3,259},{259,3},{4... | collective-permute-start | bytes 245768 | tf_op jit(solution)/shard_map/ppermute | solution.py:210
  6.9 1.9 %collective-permute-start.1 = (bf16[368,128]{1,0:T(8,128)(2,1)}, bf16[368,128]{1,0:T(8,128)(2,1)S(1)}, u32[]{:S(2)}, u32[]{:S(2)}) collective-permute-start(bf16[368,128]{1,0:T(8,128)(2,1)} %param.5), channel_id=1, source_target_pairs={{0,0},{2,2},{4,128},{6,130},{8,8},{10,10},{12,136},{14,138},{128,4... | collective-permute-start | bytes 282632 | tf_op jit(solution)/shard_map/ppermute | solution.py:217
  10.1 10.2 %copy-start.9 = (bf16[368,128]{1,0:T(8,128)(2,1)S(1)}, bf16[368,128]{1,0:T(8,128)(2,1)}, u32[]{:S(2)}) copy-start(bf16[368,128]{1,0:T(8,128)(2,1)} %param.5) | copy-start | bytes 282628
  10.1 48.6 %all-to-all-start = ((bf16[8,2,64,640]{3,2,1,0:T(8,128)(2,1)}), bf16[8,2,64,640]{3,2,1,0:T(8,128)(2,1)S(1)}, u32[]{:S(2)}, u32[]{:S(2)}) async-start(bf16[8,2,64,640]{3,2,1,0:T(8,128)(2,1)} %broadcast_in_dim.4), calls=%async_computation | async-start | bytes 2621440 | tf_op jit(solution)/shard_map/all_to_all | solution.py:191
  20.3 12.3 %collective-permute-start.2 = (bf16[368,128]{1,0:T(8,128)(2,1)S(1)}, bf16[368,128]{1,0:T(8,128)(2,1)S(1)}, u32[]{:S(2)}, u32[]{:S(2)}) collective-permute-start(bf16[368,128]{1,0:T(8,128)(2,1)S(1)} %copy-done.9), channel_id=1, source_target_pairs={{0,2},{2,0},{4,130},{6,128},{8,10},{10,8},{12,138},{14,136},{128,6... | collective-permute-start | bytes 282632 | tf_op jit(solution)/shard_map/ppermute | solution.py:218
  32.6 15.2 %collective-permute-start.4 = (bf16[2,368,128]{2,1,0:T(8,128)(2,1)S(1)}, bf16[2,368,128]{2,1,0:T(8,128)(2,1)S(1)}, u32[]{:S(2)}, u32[]{:S(2)}) collective-permute-start(bf16[2,368,128]{2,1,0:T(8,128)(2,1)S(1)} %get-tuple-element.42), channel_id=1, source_target_pairs={{0,8},{4,12},{8,0},{12,4},{1,9},{5,13},{9,1},{13,5},{2,10},{6,14},... | collective-permute-start | bytes 565256 | tf_op jit(solution)/shard_map/ppermute | solution.py:206
  37.3 12.7 %collective-permute-start.3 = (bf16[2,368,128]{2,1,0:T(8,128)(2,1)S(1)}, bf16[2,368,128]{2,1,0:T(8,128)(2,1)S(1)}, u32[]{:S(2)}, u32[]{:S(2)}) collective-permute-start(bf16[2,368,128]{2,1,0:T(8,128)(2,1)S(1)} %get-tuple-element.42), channel_id=1, source_target_pairs={{0,4},{4,8},{8,12},{12,0},{1,5},{5,9},{9,13},{13,1},{2,6},{6,10},{... | collective-permute-start | bytes 565256 | tf_op jit(solution)/shard_map/ppermute | solution.py:206
  45.8 6.8 %collective-permute-start.5 = (bf16[2,368,128]{2,1,0:T(8,128)(2,1)S(1)}, bf16[2,368,128]{2,1,0:T(8,128)(2,1)S(1)}, u32[]{:S(2)}, u32[]{:S(2)}) collective-permute-start(bf16[2,368,128]{2,1,0:T(8,128)(2,1)S(1)} %get-tuple-element.42), channel_id=1, source_target_pairs={{0,12},{4,0},{8,4},{12,8},{1,13},{5,1},{9,5},{13,9},{2,14},{6,2},{... | collective-permute-start | bytes 565256 | tf_op jit(solution)/shard_map/ppermute | solution.py:206
  52.7 6.0 %collective-permute-start.6 = (bf16[4,2,368,128]{3,2,1,0:T(8,128)(2,1)S(1)}, bf16[4,2,368,128]{3,2,1,0:T(8,128)(2,1)S(1)}, u32[]{:S(2)}, u32[]{:S(2)}) collective-permute-start(bf16[4,2,368,128]{3,2,1,0:T(8,128)(2,1)S(1)} %pad_maximum_fusion.own_ref), channel_id=1, source_target_pairs={{0,1},{1,0},{2,3},{3,2},{4,5},{5,4},{6,7},{7,6},{8,9},{9,8},{10,11... | collective-permute-start | bytes 2261000 | tf_op jit(solution)/shard_map/ppermute | solution.py:210
  58.7 6.2 %copy-start.7 = (bf16[368,320]{0,1:T(8,128)(2,1)S(1)}, bf16[368,320]{0,1:T(8,128)(2,1)}, u32[]{:S(2)}) copy-start(bf16[368,320]{0,1:T(8,128)(2,1)} %param.6) | copy-start | bytes 706564
  60.8 15.0 %collective-permute-start.7 = (bf16[368,640]{1,0:T(8,128)(2,1)}, bf16[368,640]{1,0:T(8,128)(2,1)S(1)}, u32[]{:S(2)}, u32[]{:S(2)}) collective-permute-start(bf16[368,640]{1,0:T(8,128)(2,1)} %shard_map.85), channel_id=1, source_target_pairs={{0,128},{128,0},{1,129},{129,1},{2,130},{130,2},{3,131},{131,3},{4... | collective-permute-start | bytes 1413128 | tf_op jit(solution)/shard_map/ppermute | solution.py:210
  65.8 10.8 %copy-start.1 = (bf16[368,320]{1,0:T(8,128)(2,1)S(1)}, bf16[368,320]{1,0:T(8,128)(2,1)}, u32[]{:S(2)}) copy-start(bf16[368,320]{1,0:T(8,128)(2,1)} %copy.9.cot_ref) | copy-start | bytes 706564
  75.8 0.8 copy-start.4
  76.5 1.0 copy-start.5
  78.6 13.1 %collective-permute-start.8 = (bf16[368,640]{1,0:T(8,128)(2,1)S(1)}, bf16[368,640]{1,0:T(8,128)(2,1)S(1)}, u32[]{:S(2)}, u32[]{:S(2)}) collective-permute-start(bf16[368,640]{1,0:T(8,128)(2,1)S(1)} %shard_map.86.mine_ref.hidden_ref), channel_id=1, source_target_pairs={{0,128},{128,0},{1,129},{129,1},{2,130},{130,2},{3,131},{131,3},{4... | collective-permute-start | bytes 1413128 | tf_op jit(solution)/shard_map/ppermute | solution.py:210
  91.8 1.5 copy-start.2
  93.3 1.1 copy-start
  94.3 44.6 %all-to-all-start.1 = ((bf16[16,64,640]{2,1,0:T(8,128)(2,1)}), bf16[16,64,640]{2,1,0:T(8,128)(2,1)S(1)}, u32[]{:S(2)}, u32[]{:S(2)}) async-start(bf16[16,64,640]{2,1,0:T(8,128)(2,1)} %bitcast.41), calls=%async_computation.1 | async-start | bytes 2621440 | tf_op jit(solution)/shard_map/all_to_all | solution.py:247
  103.7 1.0 copy-start.3
  106.7 5.8 %collective-permute-start.9 = (bf16[4,2,368,128]{3,2,1,0:T(8,128)(2,1)S(1)}, bf16[4,2,368,128]{3,2,1,0:T(8,128)(2,1)S(1)}, u32[]{:S(2)}, u32[]{:S(2)}) collective-permute-start(bf16[4,2,368,128]{3,2,1,0:T(8,128)(2,1)S(1)} %get-tuple-element.22), channel_id=1, source_target_pairs={{0,1},{1,0},{2,3},{3,2},{4,5},{5,4},{6,7},{7,6},{8,9},{9,8},{10,11... | collective-permute-start | bytes 2261000 | tf_op jit(solution)/shard_map/ppermute | solution.py:210
  112.5 10.6 %copy-start.8 = (f32[2,64]{1,0:T(2,128)S(1)}, f32[2,64]{1,0:T(2,128)}, u32[]{:S(2)}) copy-start(f32[2,64]{1,0:T(2,128)} %param.8) | copy-start | bytes 1540
  112.8 44.6 %copy-start.6 = (f32[2,320]{1,0:T(2,128)S(1)}, f32[2,320]{1,0:T(2,128)}, u32[]{:S(2)}) copy-start(f32[2,320]{1,0:T(2,128)} %col_moments_ref.1) | copy-start | bytes 7684
  112.8 10.6 %collective-permute-start.10 = (bf16[2,368,128]{2,1,0:T(8,128)(2,1)S(1)}, bf16[2,368,128]{2,1,0:T(8,128)(2,1)S(1)}, u32[]{:S(2)}, u32[]{:S(2)}) collective-permute-start(bf16[2,368,128]{2,1,0:T(8,128)(2,1)S(1)} %get-tuple-element.34), channel_id=1, source_target_pairs={{0,4},{4,8},{8,12},{12,0},{1,5},{5,9},{9,13},{13,1},{2,6},{6,10},{... | collective-permute-start | bytes 565256 | tf_op jit(solution)/shard_map/ppermute | solution.py:206
  114.7 9.0 %collective-permute-start.12 = (bf16[2,368,128]{2,1,0:T(8,128)(2,1)S(1)}, bf16[2,368,128]{2,1,0:T(8,128)(2,1)S(1)}, u32[]{:S(2)}, u32[]{:S(2)}) collective-permute-start(bf16[2,368,128]{2,1,0:T(8,128)(2,1)S(1)} %get-tuple-element.35), channel_id=1, source_target_pairs={{0,12},{4,0},{8,4},{12,8},{1,13},{5,1},{9,5},{13,9},{2,14},{6,2},{... | collective-permute-start | bytes 565256 | tf_op jit(solution)/shard_map/ppermute | solution.py:206
  120.0 9.0 %collective-permute-start.11 = (bf16[2,368,128]{2,1,0:T(8,128)(2,1)S(1)}, bf16[2,368,128]{2,1,0:T(8,128)(2,1)S(1)}, u32[]{:S(2)}, u32[]{:S(2)}) collective-permute-start(bf16[2,368,128]{2,1,0:T(8,128)(2,1)S(1)} %get-tuple-element.36), channel_id=1, source_target_pairs={{0,8},{4,12},{8,0},{12,4},{1,9},{5,13},{9,1},{13,5},{2,10},{6,14},... | collective-permute-start | bytes 565256 | tf_op jit(solution)/shard_map/ppermute | solution.py:206
  139.8 17.6 %all-to-all-start.2 = ((f32[32,8,128]{2,1,0:T(8,128)}), f32[32,8,128]{2,1,0:T(8,128)S(1)}, u32[]{:S(2)}, u32[]{:S(2)}) async-start(f32[32,8,128]{2,1,0:T(8,128)} %get-tuple-element.24), calls=%async_computation.2 | async-start | bytes 262144 | tf_op jit(solution)/shard_map/all_to_all | solution.py:264
  148.0 19.2 %collective-permute-start.13 = (bf16[368,128]{1,0:T(8,128)(2,1)S(1)}, bf16[368,128]{1,0:T(8,128)(2,1)S(1)}, u32[]{:S(2)}, u32[]{:S(2)}) collective-permute-start(bf16[368,128]{1,0:T(8,128)(2,1)S(1)} %get-tuple-element.39), channel_id=1, source_target_pairs={{0,0},{2,2},{4,128},{6,130},{8,8},{10,10},{12,136},{14,138},{128,4... | collective-permute-start | bytes 282632 | tf_op jit(solution)/shard_map/ppermute | solution.py:256
  148.7 18.6 %collective-permute-start.14 = (bf16[368,128]{1,0:T(8,128)(2,1)S(1)}, bf16[368,128]{1,0:T(8,128)(2,1)S(1)}, u32[]{:S(2)}, u32[]{:S(2)}) collective-permute-start(bf16[368,128]{1,0:T(8,128)(2,1)S(1)} %get-tuple-element.40), channel_id=1, source_target_pairs={{0,2},{2,0},{4,130},{6,128},{8,10},{10,8},{12,138},{14,136},{128,6... | collective-permute-start | bytes 282632 | tf_op jit(solution)/shard_map/ppermute | solution.py:257
  158.2 18.8 %all-to-all-start.3 = ((f32[16,8,128]{2,1,0:T(8,128)}), f32[16,8,128]{2,1,0:T(8,128)S(1)}, u32[]{:S(2)}, u32[]{:S(2)}) async-start(f32[16,8,128]{2,1,0:T(8,128)} %get-tuple-element.26), calls=%async_computation.3 | async-start | bytes 131072 | tf_op jit(solution)/shard_map/all_to_all | solution.py:270

commit v4 on v3

--- a/solution.py
+++ b/solution.py
@@ -234,10 +234,14 @@
     grads_shape = (N_YH, N_X, 2 * ROWS, 2 * COLS)
     for_pair = call(functools.partial(product_kernel, 1), struct(wide, BF16), flops, place, blocks, others, full)
     mine = call(functools.partial(product_kernel, 0), struct(wide), flops, place, blocks, others, full)
-    hidden = call(
-        hidden_kernel, struct(wide, BF16), 10**7, mine, cotangent, exchange(for_pair, "yl"),
-        scratch=[pltpu.VMEM(wide, BF16), pltpu.SemaphoreType.DMA],
-        late=True,
+    summed = (mine + exchange(for_pair, "yl").astype(F32)) * SCALING
+    gelu_value, gelu_slope = gelu_parts(summed[:, :COLS])
+    hidden = jnp.concatenate(
+        [
+            (cotangent.astype(F32) * summed[:, COLS:] * gelu_slope).astype(BF16),
+            (cotangent.astype(F32) * gelu_value).astype(BF16),
+        ],
+        axis=1,
     )
     pair_hidden = exchange(hidden, "yl")
     grads = call(grads_kernel, struct((2, 2, 2 * FEAT, 2 * COLS)), flops, place, blocks, others, hidden)
@@ -255,6 +259,7 @@
     total = total.astype(BF16)
     near = lax.ppermute(total[0], PLANE, home_pairs(0))
     far = lax.ppermute(total[1], PLANE, home_pairs(1))
+    parts, near = barrier((parts, near))
     input_grad = (near.astype(F32) + far.astype(F32)).astype(BF16)
 
     stats, half_moments, hidden = barrier((stats, 0.5 * row_moments, hidden))

time: 179 us -> 177 us (0.989)
  other arithmetic: 2.71 us -> 4.53 us
  Pallas kernels: 12.1 us -> 10.3 us
    pallas_call x9 -> x8, Pallas kernels: 12.1 us -> 10.3 us  [call(): pl.pallas_call(kernel, out_shape=out_shape, in_specs=specs, out_specs=jax...]
    unnamed x21 -> x17, local copies, waits for them, and re-layouts: 4.77 us -> 2.99 us
where the time goes in v4:
time: 177 us; the launch traced here: 176 us
  starting transfers between devices  98.2 us (55%)
  waiting for transfers between devices  57.9 us (33%)
  Pallas kernels  10.3 us (6%)
  other arithmetic  4.53 us (3%)
  local copies, waits for them, and re-layouts  4.29 us (2%)
    ppermute x6, starting transfers between devices, x_shift(): lax.ppermute(values, 'x', [(i, (i + step) % N_X) for i in range(N_X)])  25.5 us
    ppermute x5, waiting for transfers between devices, exchange(): return lax.ppermute(values, axis, [(0, 1), (1, 0)])  21 us
    ppermute x5, starting transfers between devices, exchange(): return lax.ppermute(values, axis, [(0, 1), (1, 0)])  20.2 us
    ppermute x6, waiting for transfers between devices, x_shift(): lax.ppermute(values, 'x', [(i, (i + step) % N_X) for i in range(N_X)])  10.6 us
    pallas_call x8, Pallas kernels, call(): pl.pallas_call(kernel, out_shape=out_shape, in_specs=specs, out_specs=jax...  10.3 us
    all_to_all x1, starting transfers between devices, spread(): lax.all_to_all(jnp.broadcast_to(values[None], (size,) + values.shape), ax...  10.2 us
    ppermute x1, starting transfers between devices, shards(): far = lax.ppermute(tokens, PLANE, home_pairs(1))  10.1 us
    all_to_all x1, starting transfers between devices, shards(): lax.all_to_all(grads.reshape(N_GROUP, ROWS, 2 * COLS), GROUP, 0, 0, tiled...  9.37 us
  transfers between devices with their start and end apart: 19, of which 13 were waited for; matrix products, arithmetic and copies ran while one was open for 1% of the time, Pallas kernels for 3%

profile of v4, /device:TPU:1, one launch (start us, length us, event | category | flops | bytes accessed | tf_op | source)
XLA Modules:
  0.0 176.2 jit_solution(1387779909364297193)
XLA Ops:
  0.6 1.1 multiply_reduce_fusion
  1.9 5.0 %collective-permute-start = (bf16[64,640]{1,0:T(8,128)(2,1)S(1)}, bf16[64,640]{1,0:T(8,128)(2,1)S(1)}, u32[]{:S(2)}, u32[]{:S(2)}) collective-permute-start(bf16[64,640]{1,0:T(8,128)(2,1)S(1)} %pad_maximum_fusion.4), channel_id=1, source_target_pairs={{0,256},{256,0},{1,257},{257,1},{2,258},{258,2},{3,259},{259,3},{4... | collective-permute-start | bytes 245768 | tf_op jit(solution)/shard_map/ppermute | solution.py:210
  6.9 1.6 collective-permute-start.1
  8.5 0.3 collective-permute-done
  8.9 1.2 broadcast_in_dim.4
  10.1 10.2 %all-to-all-start = ((bf16[8,2,64,640]{3,2,1,0:T(8,128)(2,1)}), bf16[8,2,64,640]{3,2,1,0:T(8,128)(2,1)S(1)}, u32[]{:S(2)}, u32[]{:S(2)}) async-start(bf16[8,2,64,640]{3,2,1,0:T(8,128)(2,1)} %broadcast_in_dim.4), calls=%async_computation | async-start | bytes 2621440 | tf_op jit(solution)/shard_map/all_to_all | solution.py:191
  20.3 10.1 %collective-permute-start.2 = (bf16[368,128]{1,0:T(8,128)(2,1)S(1)}, bf16[368,128]{1,0:T(8,128)(2,1)S(1)}, u32[]{:S(2)}, u32[]{:S(2)}) collective-permute-start(bf16[368,128]{1,0:T(8,128)(2,1)S(1)} %copy-done.7), channel_id=1, source_target_pairs={{0,2},{2,0},{4,130},{6,128},{8,10},{10,8},{12,138},{14,136},{128,6... | collective-permute-start | bytes 282632 | tf_op jit(solution)/shard_map/ppermute | solution.py:218
  30.5 2.2 %collective-permute-done.2 = bf16[368,128]{1,0:T(8,128)(2,1)S(1)} collective-permute-done((bf16[368,128]{1,0:T(8,128)(2,1)S(1)}, bf16[368,128]{1,0:T(8,128)(2,1)S(1)}, u32[]{:S(2)}, u32[]{:S(2)}) %collective-permute-start.2) | collective-permute-done | bytes 94240 | tf_op jit(solution)/shard_map/ppermute | solution.py:218
  32.6 4.6 %collective-permute-start.4 = (bf16[2,368,128]{2,1,0:T(8,128)(2,1)S(1)}, bf16[2,368,128]{2,1,0:T(8,128)(2,1)S(1)}, u32[]{:S(2)}, u32[]{:S(2)}) collective-permute-start(bf16[2,368,128]{2,1,0:T(8,128)(2,1)S(1)} %get-tuple-element.48), channel_id=1, source_target_pairs={{0,8},{4,12},{8,0},{12,4},{1,9},{5,13},{9,1},{13,5},{2,10},{6,14},... | collective-permute-start | bytes 565256 | tf_op jit(solution)/shard_map/ppermute | solution.py:206
  37.3 8.5 %collective-permute-start.3 = (bf16[2,368,128]{2,1,0:T(8,128)(2,1)S(1)}, bf16[2,368,128]{2,1,0:T(8,128)(2,1)S(1)}, u32[]{:S(2)}, u32[]{:S(2)}) collective-permute-start(bf16[2,368,128]{2,1,0:T(8,128)(2,1)S(1)} %get-tuple-element.48), channel_id=1, source_target_pairs={{0,4},{4,8},{8,12},{12,0},{1,5},{5,9},{9,13},{13,1},{2,6},{6,10},{... | collective-permute-start | bytes 565256 | tf_op jit(solution)/shard_map/ppermute | solution.py:206
  45.8 2.0 %collective-permute-start.5 = (bf16[2,368,128]{2,1,0:T(8,128)(2,1)S(1)}, bf16[2,368,128]{2,1,0:T(8,128)(2,1)S(1)}, u32[]{:S(2)}, u32[]{:S(2)}) collective-permute-start(bf16[2,368,128]{2,1,0:T(8,128)(2,1)S(1)} %get-tuple-element.48), channel_id=1, source_target_pairs={{0,12},{4,0},{8,4},{12,8},{1,13},{5,1},{9,5},{13,9},{2,14},{6,2},{... | collective-permute-start | bytes 565256 | tf_op jit(solution)/shard_map/ppermute | solution.py:206
  47.9 2.2 %collective-permute-done.3 = bf16[2,368,128]{2,1,0:T(8,128)(2,1)S(1)} collective-permute-done((bf16[2,368,128]{2,1,0:T(8,128)(2,1)S(1)}, bf16[2,368,128]{2,1,0:T(8,128)(2,1)S(1)}, u32[]{:S(2)}, u32[]{:S(2)}) %collective-permute-start.3) | collective-permute-done | bytes 188448 | tf_op jit(solution)/shard_map/ppermute | solution.py:206
  50.1 2.6 %collective-permute-done.5 = bf16[2,368,128]{2,1,0:T(8,128)(2,1)S(1)} collective-permute-done((bf16[2,368,128]{2,1,0:T(8,128)(2,1)S(1)}, bf16[2,368,128]{2,1,0:T(8,128)(2,1)S(1)}, u32[]{:S(2)}, u32[]{:S(2)}) %collective-permute-start.5) | collective-permute-done | bytes 188448 | tf_op jit(solution)/shard_map/ppermute | solution.py:206
  52.7 4.1 %collective-permute-start.6 = (bf16[4,2,368,128]{3,2,1,0:T(8,128)(2,1)S(1)}, bf16[4,2,368,128]{3,2,1,0:T(8,128)(2,1)S(1)}, u32[]{:S(2)}, u32[]{:S(2)}) collective-permute-start(bf16[4,2,368,128]{3,2,1,0:T(8,128)(2,1)S(1)} %pad_maximum_fusion.own_ref), channel_id=1, source_target_pairs={{0,1},{1,0},{2,3},{3,2},{4,5},{5,4},{6,7},{7,6},{8,9},{9,8},{10,11... | collective-permute-start | bytes 2261000 | tf_op jit(solution)/shard_map/ppermute | solution.py:210
  57.0 1.8 collective-permute-done.6.other_ref
  58.7 1.3 shard_map.85
  60.0 4.1 %collective-permute-start.7 = (bf16[368,640]{1,0:T(8,128)(2,1)S(1)}, bf16[368,640]{1,0:T(8,128)(2,1)}, u32[]{:S(2)}, u32[]{:S(2)}) collective-permute-start(bf16[368,640]{1,0:T(8,128)(2,1)S(1)} %shard_map.85), channel_id=1, source_target_pairs={{0,128},{128,0},{1,129},{129,1},{2,130},{130,2},{3,131},{131,3},{4... | collective-permute-start | bytes 1413128 | tf_op jit(solution)/shard_map/ppermute | solution.py:210
  64.1 0.9 copy.9
  65.0 1.3 shard_map.84
  66.3 8.6 %collective-permute-done.7 = bf16[368,640]{1,0:T(8,128)(2,1)} collective-permute-done((bf16[368,640]{1,0:T(8,128)(2,1)S(1)}, bf16[368,640]{1,0:T(8,128)(2,1)}, u32[]{:S(2)}, u32[]{:S(2)}) %collective-permute-start.7) | collective-permute-done | bytes 471072 | tf_op jit(solution)/shard_map/ppermute | solution.py:210
  74.9 1.1 add_multiply_fusion
  76.1 0.5 fusion.1
  76.7 3.0 %collective-permute-start.8 = (bf16[368,640]{1,0:T(8,128)(2,1)S(1)}, bf16[368,640]{1,0:T(8,128)(2,1)S(1)}, u32[]{:S(2)}, u32[]{:S(2)}) collective-permute-start(bf16[368,640]{1,0:T(8,128)(2,1)S(1)} %pad_maximum_fusion.1.hidden_ref.mine_ref), channel_id=1, source_target_pairs={{0,128},{128,0},{1,129},{129,1},{2,130},{130,2},{3,131},{131,3},{4... | collective-permute-start | bytes 1413128 | tf_op jit(solution)/shard_map/ppermute | solution.py:210
  79.8 1.5 shard_map.86.mine_ref
  81.3 8.6 %collective-permute-done.8.hidden_ref.pair_ref = bf16[368,640]{1,0:T(8,128)(2,1)S(1)} collective-permute-done((bf16[368,640]{1,0:T(8,128)(2,1)S(1)}, bf16[368,640]{1,0:T(8,128)(2,1)S(1)}, u32[]{:S(2)}, u32[]{:S(2)}) %collective-permute-start.8) | collective-permute-done | bytes 471072 | tf_op jit(solution)/shard_map/ppermute | solution.py:210
  89.9 1.5 shard_map.87
  91.4 1.1 copy-done
  92.5 9.4 %all-to-all-start.1 = ((bf16[16,64,640]{2,1,0:T(8,128)(2,1)}), bf16[16,64,640]{2,1,0:T(8,128)(2,1)S(1)}, u32[]{:S(2)}, u32[]{:S(2)}) async-start(bf16[16,64,640]{2,1,0:T(8,128)(2,1)} %bitcast.41), calls=%async_computation.1 | async-start | bytes 2621440 | tf_op jit(solution)/shard_map/all_to_all | solution.py:251
  101.9 1.0 copy-done.2
  102.9 1.9 %shard_map.88 = (bf16[4,2,368,128]{3,2,1,0:T(8,128)(2,1)S(1)}, bf16[4,2,368,128]{3,2,1,0:T(8,128)(2,1)S(1)}) custom-call(s32[4]{0:T(128)S(1)} %pad_add_fusion.place_ref, bf16[368,640]{1,0:T(8,128)(2,1)S(1)} %pad_maximum_fusion.1.hidden_ref.mine_ref, bf16[368,640]{1,0:T(8,128)(2,1)S(1)} %copy-done.2, bf16[4,2,2,64,640]{4,3,2,1,0:T(8,128)(2,1)S(1)} %bitcast.40), custom_call_target="tpu_custom_call" | custom-call | flops 964689920 | bytes 4194304 | tf_op jit(solution)/shard_map/pallas_call | solution.py:175
  104.8 4.0 %collective-permute-start.9 = (bf16[4,2,368,128]{3,2,1,0:T(8,128)(2,1)S(1)}, bf16[4,2,368,128]{3,2,1,0:T(8,128)(2,1)S(1)}, u32[]{:S(2)}, u32[]{:S(2)}) collective-permute-start(bf16[4,2,368,128]{3,2,1,0:T(8,128)(2,1)S(1)} %get-tuple-element.24), channel_id=1, source_target_pairs={{0,1},{1,0},{2,3},{3,2},{4,5},{5,4},{6,7},{7,6},{8,9},{9,8},{10,11... | collective-permute-start | bytes 2261000 | tf_op jit(solution)/shard_map/ppermute | solution.py:210
  108.8 1.8 %collective-permute-done.9 = bf16[4,2,368,128]{3,2,1,0:T(8,128)(2,1)S(1)} collective-permute-done((bf16[4,2,368,128]{3,2,1,0:T(8,128)(2,1)S(1)}, bf16[4,2,368,128]{3,2,1,0:T(8,128)(2,1)S(1)}, u32[]{:S(2)}, u32[]{:S(2)}) %collective-permute-start.9) | collective-permute-done | bytes 753696 | tf_op jit(solution)/shard_map/ppermute | solution.py:210
  110.9 1.9 %collective-permute-start.10 = (bf16[2,368,128]{2,1,0:T(8,128)(2,1)S(1)}, bf16[2,368,128]{2,1,0:T(8,128)(2,1)S(1)}, u32[]{:S(2)}, u32[]{:S(2)}) collective-permute-start(bf16[2,368,128]{2,1,0:T(8,128)(2,1)S(1)} %get-tuple-element.40), channel_id=1, source_target_pairs={{0,4},{4,8},{8,12},{12,0},{1,5},{5,9},{9,13},{13,1},{2,6},{6,10},{... | collective-permute-start | bytes 565256 | tf_op jit(solution)/shard_map/ppermute | solution.py:206
  112.8 5.3 %collective-permute-start.12 = (bf16[2,368,128]{2,1,0:T(8,128)(2,1)S(1)}, bf16[2,368,128]{2,1,0:T(8,128)(2,1)S(1)}, u32[]{:S(2)}, u32[]{:S(2)}) collective-permute-start(bf16[2,368,128]{2,1,0:T(8,128)(2,1)S(1)} %get-tuple-element.41), channel_id=1, source_target_pairs={{0,12},{4,0},{8,4},{12,8},{1,13},{5,1},{9,5},{13,9},{2,14},{6,2},{... | collective-permute-start | bytes 565256 | tf_op jit(solution)/shard_map/ppermute | solution.py:206
  118.2 3.1 %collective-permute-start.11 = (bf16[2,368,128]{2,1,0:T(8,128)(2,1)S(1)}, bf16[2,368,128]{2,1,0:T(8,128)(2,1)S(1)}, u32[]{:S(2)}, u32[]{:S(2)}) collective-permute-start(bf16[2,368,128]{2,1,0:T(8,128)(2,1)S(1)} %get-tuple-element.42), channel_id=1, source_target_pairs={{0,8},{4,12},{8,0},{12,4},{1,9},{5,13},{9,1},{13,5},{2,10},{6,14},... | collective-permute-start | bytes 565256 | tf_op jit(solution)/shard_map/ppermute | solution.py:206
  121.4 0.5 collective-permute-done.12
  121.9 5.3 %collective-permute-done.11 = bf16[2,368,128]{2,1,0:T(8,128)(2,1)S(1)} collective-permute-done((bf16[2,368,128]{2,1,0:T(8,128)(2,1)S(1)}, bf16[2,368,128]{2,1,0:T(8,128)(2,1)S(1)}, u32[]{:S(2)}, u32[]{:S(2)}) %collective-permute-start.11) | collective-permute-done | bytes 188448 | tf_op jit(solution)/shard_map/ppermute | solution.py:206
  127.3 0.7 collective-permute-start.13
  128.1 9.0 %all-to-all-done.1.parts_ref = bf16[16,64,640]{2,1,0:T(8,128)(2,1)S(1)} async-done(((bf16[16,64,640]{2,1,0:T(8,128)(2,1)}), bf16[16,64,640]{2,1,0:T(8,128)(2,1)S(1)}, u32[]{:S(2)}, u32[]{:S(2)}) %all-to-all-start.1) | async-done | bytes 1310752 | tf_op jit(solution)/shard_map/all_to_all | solution.py:251
  137.1 0.9 shard_map.89
  137.9 8.2 %all-to-all-start.2 = ((f32[32,8,128]{2,1,0:T(8,128)}), f32[32,8,128]{2,1,0:T(8,128)S(1)}, u32[]{:S(2)}, u32[]{:S(2)}) async-start(f32[32,8,128]{2,1,0:T(8,128)} %get-tuple-element.28), calls=%async_computation.2 | async-start | bytes 262144 | tf_op jit(solution)/shard_map/all_to_all | solution.py:269
  146.2 3.3 %collective-permute-start.14 = (bf16[368,128]{1,0:T(8,128)(2,1)S(1)}, bf16[368,128]{1,0:T(8,128)(2,1)S(1)}, u32[]{:S(2)}, u32[]{:S(2)}) collective-permute-start(bf16[368,128]{1,0:T(8,128)(2,1)S(1)} %get-tuple-element.46), channel_id=1, source_target_pairs={{0,2},{2,0},{4,130},{6,128},{8,10},{10,8},{12,138},{14,136},{128,6... | collective-permute-start | bytes 282632 | tf_op jit(solution)/shard_map/ppermute | solution.py:261
  149.4 6.2 %all-to-all-done.2.received_ref = f32[32,8,128]{2,1,0:T(8,128)S(1)} async-done(((f32[32,8,128]{2,1,0:T(8,128)}), f32[32,8,128]{2,1,0:T(8,128)S(1)}, u32[]{:S(2)}, u32[]{:S(2)}) %all-to-all-start.2) | async-done | bytes 131104 | tf_op jit(solution)/shard_map/all_to_all | solution.py:269
  155.6 0.8 shard_map.90
  156.4 9.0 %all-to-all-start.3 = ((f32[16,8,128]{2,1,0:T(8,128)}), f32[16,8,128]{2,1,0:T(8,128)S(1)}, u32[]{:S(2)}, u32[]{:S(2)}) async-start(f32[16,8,128]{2,1,0:T(8,128)} %get-tuple-element.30), calls=%async_computation.3 | async-start | bytes 131072 | tf_op jit(solution)/shard_map/all_to_all | solution.py:275
  165.4 0.7 add_convert_fusion.1
  166.1 9.1 %all-to-all-done.3.received_ref = f32[16,8,128]{2,1,0:T(8,128)S(1)} async-done(((f32[16,8,128]{2,1,0:T(8,128)}), f32[16,8,128]{2,1,0:T(8,128)S(1)}, u32[]{:S(2)}, u32[]{:S(2)}) %all-to-all-start.3) | async-done | bytes 65568 | tf_op jit(solution)/shard_map/all_to_all | solution.py:275
  175.2 1.0 shard_map.91
  (35 shorter events, 1.2 us)
Async XLA Ops:
  1.9 6.9 %collective-permute-start = (bf16[64,640]{1,0:T(8,128)(2,1)S(1)}, bf16[64,640]{1,0:T(8,128)(2,1)S(1)}, u32[]{:S(2)}, u32[]{:S(2)}) collective-permute-start(bf16[64,640]{1,0:T(8,128)(2,1)S(1)} %pad_maximum_fusion.4), channel_id=1, source_target_pairs={{0,256},{256,0},{1,257},{257,1},{2,258},{258,2},{3,259},{259,3},{4... | collective-permute-start | bytes 245768 | tf_op jit(solution)/shard_map/ppermute | solution.py:210
  6.9 1.9 %collective-permute-start.1 = (bf16[368,128]{1,0:T(8,128)(2,1)}, bf16[368,128]{1,0:T(8,128)(2,1)S(1)}, u32[]{:S(2)}, u32[]{:S(2)}) collective-permute-start(bf16[368,128]{1,0:T(8,128)(2,1)} %param.5), channel_id=1, source_target_pairs={{0,0},{2,2},{4,128},{6,130},{8,8},{10,10},{12,136},{14,138},{128,4... | collective-permute-start | bytes 282632 | tf_op jit(solution)/shard_map/ppermute | solution.py:217
  10.1 10.2 %copy-start.7 = (bf16[368,128]{1,0:T(8,128)(2,1)S(1)}, bf16[368,128]{1,0:T(8,128)(2,1)}, u32[]{:S(2)}) copy-start(bf16[368,128]{1,0:T(8,128)(2,1)} %param.5) | copy-start | bytes 282628
  10.1 48.6 %all-to-all-start = ((bf16[8,2,64,640]{3,2,1,0:T(8,128)(2,1)}), bf16[8,2,64,640]{3,2,1,0:T(8,128)(2,1)S(1)}, u32[]{:S(2)}, u32[]{:S(2)}) async-start(bf16[8,2,64,640]{3,2,1,0:T(8,128)(2,1)} %broadcast_in_dim.4), calls=%async_computation | async-start | bytes 2621440 | tf_op jit(solution)/shard_map/all_to_all | solution.py:191
  20.3 12.3 %collective-permute-start.2 = (bf16[368,128]{1,0:T(8,128)(2,1)S(1)}, bf16[368,128]{1,0:T(8,128)(2,1)S(1)}, u32[]{:S(2)}, u32[]{:S(2)}) collective-permute-start(bf16[368,128]{1,0:T(8,128)(2,1)S(1)} %copy-done.7), channel_id=1, source_target_pairs={{0,2},{2,0},{4,130},{6,128},{8,10},{10,8},{12,138},{14,136},{128,6... | collective-permute-start | bytes 282632 | tf_op jit(solution)/shard_map/ppermute | solution.py:218
  32.6 15.2 %collective-permute-start.4 = (bf16[2,368,128]{2,1,0:T(8,128)(2,1)S(1)}, bf16[2,368,128]{2,1,0:T(8,128)(2,1)S(1)}, u32[]{:S(2)}, u32[]{:S(2)}) collective-permute-start(bf16[2,368,128]{2,1,0:T(8,128)(2,1)S(1)} %get-tuple-element.48), channel_id=1, source_target_pairs={{0,8},{4,12},{8,0},{12,4},{1,9},{5,13},{9,1},{13,5},{2,10},{6,14},... | collective-permute-start | bytes 565256 | tf_op jit(solution)/shard_map/ppermute | solution.py:206
  37.3 12.7 %collective-permute-start.3 = (bf16[2,368,128]{2,1,0:T(8,128)(2,1)S(1)}, bf16[2,368,128]{2,1,0:T(8,128)(2,1)S(1)}, u32[]{:S(2)}, u32[]{:S(2)}) collective-permute-start(bf16[2,368,128]{2,1,0:T(8,128)(2,1)S(1)} %get-tuple-element.48), channel_id=1, source_target_pairs={{0,4},{4,8},{8,12},{12,0},{1,5},{5,9},{9,13},{13,1},{2,6},{6,10},{... | collective-permute-start | bytes 565256 | tf_op jit(solution)/shard_map/ppermute | solution.py:206
  45.8 6.8 %collective-permute-start.5 = (bf16[2,368,128]{2,1,0:T(8,128)(2,1)S(1)}, bf16[2,368,128]{2,1,0:T(8,128)(2,1)S(1)}, u32[]{:S(2)}, u32[]{:S(2)}) collective-permute-start(bf16[2,368,128]{2,1,0:T(8,128)(2,1)S(1)} %get-tuple-element.48), channel_id=1, source_target_pairs={{0,12},{4,0},{8,4},{12,8},{1,13},{5,1},{9,5},{13,9},{2,14},{6,2},{... | collective-permute-start | bytes 565256 | tf_op jit(solution)/shard_map/ppermute | solution.py:206
  52.7 6.0 %collective-permute-start.6 = (bf16[4,2,368,128]{3,2,1,0:T(8,128)(2,1)S(1)}, bf16[4,2,368,128]{3,2,1,0:T(8,128)(2,1)S(1)}, u32[]{:S(2)}, u32[]{:S(2)}) collective-permute-start(bf16[4,2,368,128]{3,2,1,0:T(8,128)(2,1)S(1)} %pad_maximum_fusion.own_ref), channel_id=1, source_target_pairs={{0,1},{1,0},{2,3},{3,2},{4,5},{5,4},{6,7},{7,6},{8,9},{9,8},{10,11... | collective-permute-start | bytes 2261000 | tf_op jit(solution)/shard_map/ppermute | solution.py:210
  58.7 5.4 %copy-start.5 = (bf16[368,320]{0,1:T(8,128)(2,1)S(1)}, bf16[368,320]{0,1:T(8,128)(2,1)}, u32[]{:S(2)}) copy-start(bf16[368,320]{0,1:T(8,128)(2,1)} %param.6) | copy-start | bytes 706564
  60.0 14.9 %collective-permute-start.7 = (bf16[368,640]{1,0:T(8,128)(2,1)S(1)}, bf16[368,640]{1,0:T(8,128)(2,1)}, u32[]{:S(2)}, u32[]{:S(2)}) collective-permute-start(bf16[368,640]{1,0:T(8,128)(2,1)S(1)} %shard_map.85), channel_id=1, source_target_pairs={{0,128},{128,0},{1,129},{129,1},{2,130},{130,2},{3,131},{131,3},{4... | collective-permute-start | bytes 1413128 | tf_op jit(solution)/shard_map/ppermute | solution.py:210
  66.3 9.7 %copy-start.4 = (bf16[368,320]{1,0:T(8,128)(2,1)S(1)}, bf16[368,320]{1,0:T(8,128)(2,1)}, u32[]{:S(2)}) copy-start(bf16[368,320]{1,0:T(8,128)(2,1)} %copy.9) | copy-start | bytes 706564
  76.7 13.1 %collective-permute-start.8 = (bf16[368,640]{1,0:T(8,128)(2,1)S(1)}, bf16[368,640]{1,0:T(8,128)(2,1)S(1)}, u32[]{:S(2)}, u32[]{:S(2)}) collective-permute-start(bf16[368,640]{1,0:T(8,128)(2,1)S(1)} %pad_maximum_fusion.1.hidden_ref.mine_ref), channel_id=1, source_target_pairs={{0,128},{128,0},{1,129},{129,1},{2,130},{130,2},{3,131},{131,3},{4... | collective-permute-start | bytes 1413128 | tf_op jit(solution)/shard_map/ppermute | solution.py:210
  89.9 1.5 copy-start.1
  91.4 1.1 copy-start
  92.5 44.6 %all-to-all-start.1 = ((bf16[16,64,640]{2,1,0:T(8,128)(2,1)}), bf16[16,64,640]{2,1,0:T(8,128)(2,1)S(1)}, u32[]{:S(2)}, u32[]{:S(2)}) async-start(bf16[16,64,640]{2,1,0:T(8,128)(2,1)} %bitcast.41), calls=%async_computation.1 | async-start | bytes 2621440 | tf_op jit(solution)/shard_map/all_to_all | solution.py:251
  101.9 1.0 copy-start.2
  104.8 5.8 %collective-permute-start.9 = (bf16[4,2,368,128]{3,2,1,0:T(8,128)(2,1)S(1)}, bf16[4,2,368,128]{3,2,1,0:T(8,128)(2,1)S(1)}, u32[]{:S(2)}, u32[]{:S(2)}) collective-permute-start(bf16[4,2,368,128]{3,2,1,0:T(8,128)(2,1)S(1)} %get-tuple-element.24), channel_id=1, source_target_pairs={{0,1},{1,0},{2,3},{3,2},{4,5},{5,4},{6,7},{7,6},{8,9},{9,8},{10,11... | collective-permute-start | bytes 2261000 | tf_op jit(solution)/shard_map/ppermute | solution.py:210
  110.7 10.6 %copy-start.6 = (f32[2,64]{1,0:T(2,128)S(1)}, f32[2,64]{1,0:T(2,128)}, u32[]{:S(2)}) copy-start(f32[2,64]{1,0:T(2,128)} %param.8) | copy-start | bytes 1540
  110.9 44.7 %copy-start.3 = (f32[2,320]{1,0:T(2,128)S(1)}, f32[2,320]{1,0:T(2,128)}, u32[]{:S(2)}) copy-start(f32[2,320]{1,0:T(2,128)} %col_moments_ref.1) | copy-start | bytes 7684
  110.9 10.5 %collective-permute-start.10 = (bf16[2,368,128]{2,1,0:T(8,128)(2,1)S(1)}, bf16[2,368,128]{2,1,0:T(8,128)(2,1)S(1)}, u32[]{:S(2)}, u32[]{:S(2)}) collective-permute-start(bf16[2,368,128]{2,1,0:T(8,128)(2,1)S(1)} %get-tuple-element.40), channel_id=1, source_target_pairs={{0,4},{4,8},{8,12},{12,0},{1,5},{5,9},{9,13},{13,1},{2,6},{6,10},{... | collective-permute-start | bytes 565256 | tf_op jit(solution)/shard_map/ppermute | solution.py:206
  112.8 9.0 %collective-permute-start.12 = (bf16[2,368,128]{2,1,0:T(8,128)(2,1)S(1)}, bf16[2,368,128]{2,1,0:T(8,128)(2,1)S(1)}, u32[]{:S(2)}, u32[]{:S(2)}) collective-permute-start(bf16[2,368,128]{2,1,0:T(8,128)(2,1)S(1)} %get-tuple-element.41), channel_id=1, source_target_pairs={{0,12},{4,0},{8,4},{12,8},{1,13},{5,1},{9,5},{13,9},{2,14},{6,2},{... | collective-permute-start | bytes 565256 | tf_op jit(solution)/shard_map/ppermute | solution.py:206
  118.2 9.0 %collective-permute-start.11 = (bf16[2,368,128]{2,1,0:T(8,128)(2,1)S(1)}, bf16[2,368,128]{2,1,0:T(8,128)(2,1)S(1)}, u32[]{:S(2)}, u32[]{:S(2)}) collective-permute-start(bf16[2,368,128]{2,1,0:T(8,128)(2,1)S(1)} %get-tuple-element.42), channel_id=1, source_target_pairs={{0,8},{4,12},{8,0},{12,4},{1,9},{5,13},{9,1},{13,5},{2,10},{6,14},... | collective-permute-start | bytes 565256 | tf_op jit(solution)/shard_map/ppermute | solution.py:206
  127.3 0.8 collective-permute-start.13
  137.9 17.7 %all-to-all-start.2 = ((f32[32,8,128]{2,1,0:T(8,128)}), f32[32,8,128]{2,1,0:T(8,128)S(1)}, u32[]{:S(2)}, u32[]{:S(2)}) async-start(f32[32,8,128]{2,1,0:T(8,128)} %get-tuple-element.28), calls=%async_computation.2 | async-start | bytes 262144 | tf_op jit(solution)/shard_map/all_to_all | solution.py:269
  146.2 19.3 %collective-permute-start.14 = (bf16[368,128]{1,0:T(8,128)(2,1)S(1)}, bf16[368,128]{1,0:T(8,128)(2,1)S(1)}, u32[]{:S(2)}, u32[]{:S(2)}) collective-permute-start(bf16[368,128]{1,0:T(8,128)(2,1)S(1)} %get-tuple-element.46), channel_id=1, source_target_pairs={{0,2},{2,0},{4,130},{6,128},{8,10},{10,8},{12,138},{14,136},{128,6... | collective-permute-start | bytes 282632 | tf_op jit(solution)/shard_map/ppermute | solution.py:261
  156.4 18.7 %all-to-all-start.3 = ((f32[16,8,128]{2,1,0:T(8,128)}), f32[16,8,128]{2,1,0:T(8,128)S(1)}, u32[]{:S(2)}, u32[]{:S(2)}) async-start(f32[16,8,128]{2,1,0:T(8,128)} %get-tuple-element.30), calls=%async_computation.3 | async-start | bytes 131072 | tf_op jit(solution)/shard_map/all_to_all | solution.py:275

commit v5 on v4

--- a/solution.py
+++ b/solution.py
@@ -97,8 +97,8 @@
             mine_row = weight_places(place_ref, 0, 0, j, -1)[0]
             product = product + mine_ref[(mine_row + row) % 2, j]
             product = (product * SCALING).astype(BF16)
-            out_ref[row, first] = product[:FEAT]
-            out_ref[row, second] = product[FEAT:]
+            for k in range(4):
+                out_ref[second if k // 2 else first, k % 2, row] = product[k * ROWS : (k + 1) * ROWS]
 
 
 def input_kernel(place_ref, mine_ref, pair_ref, w_ref, own_ref, other_ref):
@@ -114,10 +114,8 @@
                 other_ref[e, j] = product[:, FEAT:]
 
 
-def squares_kernel(parts_ref, stats_ref, own_ref, payload_ref, rows_ref):
-    own = parts_ref[0].astype(F32)
-    for part in range(1, N_GROUP):
-        own = own + parts_ref[part].astype(F32)
+def squares_kernel(part_ref, received_ref, stats_ref, own_ref, payload_ref, rows_ref):
+    own = part_ref[...] + received_ref[...].astype(F32)
     own_ref[...] = own
     squares = own * own + 1e-30
     cols = jnp.sum(squares, axis=0, keepdims=True)
@@ -231,7 +229,7 @@
 
     flops = 2 * TOK * (D // 2) * 2 * COLS
     wide = (TOK, 2 * COLS)
-    grads_shape = (N_YH, N_X, 2 * ROWS, 2 * COLS)
+    grads_shape = (N_Z // 2, 2, N_YH, ROWS, 2 * COLS)
     for_pair = call(functools.partial(product_kernel, 1), struct(wide, BF16), flops, place, blocks, others, full)
     mine = call(functools.partial(product_kernel, 0), struct(wide), flops, place, blocks, others, full)
     summed = (mine + exchange(for_pair, "yl").astype(F32)) * SCALING
@@ -248,7 +246,10 @@
     grads = call(
         grads_sum_kernel, struct(grads_shape, BF16), flops, place, blocks, others, pair_hidden, grads
     )
-    parts = lax.all_to_all(grads.reshape(N_GROUP, ROWS, 2 * COLS), GROUP, 0, 0, tiled=True)
+    parts = lax.all_to_all(grads.reshape(N_Z, N_YH, ROWS, 2 * COLS), "z", 0, 0, tiled=True)
+    parts = jnp.sum(parts.astype(F32), axis=0)
+    own_part = jnp.where(first, parts[0], parts[1])
+    parts = exchange(jnp.where(first, parts[1], parts[0]).astype(BF16), "yh")
 
     shape = struct((N_X, N_YHI, TOK, FEAT), BF16)
     terms, others = call(input_kernel, [shape, shape], 2 * flops, place, hidden, pair_hidden, full)
@@ -264,7 +265,7 @@
 
     stats, half_moments, hidden = barrier((stats, 0.5 * row_moments, hidden))
     own, payload, rows = call(
-        squares_kernel, [struct((ROWS, 2 * COLS)), struct((N_DP, 8, 128)), struct((8, 128))], 10**6, parts, stats
+        squares_kernel, [struct((ROWS, 2 * COLS)), struct((N_DP, 8, 128)), struct((8, 128))], 10**6, own_part, parts, stats
     )
     received = lax.all_to_all(payload, DP, 0, 0, tiled=True)
     payload, new_cols, kept, cols = call(

time: 177 us -> 181 us (1.023)
  waiting for transfers between devices: 57.9 us -> 60.4 us
    ppermute x5 -> x6, starting transfers between devices: 20.2 us -> 26.7 us  [exchange(): return lax.ppermute(values, axis, [(0, 1), (1, 0)])]
    ppermute x5 -> x6, waiting for transfers between devices: 21 us -> 25.2 us  [exchange(): return lax.ppermute(values, axis, [(0, 1), (1, 0)])]
    all_to_all x1, starting transfers between devices: 9.37 us -> 5.42 us  [shards(): lax.all_to_all(grads.reshape(N_Z, N_YH, ROWS, 2 * COLS), 'z', 0, 0, tiled...]
    all_to_all x1, starting transfers between devices: 8.22 us -> 4.59 us  [shards(): received = lax.all_to_all(payload, DP, 0, 0, tiled=True)]
    all_to_all x1, waiting for transfers between devices: 6.16 us -> 3.95 us  [shards(): received = lax.all_to_all(payload, DP, 0, 0, tiled=True)]
    ppermute x1, starting transfers between devices: 3.28 us -> 5.39 us  [shards(): far = lax.ppermute(total[1], PLANE, home_pairs(1))]
  transfers between devices with their start and end apart: 19 -> 20, of which waited for: 13 -> 14; matrix products, arithmetic and copies ran while one was open for 1% -> 2% of each run, Pallas kernels for 3% -> 3%
where the time goes in v5:
time: 181 us; the launch traced here: 180 us
  starting transfers between devices  98.8 us (55%)
  waiting for transfers between devices  60.4 us (33%)
  Pallas kernels  10.1 us (6%)
  other arithmetic  6.08 us (3%)
  local copies, waits for them, and re-layouts  3.29 us (2%)
    ppermute x6, starting transfers between devices, exchange(): return lax.ppermute(values, axis, [(0, 1), (1, 0)])  26.7 us
    ppermute x6, starting transfers between devices, x_shift(): lax.ppermute(values, 'x', [(i, (i + step) % N_X) for i in range(N_X)])  25.4 us
    ppermute x6, waiting for transfers between devices, exchange(): return lax.ppermute(values, axis, [(0, 1), (1, 0)])  25.2 us
    ppermute x6, waiting for transfers between devices, x_shift(): lax.ppermute(values, 'x', [(i, (i + step) % N_X) for i in range(N_X)])  10.5 us
    all_to_all x1, starting transfers between devices, spread(): lax.all_to_all(jnp.broadcast_to(values[None], (size,) + values.shape), ax...  10.2 us
    pallas_call x8, Pallas kernels, call(): pl.pallas_call(kernel, out_shape=out_shape, in_specs=specs, out_specs=jax...  10.1 us
    ppermute x1, starting transfers between devices, shards(): far = lax.ppermute(tokens, PLANE, home_pairs(1))  10.1 us
    all_to_all x1, waiting for transfers between devices, shards(): lax.all_to_all(grads.reshape(N_Z, N_YH, ROWS, 2 * COLS), 'z', 0, 0, tiled...  9.61 us
  transfers between devices with their start and end apart: 20, of which 14 were waited for; matrix products, arithmetic and copies ran while one was open for 2% of the time, Pallas kernels for 3%

profile of v5, /device:TPU:1, one launch (start us, length us, event | category | flops | bytes accessed | tf_op | source)
XLA Modules:
  0.0 179.7 jit_solution(13290896704592199299)
XLA Ops:
  0.6 1.1 multiply_reduce_fusion
  1.9 5.0 %collective-permute-start = (bf16[64,640]{1,0:T(8,128)(2,1)S(1)}, bf16[64,640]{1,0:T(8,128)(2,1)S(1)}, u32[]{:S(2)}, u32[]{:S(2)}) collective-permute-start(bf16[64,640]{1,0:T(8,128)(2,1)S(1)} %pad_maximum_fusion.4), channel_id=1, source_target_pairs={{0,256},{256,0},{1,257},{257,1},{2,258},{258,2},{3,259},{259,3},{4... | collective-permute-start | bytes 245768 | tf_op jit(solution)/shard_map/ppermute | solution.py:208
  6.9 1.6 collective-permute-start.1
  8.9 1.2 broadcast_in_dim.4
  10.1 10.2 %all-to-all-start = ((bf16[8,2,64,640]{3,2,1,0:T(8,128)(2,1)}), bf16[8,2,64,640]{3,2,1,0:T(8,128)(2,1)S(1)}, u32[]{:S(2)}, u32[]{:S(2)}) async-start(bf16[8,2,64,640]{3,2,1,0:T(8,128)(2,1)} %broadcast_in_dim.4), calls=%async_computation | async-start | bytes 2621440 | tf_op jit(solution)/shard_map/all_to_all | solution.py:189
  20.3 10.1 %collective-permute-start.2 = (bf16[368,128]{1,0:T(8,128)(2,1)S(1)}, bf16[368,128]{1,0:T(8,128)(2,1)S(1)}, u32[]{:S(2)}, u32[]{:S(2)}) collective-permute-start(bf16[368,128]{1,0:T(8,128)(2,1)S(1)} %copy-done.7), channel_id=1, source_target_pairs={{0,2},{2,0},{4,130},{6,128},{8,10},{10,8},{12,138},{14,136},{128,6... | collective-permute-start | bytes 282632 | tf_op jit(solution)/shard_map/ppermute | solution.py:216
  30.5 2.2 %collective-permute-done.2 = bf16[368,128]{1,0:T(8,128)(2,1)S(1)} collective-permute-done((bf16[368,128]{1,0:T(8,128)(2,1)S(1)}, bf16[368,128]{1,0:T(8,128)(2,1)S(1)}, u32[]{:S(2)}, u32[]{:S(2)}) %collective-permute-start.2) | collective-permute-done | bytes 94240 | tf_op jit(solution)/shard_map/ppermute | solution.py:216
  32.6 4.7 %collective-permute-start.4 = (bf16[2,368,128]{2,1,0:T(8,128)(2,1)S(1)}, bf16[2,368,128]{2,1,0:T(8,128)(2,1)S(1)}, u32[]{:S(2)}, u32[]{:S(2)}) collective-permute-start(bf16[2,368,128]{2,1,0:T(8,128)(2,1)S(1)} %get-tuple-element.48), channel_id=1, source_target_pairs={{0,8},{4,12},{8,0},{12,4},{1,9},{5,13},{9,1},{13,5},{2,10},{6,14},... | collective-permute-start | bytes 565256 | tf_op jit(solution)/shard_map/ppermute | solution.py:204
  37.3 8.5 %collective-permute-start.3 = (bf16[2,368,128]{2,1,0:T(8,128)(2,1)S(1)}, bf16[2,368,128]{2,1,0:T(8,128)(2,1)S(1)}, u32[]{:S(2)}, u32[]{:S(2)}) collective-permute-start(bf16[2,368,128]{2,1,0:T(8,128)(2,1)S(1)} %get-tuple-element.48), channel_id=1, source_target_pairs={{0,4},{4,8},{8,12},{12,0},{1,5},{5,9},{9,13},{13,1},{2,6},{6,10},{... | collective-permute-start | bytes 565256 | tf_op jit(solution)/shard_map/ppermute | solution.py:204
  45.8 2.0 %collective-permute-start.5 = (bf16[2,368,128]{2,1,0:T(8,128)(2,1)S(1)}, bf16[2,368,128]{2,1,0:T(8,128)(2,1)S(1)}, u32[]{:S(2)}, u32[]{:S(2)}) collective-permute-start(bf16[2,368,128]{2,1,0:T(8,128)(2,1)S(1)} %get-tuple-element.48), channel_id=1, source_target_pairs={{0,12},{4,0},{8,4},{12,8},{1,13},{5,1},{9,5},{13,9},{2,14},{6,2},{... | collective-permute-start | bytes 565256 | tf_op jit(solution)/shard_map/ppermute | solution.py:204
  47.9 2.2 %collective-permute-done.3 = bf16[2,368,128]{2,1,0:T(8,128)(2,1)S(1)} collective-permute-done((bf16[2,368,128]{2,1,0:T(8,128)(2,1)S(1)}, bf16[2,368,128]{2,1,0:T(8,128)(2,1)S(1)}, u32[]{:S(2)}, u32[]{:S(2)}) %collective-permute-start.3) | collective-permute-done | bytes 188448 | tf_op jit(solution)/shard_map/ppermute | solution.py:204
  50.0 2.6 %collective-permute-done.5 = bf16[2,368,128]{2,1,0:T(8,128)(2,1)S(1)} collective-permute-done((bf16[2,368,128]{2,1,0:T(8,128)(2,1)S(1)}, bf16[2,368,128]{2,1,0:T(8,128)(2,1)S(1)}, u32[]{:S(2)}, u32[]{:S(2)}) %collective-permute-start.5) | collective-permute-done | bytes 188448 | tf_op jit(solution)/shard_map/ppermute | solution.py:204
  52.7 4.1 %collective-permute-start.6 = (bf16[4,2,368,128]{3,2,1,0:T(8,128)(2,1)S(1)}, bf16[4,2,368,128]{3,2,1,0:T(8,128)(2,1)S(1)}, u32[]{:S(2)}, u32[]{:S(2)}) collective-permute-start(bf16[4,2,368,128]{3,2,1,0:T(8,128)(2,1)S(1)} %pad_maximum_fusion.own_ref), channel_id=1, source_target_pairs={{0,1},{1,0},{2,3},{3,2},{4,5},{5,4},{6,7},{7,6},{8,9},{9,8},{10,11... | collective-permute-start | bytes 2261000 | tf_op jit(solution)/shard_map/ppermute | solution.py:208
  57.0 1.8 collective-permute-done.6.other_ref
  58.7 1.3 shard_map.85
  60.0 4.1 %collective-permute-start.7 = (bf16[368,640]{1,0:T(8,128)(2,1)S(1)}, bf16[368,640]{1,0:T(8,128)(2,1)}, u32[]{:S(2)}, u32[]{:S(2)}) collective-permute-start(bf16[368,640]{1,0:T(8,128)(2,1)S(1)} %shard_map.85), channel_id=1, source_target_pairs={{0,128},{128,0},{1,129},{129,1},{2,130},{130,2},{3,131},{131,3},{4... | collective-permute-start | bytes 1413128 | tf_op jit(solution)/shard_map/ppermute | solution.py:208
  64.1 0.9 copy.9
  65.0 1.3 shard_map.84
  66.4 8.6 %collective-permute-done.7 = bf16[368,640]{1,0:T(8,128)(2,1)} collective-permute-done((bf16[368,640]{1,0:T(8,128)(2,1)S(1)}, bf16[368,640]{1,0:T(8,128)(2,1)}, u32[]{:S(2)}, u32[]{:S(2)}) %collective-permute-start.7) | collective-permute-done | bytes 471072 | tf_op jit(solution)/shard_map/ppermute | solution.py:208
  74.9 1.1 add_multiply_fusion
  76.1 0.5 fusion.1
  76.7 3.0 %collective-permute-start.8 = (bf16[368,640]{1,0:T(8,128)(2,1)S(1)}, bf16[368,640]{1,0:T(8,128)(2,1)S(1)}, u32[]{:S(2)}, u32[]{:S(2)}) collective-permute-start(bf16[368,640]{1,0:T(8,128)(2,1)S(1)} %pad_maximum_fusion.1.hidden_ref.mine_ref), channel_id=1, source_target_pairs={{0,128},{128,0},{1,129},{129,1},{2,130},{130,2},{3,131},{131,3},{4... | collective-permute-start | bytes 1413128 | tf_op jit(solution)/shard_map/ppermute | solution.py:208
  79.8 1.5 shard_map.86.mine_ref
  81.3 8.6 %collective-permute-done.8.hidden_ref.pair_ref = bf16[368,640]{1,0:T(8,128)(2,1)S(1)} collective-permute-done((bf16[368,640]{1,0:T(8,128)(2,1)S(1)}, bf16[368,640]{1,0:T(8,128)(2,1)S(1)}, u32[]{:S(2)}, u32[]{:S(2)}) %collective-permute-start.8) | collective-permute-done | bytes 471072 | tf_op jit(solution)/shard_map/ppermute | solution.py:208
  89.9 1.5 shard_map.87
  91.4 1.1 copy-done
  92.5 5.4 %all-to-all-start.1 = ((bf16[8,2,64,640]{3,2,1,0:T(8,128)(2,1)}), bf16[8,2,64,640]{3,2,1,0:T(8,128)(2,1)}, u32[]{:S(2)}, u32[]{:S(2)}) async-start(bf16[8,2,64,640]{3,2,1,0:T(8,128)(2,1)} %bitcast.45), calls=%async_computation.1 | async-start | bytes 2621440 | tf_op jit(solution)/shard_map/all_to_all | solution.py:249
  97.9 1.9 %shard_map.88 = (bf16[4,2,368,128]{3,2,1,0:T(8,128)(2,1)S(1)}, bf16[4,2,368,128]{3,2,1,0:T(8,128)(2,1)S(1)}) custom-call(s32[4]{0:T(128)S(1)} %pad_add_fusion.place_ref, bf16[368,640]{1,0:T(8,128)(2,1)S(1)} %pad_maximum_fusion.1.hidden_ref.mine_ref, bf16[368,640]{1,0:T(8,128)(2,1)S(1)} %copy-done.2, bf16[4,2,2,64,640]{4,3,2,1,0:T(8,128)(2,1)S(1)} %bitcast.44), custom_call_target="tpu_custom_call" | custom-call | flops 964689920 | bytes 4194304 | tf_op jit(solution)/shard_map/pallas_call | solution.py:173
  99.9 4.3 %collective-permute-start.10 = (bf16[4,2,368,128]{3,2,1,0:T(8,128)(2,1)S(1)}, bf16[4,2,368,128]{3,2,1,0:T(8,128)(2,1)S(1)}, u32[]{:S(2)}, u32[]{:S(2)}) collective-permute-start(bf16[4,2,368,128]{3,2,1,0:T(8,128)(2,1)S(1)} %get-tuple-element.24), channel_id=1, source_target_pairs={{0,1},{1,0},{2,3},{3,2},{4,5},{5,4},{6,7},{7,6},{8,9},{9,8},{10,11... | collective-permute-start | bytes 2261000 | tf_op jit(solution)/shard_map/ppermute | solution.py:208
  104.2 1.8 %collective-permute-done.10 = bf16[4,2,368,128]{3,2,1,0:T(8,128)(2,1)S(1)} collective-permute-done((bf16[4,2,368,128]{3,2,1,0:T(8,128)(2,1)S(1)}, bf16[4,2,368,128]{3,2,1,0:T(8,128)(2,1)S(1)}, u32[]{:S(2)}, u32[]{:S(2)}) %collective-permute-start.10) | collective-permute-done | bytes 753696 | tf_op jit(solution)/shard_map/ppermute | solution.py:208
  106.3 2.0 %collective-permute-start.11 = (bf16[2,368,128]{2,1,0:T(8,128)(2,1)S(1)}, bf16[2,368,128]{2,1,0:T(8,128)(2,1)S(1)}, u32[]{:S(2)}, u32[]{:S(2)}) collective-permute-start(bf16[2,368,128]{2,1,0:T(8,128)(2,1)S(1)} %get-tuple-element.40), channel_id=1, source_target_pairs={{0,4},{4,8},{8,12},{12,0},{1,5},{5,9},{9,13},{13,1},{2,6},{6,10},{... | collective-permute-start | bytes 565256 | tf_op jit(solution)/shard_map/ppermute | solution.py:204
  108.3 5.1 %collective-permute-start.13 = (bf16[2,368,128]{2,1,0:T(8,128)(2,1)S(1)}, bf16[2,368,128]{2,1,0:T(8,128)(2,1)S(1)}, u32[]{:S(2)}, u32[]{:S(2)}) collective-permute-start(bf16[2,368,128]{2,1,0:T(8,128)(2,1)S(1)} %get-tuple-element.41), channel_id=1, source_target_pairs={{0,12},{4,0},{8,4},{12,8},{1,13},{5,1},{9,5},{13,9},{2,14},{6,2},{... | collective-permute-start | bytes 565256 | tf_op jit(solution)/shard_map/ppermute | solution.py:204
  113.4 3.1 %collective-permute-start.12 = (bf16[2,368,128]{2,1,0:T(8,128)(2,1)S(1)}, bf16[2,368,128]{2,1,0:T(8,128)(2,1)S(1)}, u32[]{:S(2)}, u32[]{:S(2)}) collective-permute-start(bf16[2,368,128]{2,1,0:T(8,128)(2,1)S(1)} %get-tuple-element.42), channel_id=1, source_target_pairs={{0,8},{4,12},{8,0},{12,4},{1,9},{5,13},{9,1},{13,5},{2,10},{6,14},... | collective-permute-start | bytes 565256 | tf_op jit(solution)/shard_map/ppermute | solution.py:204
  117.1 5.3 %collective-permute-done.12 = bf16[2,368,128]{2,1,0:T(8,128)(2,1)S(1)} collective-permute-done((bf16[2,368,128]{2,1,0:T(8,128)(2,1)S(1)}, bf16[2,368,128]{2,1,0:T(8,128)(2,1)S(1)}, u32[]{:S(2)}, u32[]{:S(2)}) %collective-permute-start.12) | collective-permute-done | bytes 188448 | tf_op jit(solution)/shard_map/ppermute | solution.py:204
  122.6 0.7 collective-permute-start.14
  123.2 9.6 %all-to-all-done.1 = bf16[8,2,64,640]{3,2,1,0:T(8,128)(2,1)} async-done(((bf16[8,2,64,640]{3,2,1,0:T(8,128)(2,1)}), bf16[8,2,64,640]{3,2,1,0:T(8,128)(2,1)}, u32[]{:S(2)}, u32[]{:S(2)}) %all-to-all-start.1) | async-done | bytes 1310752 | tf_op jit(solution)/shard_map/all_to_all | solution.py:249
  132.8 1.5 convert_reduce_fusion
  134.4 6.2 %collective-permute-start.9 = (bf16[64,640]{1,0:T(8,128)(2,1)S(1)}, bf16[64,640]{1,0:T(8,128)(2,1)S(1)}, u32[]{:S(2)}, u32[]{:S(2)}) collective-permute-start(bf16[64,640]{1,0:T(8,128)(2,1)S(1)} %fusion.13), channel_id=1, source_target_pairs={{0,256},{256,0},{1,257},{257,1},{2,258},{258,2},{3,259},{259,3},{4... | collective-permute-start | bytes 245768 | tf_op jit(solution)/shard_map/ppermute | solution.py:208
  140.6 4.2 %collective-permute-done.9.received_ref = bf16[64,640]{1,0:T(8,128)(2,1)S(1)} collective-permute-done((bf16[64,640]{1,0:T(8,128)(2,1)S(1)}, bf16[64,640]{1,0:T(8,128)(2,1)S(1)}, u32[]{:S(2)}, u32[]{:S(2)}) %collective-permute-start.9) | collective-permute-done | bytes 81952 | tf_op jit(solution)/shard_map/ppermute | solution.py:208
  144.8 0.7 shard_map.89
  145.5 4.6 %all-to-all-start.2 = ((f32[32,8,128]{2,1,0:T(8,128)}), f32[32,8,128]{2,1,0:T(8,128)S(1)}, u32[]{:S(2)}, u32[]{:S(2)}) async-start(f32[32,8,128]{2,1,0:T(8,128)} %get-tuple-element.28), calls=%async_computation.2 | async-start | bytes 262144 | tf_op jit(solution)/shard_map/all_to_all | solution.py:270
  150.1 5.4 %collective-permute-start.15 = (bf16[368,128]{1,0:T(8,128)(2,1)S(1)}, bf16[368,128]{1,0:T(8,128)(2,1)S(1)}, u32[]{:S(2)}, u32[]{:S(2)}) collective-permute-start(bf16[368,128]{1,0:T(8,128)(2,1)S(1)} %get-tuple-element.46), channel_id=1, source_target_pairs={{0,2},{2,0},{4,130},{6,128},{8,10},{10,8},{12,138},{14,136},{128,6... | collective-permute-start | bytes 282632 | tf_op jit(solution)/shard_map/ppermute | solution.py:262
  155.5 4.0 %all-to-all-done.2.received_ref = f32[32,8,128]{2,1,0:T(8,128)S(1)} async-done(((f32[32,8,128]{2,1,0:T(8,128)}), f32[32,8,128]{2,1,0:T(8,128)S(1)}, u32[]{:S(2)}, u32[]{:S(2)}) %all-to-all-start.2) | async-done | bytes 131104 | tf_op jit(solution)/shard_map/all_to_all | solution.py:270
  159.4 0.8 shard_map.90
  160.2 8.7 %all-to-all-start.3 = ((f32[16,8,128]{2,1,0:T(8,128)}), f32[16,8,128]{2,1,0:T(8,128)S(1)}, u32[]{:S(2)}, u32[]{:S(2)}) async-start(f32[16,8,128]{2,1,0:T(8,128)} %get-tuple-element.30), calls=%async_computation.3 | async-start | bytes 131072 | tf_op jit(solution)/shard_map/all_to_all | solution.py:276
  169.0 0.7 add_convert_fusion.1
  169.6 9.1 %all-to-all-done.3.received_ref = f32[16,8,128]{2,1,0:T(8,128)S(1)} async-done(((f32[16,8,128]{2,1,0:T(8,128)}), f32[16,8,128]{2,1,0:T(8,128)S(1)}, u32[]{:S(2)}, u32[]{:S(2)}) %all-to-all-start.3) | async-done | bytes 65568 | tf_op jit(solution)/shard_map/all_to_all | solution.py:276
  178.7 1.0 shard_map.91
  (40 shorter events, 1.9 us)
Async XLA Ops:
  1.9 6.9 %collective-permute-start = (bf16[64,640]{1,0:T(8,128)(2,1)S(1)}, bf16[64,640]{1,0:T(8,128)(2,1)S(1)}, u32[]{:S(2)}, u32[]{:S(2)}) collective-permute-start(bf16[64,640]{1,0:T(8,128)(2,1)S(1)} %pad_maximum_fusion.4), channel_id=1, source_target_pairs={{0,256},{256,0},{1,257},{257,1},{2,258},{258,2},{3,259},{259,3},{4... | collective-permute-start | bytes 245768 | tf_op jit(solution)/shard_map/ppermute | solution.py:208
  6.9 1.9 %collective-permute-start.1 = (bf16[368,128]{1,0:T(8,128)(2,1)}, bf16[368,128]{1,0:T(8,128)(2,1)S(1)}, u32[]{:S(2)}, u32[]{:S(2)}) collective-permute-start(bf16[368,128]{1,0:T(8,128)(2,1)} %param.5), channel_id=1, source_target_pairs={{0,0},{2,2},{4,128},{6,130},{8,8},{10,10},{12,136},{14,138},{128,4... | collective-permute-start | bytes 282632 | tf_op jit(solution)/shard_map/ppermute | solution.py:215
  10.1 10.2 %copy-start.7 = (bf16[368,128]{1,0:T(8,128)(2,1)S(1)}, bf16[368,128]{1,0:T(8,128)(2,1)}, u32[]{:S(2)}) copy-start(bf16[368,128]{1,0:T(8,128)(2,1)} %param.5) | copy-start | bytes 282628
  10.1 48.6 %all-to-all-start = ((bf16[8,2,64,640]{3,2,1,0:T(8,128)(2,1)}), bf16[8,2,64,640]{3,2,1,0:T(8,128)(2,1)S(1)}, u32[]{:S(2)}, u32[]{:S(2)}) async-start(bf16[8,2,64,640]{3,2,1,0:T(8,128)(2,1)} %broadcast_in_dim.4), calls=%async_computation | async-start | bytes 2621440 | tf_op jit(solution)/shard_map/all_to_all | solution.py:189
  20.3 12.3 %collective-permute-start.2 = (bf16[368,128]{1,0:T(8,128)(2,1)S(1)}, bf16[368,128]{1,0:T(8,128)(2,1)S(1)}, u32[]{:S(2)}, u32[]{:S(2)}) collective-permute-start(bf16[368,128]{1,0:T(8,128)(2,1)S(1)} %copy-done.7), channel_id=1, source_target_pairs={{0,2},{2,0},{4,130},{6,128},{8,10},{10,8},{12,138},{14,136},{128,6... | collective-permute-start | bytes 282632 | tf_op jit(solution)/shard_map/ppermute | solution.py:216
  32.6 15.2 %collective-permute-start.4 = (bf16[2,368,128]{2,1,0:T(8,128)(2,1)S(1)}, bf16[2,368,128]{2,1,0:T(8,128)(2,1)S(1)}, u32[]{:S(2)}, u32[]{:S(2)}) collective-permute-start(bf16[2,368,128]{2,1,0:T(8,128)(2,1)S(1)} %get-tuple-element.48), channel_id=1, source_target_pairs={{0,8},{4,12},{8,0},{12,4},{1,9},{5,13},{9,1},{13,5},{2,10},{6,14},... | collective-permute-start | bytes 565256 | tf_op jit(solution)/shard_map/ppermute | solution.py:204
  37.3 12.7 %collective-permute-start.3 = (bf16[2,368,128]{2,1,0:T(8,128)(2,1)S(1)}, bf16[2,368,128]{2,1,0:T(8,128)(2,1)S(1)}, u32[]{:S(2)}, u32[]{:S(2)}) collective-permute-start(bf16[2,368,128]{2,1,0:T(8,128)(2,1)S(1)} %get-tuple-element.48), channel_id=1, source_target_pairs={{0,4},{4,8},{8,12},{12,0},{1,5},{5,9},{9,13},{13,1},{2,6},{6,10},{... | collective-permute-start | bytes 565256 | tf_op jit(solution)/shard_map/ppermute | solution.py:204
  45.8 6.8 %collective-permute-start.5 = (bf16[2,368,128]{2,1,0:T(8,128)(2,1)S(1)}, bf16[2,368,128]{2,1,0:T(8,128)(2,1)S(1)}, u32[]{:S(2)}, u32[]{:S(2)}) collective-permute-start(bf16[2,368,128]{2,1,0:T(8,128)(2,1)S(1)} %get-tuple-element.48), channel_id=1, source_target_pairs={{0,12},{4,0},{8,4},{12,8},{1,13},{5,1},{9,5},{13,9},{2,14},{6,2},{... | collective-permute-start | bytes 565256 | tf_op jit(solution)/shard_map/ppermute | solution.py:204
  52.7 6.0 %collective-permute-start.6 = (bf16[4,2,368,128]{3,2,1,0:T(8,128)(2,1)S(1)}, bf16[4,2,368,128]{3,2,1,0:T(8,128)(2,1)S(1)}, u32[]{:S(2)}, u32[]{:S(2)}) collective-permute-start(bf16[4,2,368,128]{3,2,1,0:T(8,128)(2,1)S(1)} %pad_maximum_fusion.own_ref), channel_id=1, source_target_pairs={{0,1},{1,0},{2,3},{3,2},{4,5},{5,4},{6,7},{7,6},{8,9},{9,8},{10,11... | collective-permute-start | bytes 2261000 | tf_op jit(solution)/shard_map/ppermute | solution.py:208
  58.7 5.4 %copy-start.5 = (bf16[368,320]{0,1:T(8,128)(2,1)S(1)}, bf16[368,320]{0,1:T(8,128)(2,1)}, u32[]{:S(2)}) copy-start(bf16[368,320]{0,1:T(8,128)(2,1)} %param.6) | copy-start | bytes 706564
  60.0 14.9 %collective-permute-start.7 = (bf16[368,640]{1,0:T(8,128)(2,1)S(1)}, bf16[368,640]{1,0:T(8,128)(2,1)}, u32[]{:S(2)}, u32[]{:S(2)}) collective-permute-start(bf16[368,640]{1,0:T(8,128)(2,1)S(1)} %shard_map.85), channel_id=1, source_target_pairs={{0,128},{128,0},{1,129},{129,1},{2,130},{130,2},{3,131},{131,3},{4... | collective-permute-start | bytes 1413128 | tf_op jit(solution)/shard_map/ppermute | solution.py:208
  66.3 9.7 %copy-start.4 = (bf16[368,320]{1,0:T(8,128)(2,1)S(1)}, bf16[368,320]{1,0:T(8,128)(2,1)}, u32[]{:S(2)}) copy-start(bf16[368,320]{1,0:T(8,128)(2,1)} %copy.9) | copy-start | bytes 706564
  76.7 13.1 %collective-permute-start.8 = (bf16[368,640]{1,0:T(8,128)(2,1)S(1)}, bf16[368,640]{1,0:T(8,128)(2,1)S(1)}, u32[]{:S(2)}, u32[]{:S(2)}) collective-permute-start(bf16[368,640]{1,0:T(8,128)(2,1)S(1)} %pad_maximum_fusion.1.hidden_ref.mine_ref), channel_id=1, source_target_pairs={{0,128},{128,0},{1,129},{129,1},{2,130},{130,2},{3,131},{131,3},{4... | collective-permute-start | bytes 1413128 | tf_op jit(solution)/shard_map/ppermute | solution.py:208
  89.9 1.5 copy-start.1
  91.4 1.1 copy-start
  92.5 5.4 %copy-start.2 = (bf16[368,640]{1,0:T(8,128)(2,1)S(1)}, bf16[368,640]{1,0:T(8,128)(2,1)}, u32[]{:S(2)}) copy-start(bf16[368,640]{1,0:T(8,128)(2,1)} %copy-done.1) | copy-start | bytes 1413124
  92.5 40.3 %all-to-all-start.1 = ((bf16[8,2,64,640]{3,2,1,0:T(8,128)(2,1)}), bf16[8,2,64,640]{3,2,1,0:T(8,128)(2,1)}, u32[]{:S(2)}, u32[]{:S(2)}) async-start(bf16[8,2,64,640]{3,2,1,0:T(8,128)(2,1)} %bitcast.45), calls=%async_computation.1 | async-start | bytes 2621440 | tf_op jit(solution)/shard_map/all_to_all | solution.py:249
  99.9 6.2 %collective-permute-start.10 = (bf16[4,2,368,128]{3,2,1,0:T(8,128)(2,1)S(1)}, bf16[4,2,368,128]{3,2,1,0:T(8,128)(2,1)S(1)}, u32[]{:S(2)}, u32[]{:S(2)}) collective-permute-start(bf16[4,2,368,128]{3,2,1,0:T(8,128)(2,1)S(1)} %get-tuple-element.24), channel_id=1, source_target_pairs={{0,1},{1,0},{2,3},{3,2},{4,5},{5,4},{6,7},{7,6},{8,9},{9,8},{10,11... | collective-permute-start | bytes 2261000 | tf_op jit(solution)/shard_map/ppermute | solution.py:208
  106.0 10.5 %copy-start.6 = (f32[2,64]{1,0:T(2,128)S(1)}, f32[2,64]{1,0:T(2,128)}, u32[]{:S(2)}) copy-start(f32[2,64]{1,0:T(2,128)} %param.8) | copy-start | bytes 1540
  106.3 10.4 %collective-permute-start.11 = (bf16[2,368,128]{2,1,0:T(8,128)(2,1)S(1)}, bf16[2,368,128]{2,1,0:T(8,128)(2,1)S(1)}, u32[]{:S(2)}, u32[]{:S(2)}) collective-permute-start(bf16[2,368,128]{2,1,0:T(8,128)(2,1)S(1)} %get-tuple-element.40), channel_id=1, source_target_pairs={{0,4},{4,8},{8,12},{12,0},{1,5},{5,9},{9,13},{13,1},{2,6},{6,10},{... | collective-permute-start | bytes 565256 | tf_op jit(solution)/shard_map/ppermute | solution.py:204
  108.3 8.8 %collective-permute-start.13 = (bf16[2,368,128]{2,1,0:T(8,128)(2,1)S(1)}, bf16[2,368,128]{2,1,0:T(8,128)(2,1)S(1)}, u32[]{:S(2)}, u32[]{:S(2)}) collective-permute-start(bf16[2,368,128]{2,1,0:T(8,128)(2,1)S(1)} %get-tuple-element.41), channel_id=1, source_target_pairs={{0,12},{4,0},{8,4},{12,8},{1,13},{5,1},{9,5},{13,9},{2,14},{6,2},{... | collective-permute-start | bytes 565256 | tf_op jit(solution)/shard_map/ppermute | solution.py:204
  113.4 9.0 %collective-permute-start.12 = (bf16[2,368,128]{2,1,0:T(8,128)(2,1)S(1)}, bf16[2,368,128]{2,1,0:T(8,128)(2,1)S(1)}, u32[]{:S(2)}, u32[]{:S(2)}) collective-permute-start(bf16[2,368,128]{2,1,0:T(8,128)(2,1)S(1)} %get-tuple-element.42), channel_id=1, source_target_pairs={{0,8},{4,12},{8,0},{12,4},{1,9},{5,13},{9,1},{13,5},{2,10},{6,14},... | collective-permute-start | bytes 565256 | tf_op jit(solution)/shard_map/ppermute | solution.py:204
  122.5 36.9 %copy-start.3 = (f32[2,320]{1,0:T(2,128)S(1)}, f32[2,320]{1,0:T(2,128)}, u32[]{:S(2)}) copy-start(f32[2,320]{1,0:T(2,128)} %col_moments_ref.1) | copy-start | bytes 7684
  122.6 18.0 %collective-permute-start.14 = (bf16[368,128]{1,0:T(8,128)(2,1)S(1)}, bf16[368,128]{1,0:T(8,128)(2,1)S(1)}, u32[]{:S(2)}, u32[]{:S(2)}) collective-permute-start(bf16[368,128]{1,0:T(8,128)(2,1)S(1)} %get-tuple-element.45), channel_id=1, source_target_pairs={{0,0},{2,2},{4,128},{6,130},{8,8},{10,10},{12,136},{14,138},{128,4... | collective-permute-start | bytes 282632 | tf_op jit(solution)/shard_map/ppermute | solution.py:261
  134.4 10.4 %collective-permute-start.9 = (bf16[64,640]{1,0:T(8,128)(2,1)S(1)}, bf16[64,640]{1,0:T(8,128)(2,1)S(1)}, u32[]{:S(2)}, u32[]{:S(2)}) collective-permute-start(bf16[64,640]{1,0:T(8,128)(2,1)S(1)} %fusion.13), channel_id=1, source_target_pairs={{0,256},{256,0},{1,257},{257,1},{2,258},{258,2},{3,259},{259,3},{4... | collective-permute-start | bytes 245768 | tf_op jit(solution)/shard_map/ppermute | solution.py:208
  145.5 13.9 %all-to-all-start.2 = ((f32[32,8,128]{2,1,0:T(8,128)}), f32[32,8,128]{2,1,0:T(8,128)S(1)}, u32[]{:S(2)}, u32[]{:S(2)}) async-start(f32[32,8,128]{2,1,0:T(8,128)} %get-tuple-element.28), calls=%async_computation.2 | async-start | bytes 262144 | tf_op jit(solution)/shard_map/all_to_all | solution.py:270
  150.1 18.9 %collective-permute-start.15 = (bf16[368,128]{1,0:T(8,128)(2,1)S(1)}, bf16[368,128]{1,0:T(8,128)(2,1)S(1)}, u32[]{:S(2)}, u32[]{:S(2)}) collective-permute-start(bf16[368,128]{1,0:T(8,128)(2,1)S(1)} %get-tuple-element.46), channel_id=1, source_target_pairs={{0,2},{2,0},{4,130},{6,128},{8,10},{10,8},{12,138},{14,136},{128,6... | collective-permute-start | bytes 282632 | tf_op jit(solution)/shard_map/ppermute | solution.py:262
  160.2 18.4 %all-to-all-start.3 = ((f32[16,8,128]{2,1,0:T(8,128)}), f32[16,8,128]{2,1,0:T(8,128)S(1)}, u32[]{:S(2)}, u32[]{:S(2)}) async-start(f32[16,8,128]{2,1,0:T(8,128)} %get-tuple-element.30), calls=%async_computation.3 | async-start | bytes 131072 | tf_op jit(solution)/shard_map/all_to_all | solution.py:276

commit v6 on v4

--- a/solution.py
+++ b/solution.py
@@ -260,7 +260,6 @@
     near = lax.ppermute(total[0], PLANE, home_pairs(0))
     far = lax.ppermute(total[1], PLANE, home_pairs(1))
     parts, near = barrier((parts, near))
-    input_grad = (near.astype(F32) + far.astype(F32)).astype(BF16)
 
     stats, half_moments, hidden = barrier((stats, 0.5 * row_moments, hidden))
     own, payload, rows = call(
@@ -273,6 +272,8 @@
         10**6, received, rows, col_moments,
     )
     received = lax.all_to_all(payload, MP, 0, 0, tiled=True)
+    received, near, far = barrier((received, near, far))
+    input_grad = (near.astype(F32) + far.astype(F32)).astype(BF16)
     weight_step, new_rows = call(
         step_kernel, [struct((2, ROWS, COLS)), struct((2, ROWS))], 10**6, received, own, kept, half_moments, cols
     )

time: 177 us -> 183 us (1.034)
  the two profiles are of different devices: /device:TPU:1 before, /device:TPU:51 now
where the time goes in v6:
time: 183 us; the launch traced here: 182 us
  starting transfers between devices  79.1 us (43%)
  waiting for transfers between devices  65.7 us (36%)
  blocking collectives  17.5 us (10%)
  Pallas kernels  10 us (5%)
  other arithmetic  4.51 us (2%)
  local copies, waits for them, and re-layouts  4.31 us (2%)
    ppermute x5, waiting for transfers between devices, exchange(): return lax.ppermute(values, axis, [(0, 1), (1, 0)])  23.8 us
    ppermute x6, starting transfers between devices, x_shift(): lax.ppermute(values, 'x', [(i, (i + step) % N_X) for i in range(N_X)])  19.6 us
    all_to_all x1, blocking collectives, shards(): received = lax.all_to_all(payload, DP, 0, 0, tiled=True)  17.5 us
    ppermute x5, starting transfers between devices, exchange(): return lax.ppermute(values, axis, [(0, 1), (1, 0)])  17.1 us
    ppermute x1, waiting for transfers between devices, shards(): far = lax.ppermute(total[1], PLANE, home_pairs(1))  14.6 us
    all_to_all x1, starting transfers between devices, shards(): received = lax.all_to_all(payload, MP, 0, 0, tiled=True)  13.7 us
    all_to_all x1, starting transfers between devices, spread(): lax.all_to_all(jnp.broadcast_to(values[None], (size,) + values.shape), ax...  10.2 us
    pallas_call x8, Pallas kernels, call(): pl.pallas_call(kernel, out_shape=out_shape, in_specs=specs, out_specs=jax...  10 us
  transfers between devices with their start and end apart: 18, of which 14 were waited for; matrix products, arithmetic and copies ran while one was open for 1% of the time, Pallas kernels for 3%

profile of v6, /device:TPU:51, one launch (start us, length us, event | category | flops | bytes accessed | tf_op | source)
XLA Modules:
  0.0 182.1 jit_solution(1136816239177694836)
XLA Ops:
  0.6 1.1 multiply_reduce_fusion
  1.9 3.8 %collective-permute-start = (bf16[64,640]{1,0:T(8,128)(2,1)S(1)}, bf16[64,640]{1,0:T(8,128)(2,1)S(1)}, u32[]{:S(2)}, u32[]{:S(2)}) collective-permute-start(bf16[64,640]{1,0:T(8,128)(2,1)S(1)} %pad_maximum_fusion.4), channel_id=1, source_target_pairs={{0,256},{256,0},{1,257},{257,1},{2,258},{258,2},{3,259},{259,3},{4... | collective-permute-start | bytes 245768 | tf_op jit(solution)/shard_map/ppermute | solution.py:210
  5.6 2.3 %collective-permute-start.1 = (bf16[368,128]{1,0:T(8,128)(2,1)}, bf16[368,128]{1,0:T(8,128)(2,1)S(1)}, u32[]{:S(2)}, u32[]{:S(2)}) collective-permute-start(bf16[368,128]{1,0:T(8,128)(2,1)} %param.5), channel_id=1, source_target_pairs={{0,0},{2,2},{4,128},{6,130},{8,8},{10,10},{12,136},{14,138},{128,4... | collective-permute-start | bytes 282632 | tf_op jit(solution)/shard_map/ppermute | solution.py:217
  7.9 1.4 collective-permute-done
  9.5 2.6 %collective-permute-done.1 = bf16[368,128]{1,0:T(8,128)(2,1)S(1)} collective-permute-done((bf16[368,128]{1,0:T(8,128)(2,1)}, bf16[368,128]{1,0:T(8,128)(2,1)S(1)}, u32[]{:S(2)}, u32[]{:S(2)}) %collective-permute-start.1) | collective-permute-done | bytes 94240 | tf_op jit(solution)/shard_map/ppermute | solution.py:217
  12.1 1.2 broadcast_in_dim.4
  13.3 10.2 %all-to-all-start = ((bf16[8,2,64,640]{3,2,1,0:T(8,128)(2,1)}), bf16[8,2,64,640]{3,2,1,0:T(8,128)(2,1)S(1)}, u32[]{:S(2)}, u32[]{:S(2)}) async-start(bf16[8,2,64,640]{3,2,1,0:T(8,128)(2,1)} %broadcast_in_dim.4), calls=%async_computation | async-start | bytes 2621440 | tf_op jit(solution)/shard_map/all_to_all | solution.py:191
  23.5 3.8 %collective-permute-start.2 = (bf16[368,128]{1,0:T(8,128)(2,1)S(1)}, bf16[368,128]{1,0:T(8,128)(2,1)S(1)}, u32[]{:S(2)}, u32[]{:S(2)}) collective-permute-start(bf16[368,128]{1,0:T(8,128)(2,1)S(1)} %copy-done.7), channel_id=1, source_target_pairs={{0,2},{2,0},{4,130},{6,128},{8,10},{10,8},{12,138},{14,136},{128,6... | collective-permute-start | bytes 282632 | tf_op jit(solution)/shard_map/ppermute | solution.py:218
  27.3 7.7 %collective-permute-done.2 = bf16[368,128]{1,0:T(8,128)(2,1)S(1)} collective-permute-done((bf16[368,128]{1,0:T(8,128)(2,1)S(1)}, bf16[368,128]{1,0:T(8,128)(2,1)S(1)}, u32[]{:S(2)}, u32[]{:S(2)}) %collective-permute-start.2) | collective-permute-done | bytes 94240 | tf_op jit(solution)/shard_map/ppermute | solution.py:218
  35.0 3.9 %collective-permute-start.4 = (bf16[2,368,128]{2,1,0:T(8,128)(2,1)S(1)}, bf16[2,368,128]{2,1,0:T(8,128)(2,1)S(1)}, u32[]{:S(2)}, u32[]{:S(2)}) collective-permute-start(bf16[2,368,128]{2,1,0:T(8,128)(2,1)S(1)} %get-tuple-element.54), channel_id=1, source_target_pairs={{0,8},{4,12},{8,0},{12,4},{1,9},{5,13},{9,1},{13,5},{2,10},{6,14},... | collective-permute-start | bytes 565256 | tf_op jit(solution)/shard_map/ppermute | solution.py:206
  38.9 1.9 %collective-permute-start.3 = (bf16[2,368,128]{2,1,0:T(8,128)(2,1)S(1)}, bf16[2,368,128]{2,1,0:T(8,128)(2,1)S(1)}, u32[]{:S(2)}, u32[]{:S(2)}) collective-permute-start(bf16[2,368,128]{2,1,0:T(8,128)(2,1)S(1)} %get-tuple-element.54), channel_id=1, source_target_pairs={{0,4},{4,8},{8,12},{12,0},{1,5},{5,9},{9,13},{13,1},{2,6},{6,10},{... | collective-permute-start | bytes 565256 | tf_op jit(solution)/shard_map/ppermute | solution.py:206
  40.8 3.4 %collective-permute-start.5 = (bf16[2,368,128]{2,1,0:T(8,128)(2,1)S(1)}, bf16[2,368,128]{2,1,0:T(8,128)(2,1)S(1)}, u32[]{:S(2)}, u32[]{:S(2)}) collective-permute-start(bf16[2,368,128]{2,1,0:T(8,128)(2,1)S(1)} %get-tuple-element.54), channel_id=1, source_target_pairs={{0,12},{4,0},{8,4},{12,8},{1,13},{5,1},{9,5},{13,9},{2,14},{6,2},{... | collective-permute-start | bytes 565256 | tf_op jit(solution)/shard_map/ppermute | solution.py:206
  44.2 1.3 collective-permute-done.3
  45.5 1.9 %collective-permute-done.5 = bf16[2,368,128]{2,1,0:T(8,128)(2,1)S(1)} collective-permute-done((bf16[2,368,128]{2,1,0:T(8,128)(2,1)S(1)}, bf16[2,368,128]{2,1,0:T(8,128)(2,1)S(1)}, u32[]{:S(2)}, u32[]{:S(2)}) %collective-permute-start.5) | collective-permute-done | bytes 188448 | tf_op jit(solution)/shard_map/ppermute | solution.py:206
  47.5 4.6 %collective-permute-start.6 = (bf16[4,2,368,128]{3,2,1,0:T(8,128)(2,1)S(1)}, bf16[4,2,368,128]{3,2,1,0:T(8,128)(2,1)S(1)}, u32[]{:S(2)}, u32[]{:S(2)}) collective-permute-start(bf16[4,2,368,128]{3,2,1,0:T(8,128)(2,1)S(1)} %pad_maximum_fusion.own_ref), channel_id=1, source_target_pairs={{0,1},{1,0},{2,3},{3,2},{4,5},{5,4},{6,7},{7,6},{8,9},{9,8},{10,11... | collective-permute-start | bytes 2261000 | tf_op jit(solution)/shard_map/ppermute | solution.py:210
  52.2 1.8 collective-permute-done.6.other_ref
  53.9 4.3 %all-to-all-done = bf16[8,2,64,640]{3,2,1,0:T(8,128)(2,1)S(1)} async-done(((bf16[8,2,64,640]{3,2,1,0:T(8,128)(2,1)}), bf16[8,2,64,640]{3,2,1,0:T(8,128)(2,1)S(1)}, u32[]{:S(2)}, u32[]{:S(2)}) %all-to-all-start) | async-done | bytes 1310752 | tf_op jit(solution)/shard_map/all_to_all | solution.py:191
  58.3 1.3 shard_map.85
  59.6 1.9 %collective-permute-start.7 = (bf16[368,640]{1,0:T(8,128)(2,1)S(1)}, bf16[368,640]{1,0:T(8,128)(2,1)}, u32[]{:S(2)}, u32[]{:S(2)}) collective-permute-start(bf16[368,640]{1,0:T(8,128)(2,1)S(1)} %shard_map.85), channel_id=1, source_target_pairs={{0,128},{128,0},{1,129},{129,1},{2,130},{130,2},{3,131},{131,3},{4... | collective-permute-start | bytes 1413128 | tf_op jit(solution)/shard_map/ppermute | solution.py:210
  61.6 0.9 copy.9
  62.5 1.3 shard_map.84
  63.8 9.7 %collective-permute-done.7 = bf16[368,640]{1,0:T(8,128)(2,1)} collective-permute-done((bf16[368,640]{1,0:T(8,128)(2,1)S(1)}, bf16[368,640]{1,0:T(8,128)(2,1)}, u32[]{:S(2)}, u32[]{:S(2)}) %collective-permute-start.7) | collective-permute-done | bytes 471072 | tf_op jit(solution)/shard_map/ppermute | solution.py:210
  73.5 1.1 add_multiply_fusion
  75.3 2.2 %collective-permute-start.8 = (bf16[368,640]{1,0:T(8,128)(2,1)S(1)}, bf16[368,640]{1,0:T(8,128)(2,1)S(1)}, u32[]{:S(2)}, u32[]{:S(2)}) collective-permute-start(bf16[368,640]{1,0:T(8,128)(2,1)S(1)} %pad_maximum_fusion.1.hidden_ref.mine_ref), channel_id=1, source_target_pairs={{0,128},{128,0},{1,129},{129,1},{2,130},{130,2},{3,131},{131,3},{4... | collective-permute-start | bytes 1413128 | tf_op jit(solution)/shard_map/ppermute | solution.py:210
  77.5 1.5 shard_map.86.mine_ref
  79.0 9.1 %collective-permute-done.8.hidden_ref.pair_ref = bf16[368,640]{1,0:T(8,128)(2,1)S(1)} collective-permute-done((bf16[368,640]{1,0:T(8,128)(2,1)S(1)}, bf16[368,640]{1,0:T(8,128)(2,1)S(1)}, u32[]{:S(2)}, u32[]{:S(2)}) %collective-permute-start.8) | collective-permute-done | bytes 471072 | tf_op jit(solution)/shard_map/ppermute | solution.py:210
  88.1 1.5 shard_map.87
  89.6 1.1 copy-done
  90.7 7.4 %all-to-all-start.1 = ((bf16[16,64,640]{2,1,0:T(8,128)(2,1)}), bf16[16,64,640]{2,1,0:T(8,128)(2,1)S(1)}, u32[]{:S(2)}, u32[]{:S(2)}) async-start(bf16[16,64,640]{2,1,0:T(8,128)(2,1)} %bitcast.41), calls=%async_computation.1 | async-start | bytes 2621440 | tf_op jit(solution)/shard_map/all_to_all | solution.py:251
  98.1 1.0 copy-done.2
  99.1 1.9 %shard_map.88 = (bf16[4,2,368,128]{3,2,1,0:T(8,128)(2,1)S(1)}, bf16[4,2,368,128]{3,2,1,0:T(8,128)(2,1)S(1)}) custom-call(s32[4]{0:T(128)S(1)} %pad_add_fusion.place_ref, bf16[368,640]{1,0:T(8,128)(2,1)S(1)} %pad_maximum_fusion.1.hidden_ref.mine_ref, bf16[368,640]{1,0:T(8,128)(2,1)S(1)} %copy-done.2, bf16[4,2,2,64,640]{4,3,2,1,0:T(8,128)(2,1)S(1)} %bitcast.40), custom_call_target="tpu_custom_call" | custom-call | flops 964689920 | bytes 4194304 | tf_op jit(solution)/shard_map/pallas_call | solution.py:175
  101.0 4.6 %collective-permute-start.9 = (bf16[4,2,368,128]{3,2,1,0:T(8,128)(2,1)S(1)}, bf16[4,2,368,128]{3,2,1,0:T(8,128)(2,1)S(1)}, u32[]{:S(2)}, u32[]{:S(2)}) collective-permute-start(bf16[4,2,368,128]{3,2,1,0:T(8,128)(2,1)S(1)} %get-tuple-element.27), channel_id=1, source_target_pairs={{0,1},{1,0},{2,3},{3,2},{4,5},{5,4},{6,7},{7,6},{8,9},{9,8},{10,11... | collective-permute-start | bytes 2261000 | tf_op jit(solution)/shard_map/ppermute | solution.py:210
  105.6 1.8 %collective-permute-done.9 = bf16[4,2,368,128]{3,2,1,0:T(8,128)(2,1)S(1)} collective-permute-done((bf16[4,2,368,128]{3,2,1,0:T(8,128)(2,1)S(1)}, bf16[4,2,368,128]{3,2,1,0:T(8,128)(2,1)S(1)}, u32[]{:S(2)}, u32[]{:S(2)}) %collective-permute-start.9) | collective-permute-done | bytes 753696 | tf_op jit(solution)/shard_map/ppermute | solution.py:210
  107.8 2.8 %collective-permute-start.10 = (bf16[2,368,128]{2,1,0:T(8,128)(2,1)S(1)}, bf16[2,368,128]{2,1,0:T(8,128)(2,1)S(1)}, u32[]{:S(2)}, u32[]{:S(2)}) collective-permute-start(bf16[2,368,128]{2,1,0:T(8,128)(2,1)S(1)} %get-tuple-element.46), channel_id=1, source_target_pairs={{0,4},{4,8},{8,12},{12,0},{1,5},{5,9},{9,13},{13,1},{2,6},{6,10},{... | collective-permute-start | bytes 565256 | tf_op jit(solution)/shard_map/ppermute | solution.py:206
  110.6 2.5 %collective-permute-start.12 = (bf16[2,368,128]{2,1,0:T(8,128)(2,1)S(1)}, bf16[2,368,128]{2,1,0:T(8,128)(2,1)S(1)}, u32[]{:S(2)}, u32[]{:S(2)}) collective-permute-start(bf16[2,368,128]{2,1,0:T(8,128)(2,1)S(1)} %get-tuple-element.47), channel_id=1, source_target_pairs={{0,12},{4,0},{8,4},{12,8},{1,13},{5,1},{9,5},{13,9},{2,14},{6,2},{... | collective-permute-start | bytes 565256 | tf_op jit(solution)/shard_map/ppermute | solution.py:206
  113.1 5.2 %collective-permute-start.11 = (bf16[2,368,128]{2,1,0:T(8,128)(2,1)S(1)}, bf16[2,368,128]{2,1,0:T(8,128)(2,1)S(1)}, u32[]{:S(2)}, u32[]{:S(2)}) collective-permute-start(bf16[2,368,128]{2,1,0:T(8,128)(2,1)S(1)} %get-tuple-element.48), channel_id=1, source_target_pairs={{0,8},{4,12},{8,0},{12,4},{1,9},{5,13},{9,1},{13,5},{2,10},{6,14},... | collective-permute-start | bytes 565256 | tf_op jit(solution)/shard_map/ppermute | solution.py:206
  118.4 1.2 collective-permute-done.12
  119.6 4.9 %collective-permute-done.11 = bf16[2,368,128]{2,1,0:T(8,128)(2,1)S(1)} collective-permute-done((bf16[2,368,128]{2,1,0:T(8,128)(2,1)S(1)}, bf16[2,368,128]{2,1,0:T(8,128)(2,1)S(1)}, u32[]{:S(2)}, u32[]{:S(2)}) %collective-permute-start.11) | collective-permute-done | bytes 188448 | tf_op jit(solution)/shard_map/ppermute | solution.py:206
  124.6 3.1 %collective-permute-start.13 = (bf16[368,128]{1,0:T(8,128)(2,1)S(1)}, bf16[368,128]{1,0:T(8,128)(2,1)S(1)}, u32[]{:S(2)}, u32[]{:S(2)}) collective-permute-start(bf16[368,128]{1,0:T(8,128)(2,1)S(1)} %get-tuple-element.52), channel_id=1, source_target_pairs={{0,0},{2,2},{4,128},{6,130},{8,8},{10,10},{12,136},{14,138},{128,4... | collective-permute-start | bytes 282632 | tf_op jit(solution)/shard_map/ppermute | solution.py:260
  127.8 3.4 %collective-permute-done.13 = bf16[368,128]{1,0:T(8,128)(2,1)S(1)} collective-permute-done((bf16[368,128]{1,0:T(8,128)(2,1)S(1)}, bf16[368,128]{1,0:T(8,128)(2,1)S(1)}, u32[]{:S(2)}, u32[]{:S(2)}) %collective-permute-start.13) | collective-permute-done | bytes 94240 | tf_op jit(solution)/shard_map/ppermute | solution.py:260
  131.2 0.6 shard_map.89
  131.8 17.5 %all_to_all.20.received_ref = f32[32,8,128]{2,1,0:T(8,128)S(1)} all-to-all(f32[32,8,128]{2,1,0:T(8,128)S(1)} %get-tuple-element.30), channel_id=1, replica_groups=mesh['yh'=2,'yl'=2,'z'=8,'x'=4,'yhi'=2,'core'=2] {'yh','yl','z'}, dimensions={0} | all-to-all | bytes 262144 | tf_op jit(solution)/shard_map/all_to_all | solution.py:268
  149.3 0.8 shard_map.90
  150.1 13.7 %all-to-all-start.3 = ((f32[16,8,128]{2,1,0:T(8,128)}), f32[16,8,128]{2,1,0:T(8,128)S(1)}, u32[]{:S(2)}, u32[]{:S(2)}) async-start(f32[16,8,128]{2,1,0:T(8,128)} %get-tuple-element.32), calls=%async_computation.3 | async-start | bytes 131072 | tf_op jit(solution)/shard_map/all_to_all | solution.py:274
  163.9 1.9 %collective-permute-start.14 = (bf16[368,128]{1,0:T(8,128)(2,1)S(1)}, bf16[368,128]{1,0:T(8,128)(2,1)S(1)}, u32[]{:S(2)}, u32[]{:S(2)}) collective-permute-start(bf16[368,128]{1,0:T(8,128)(2,1)S(1)} %get-tuple-element.51), channel_id=1, source_target_pairs={{0,2},{2,0},{4,130},{6,128},{8,10},{10,8},{12,138},{14,136},{128,6... | collective-permute-start | bytes 282632 | tf_op jit(solution)/shard_map/ppermute | solution.py:261
  165.8 14.6 %collective-permute-done.14 = bf16[368,128]{1,0:T(8,128)(2,1)S(1)} collective-permute-done((bf16[368,128]{1,0:T(8,128)(2,1)S(1)}, bf16[368,128]{1,0:T(8,128)(2,1)S(1)}, u32[]{:S(2)}, u32[]{:S(2)}) %collective-permute-start.14) | collective-permute-done | bytes 94240 | tf_op jit(solution)/shard_map/ppermute | solution.py:261
  180.3 0.7 add_convert_fusion.1
  181.0 1.0 shard_map.91
  (34 shorter events, 1.7 us)
Async XLA Ops:
  1.9 7.5 %collective-permute-start = (bf16[64,640]{1,0:T(8,128)(2,1)S(1)}, bf16[64,640]{1,0:T(8,128)(2,1)S(1)}, u32[]{:S(2)}, u32[]{:S(2)}) collective-permute-start(bf16[64,640]{1,0:T(8,128)(2,1)S(1)} %pad_maximum_fusion.4), channel_id=1, source_target_pairs={{0,256},{256,0},{1,257},{257,1},{2,258},{258,2},{3,259},{259,3},{4... | collective-permute-start | bytes 245768 | tf_op jit(solution)/shard_map/ppermute | solution.py:210
  5.6 6.4 %collective-permute-start.1 = (bf16[368,128]{1,0:T(8,128)(2,1)}, bf16[368,128]{1,0:T(8,128)(2,1)S(1)}, u32[]{:S(2)}, u32[]{:S(2)}) collective-permute-start(bf16[368,128]{1,0:T(8,128)(2,1)} %param.5), channel_id=1, source_target_pairs={{0,0},{2,2},{4,128},{6,130},{8,8},{10,10},{12,136},{14,138},{128,4... | collective-permute-start | bytes 282632 | tf_op jit(solution)/shard_map/ppermute | solution.py:217
  13.3 10.2 %copy-start.7 = (bf16[368,128]{1,0:T(8,128)(2,1)S(1)}, bf16[368,128]{1,0:T(8,128)(2,1)}, u32[]{:S(2)}) copy-start(bf16[368,128]{1,0:T(8,128)(2,1)} %param.5) | copy-start | bytes 282628
  13.3 45.0 %all-to-all-start = ((bf16[8,2,64,640]{3,2,1,0:T(8,128)(2,1)}), bf16[8,2,64,640]{3,2,1,0:T(8,128)(2,1)S(1)}, u32[]{:S(2)}, u32[]{:S(2)}) async-start(bf16[8,2,64,640]{3,2,1,0:T(8,128)(2,1)} %broadcast_in_dim.4), calls=%async_computation | async-start | bytes 2621440 | tf_op jit(solution)/shard_map/all_to_all | solution.py:191
  23.5 11.5 %collective-permute-start.2 = (bf16[368,128]{1,0:T(8,128)(2,1)S(1)}, bf16[368,128]{1,0:T(8,128)(2,1)S(1)}, u32[]{:S(2)}, u32[]{:S(2)}) collective-permute-start(bf16[368,128]{1,0:T(8,128)(2,1)S(1)} %copy-done.7), channel_id=1, source_target_pairs={{0,2},{2,0},{4,130},{6,128},{8,10},{10,8},{12,138},{14,136},{128,6... | collective-permute-start | bytes 282632 | tf_op jit(solution)/shard_map/ppermute | solution.py:218
  35.0 9.2 %collective-permute-start.4 = (bf16[2,368,128]{2,1,0:T(8,128)(2,1)S(1)}, bf16[2,368,128]{2,1,0:T(8,128)(2,1)S(1)}, u32[]{:S(2)}, u32[]{:S(2)}) collective-permute-start(bf16[2,368,128]{2,1,0:T(8,128)(2,1)S(1)} %get-tuple-element.54), channel_id=1, source_target_pairs={{0,8},{4,12},{8,0},{12,4},{1,9},{5,13},{9,1},{13,5},{2,10},{6,14},... | collective-permute-start | bytes 565256 | tf_op jit(solution)/shard_map/ppermute | solution.py:206
  38.9 6.6 %collective-permute-start.3 = (bf16[2,368,128]{2,1,0:T(8,128)(2,1)S(1)}, bf16[2,368,128]{2,1,0:T(8,128)(2,1)S(1)}, u32[]{:S(2)}, u32[]{:S(2)}) collective-permute-start(bf16[2,368,128]{2,1,0:T(8,128)(2,1)S(1)} %get-tuple-element.54), channel_id=1, source_target_pairs={{0,4},{4,8},{8,12},{12,0},{1,5},{5,9},{9,13},{13,1},{2,6},{6,10},{... | collective-permute-start | bytes 565256 | tf_op jit(solution)/shard_map/ppermute | solution.py:206
  40.8 6.6 %collective-permute-start.5 = (bf16[2,368,128]{2,1,0:T(8,128)(2,1)S(1)}, bf16[2,368,128]{2,1,0:T(8,128)(2,1)S(1)}, u32[]{:S(2)}, u32[]{:S(2)}) collective-permute-start(bf16[2,368,128]{2,1,0:T(8,128)(2,1)S(1)} %get-tuple-element.54), channel_id=1, source_target_pairs={{0,12},{4,0},{8,4},{12,8},{1,13},{5,1},{9,5},{13,9},{2,14},{6,2},{... | collective-permute-start | bytes 565256 | tf_op jit(solution)/shard_map/ppermute | solution.py:206
  47.5 6.4 %collective-permute-start.6 = (bf16[4,2,368,128]{3,2,1,0:T(8,128)(2,1)S(1)}, bf16[4,2,368,128]{3,2,1,0:T(8,128)(2,1)S(1)}, u32[]{:S(2)}, u32[]{:S(2)}) collective-permute-start(bf16[4,2,368,128]{3,2,1,0:T(8,128)(2,1)S(1)} %pad_maximum_fusion.own_ref), channel_id=1, source_target_pairs={{0,1},{1,0},{2,3},{3,2},{4,5},{5,4},{6,7},{7,6},{8,9},{9,8},{10,11... | collective-permute-start | bytes 2261000 | tf_op jit(solution)/shard_map/ppermute | solution.py:210
  58.3 3.3 %copy-start.5 = (bf16[368,320]{0,1:T(8,128)(2,1)S(1)}, bf16[368,320]{0,1:T(8,128)(2,1)}, u32[]{:S(2)}) copy-start(bf16[368,320]{0,1:T(8,128)(2,1)} %param.6) | copy-start | bytes 706564
  59.6 13.9 %collective-permute-start.7 = (bf16[368,640]{1,0:T(8,128)(2,1)S(1)}, bf16[368,640]{1,0:T(8,128)(2,1)}, u32[]{:S(2)}, u32[]{:S(2)}) collective-permute-start(bf16[368,640]{1,0:T(8,128)(2,1)S(1)} %shard_map.85), channel_id=1, source_target_pairs={{0,128},{128,0},{1,129},{129,1},{2,130},{130,2},{3,131},{131,3},{4... | collective-permute-start | bytes 1413128 | tf_op jit(solution)/shard_map/ppermute | solution.py:210
  63.8 10.8 %copy-start.4 = (bf16[368,320]{1,0:T(8,128)(2,1)S(1)}, bf16[368,320]{1,0:T(8,128)(2,1)}, u32[]{:S(2)}) copy-start(bf16[368,320]{1,0:T(8,128)(2,1)} %copy.9) | copy-start | bytes 706564
  75.3 12.8 %collective-permute-start.8 = (bf16[368,640]{1,0:T(8,128)(2,1)S(1)}, bf16[368,640]{1,0:T(8,128)(2,1)S(1)}, u32[]{:S(2)}, u32[]{:S(2)}) collective-permute-start(bf16[368,640]{1,0:T(8,128)(2,1)S(1)} %pad_maximum_fusion.1.hidden_ref.mine_ref), channel_id=1, source_target_pairs={{0,128},{128,0},{1,129},{129,1},{2,130},{130,2},{3,131},{131,3},{4... | collective-permute-start | bytes 1413128 | tf_op jit(solution)/shard_map/ppermute | solution.py:210
  88.1 1.5 copy-start.1
  89.6 1.1 copy-start
  90.7 40.4 %all-to-all-start.1 = ((bf16[16,64,640]{2,1,0:T(8,128)(2,1)}), bf16[16,64,640]{2,1,0:T(8,128)(2,1)S(1)}, u32[]{:S(2)}, u32[]{:S(2)}) async-start(bf16[16,64,640]{2,1,0:T(8,128)(2,1)} %bitcast.41), calls=%async_computation.1 | async-start | bytes 2621440 | tf_op jit(solution)/shard_map/all_to_all | solution.py:251
  98.1 1.0 copy-start.2
  101.0 6.4 %collective-permute-start.9 = (bf16[4,2,368,128]{3,2,1,0:T(8,128)(2,1)S(1)}, bf16[4,2,368,128]{3,2,1,0:T(8,128)(2,1)S(1)}, u32[]{:S(2)}, u32[]{:S(2)}) collective-permute-start(bf16[4,2,368,128]{3,2,1,0:T(8,128)(2,1)S(1)} %get-tuple-element.27), channel_id=1, source_target_pairs={{0,1},{1,0},{2,3},{3,2},{4,5},{5,4},{6,7},{7,6},{8,9},{9,8},{10,11... | collective-permute-start | bytes 2261000 | tf_op jit(solution)/shard_map/ppermute | solution.py:210
  107.5 10.8 %copy-start.6 = (f32[2,64]{1,0:T(2,128)S(1)}, f32[2,64]{1,0:T(2,128)}, u32[]{:S(2)}) copy-start(f32[2,64]{1,0:T(2,128)} %param.8) | copy-start | bytes 1540
  107.7 41.6 %copy-start.3 = (f32[2,320]{1,0:T(2,128)S(1)}, f32[2,320]{1,0:T(2,128)}, u32[]{:S(2)}) copy-start(f32[2,320]{1,0:T(2,128)} %col_moments_ref.1) | copy-start | bytes 7684
  107.8 10.6 %collective-permute-start.10 = (bf16[2,368,128]{2,1,0:T(8,128)(2,1)S(1)}, bf16[2,368,128]{2,1,0:T(8,128)(2,1)S(1)}, u32[]{:S(2)}, u32[]{:S(2)}) collective-permute-start(bf16[2,368,128]{2,1,0:T(8,128)(2,1)S(1)} %get-tuple-element.46), channel_id=1, source_target_pairs={{0,4},{4,8},{8,12},{12,0},{1,5},{5,9},{9,13},{13,1},{2,6},{6,10},{... | collective-permute-start | bytes 565256 | tf_op jit(solution)/shard_map/ppermute | solution.py:206
  110.6 9.0 %collective-permute-start.12 = (bf16[2,368,128]{2,1,0:T(8,128)(2,1)S(1)}, bf16[2,368,128]{2,1,0:T(8,128)(2,1)S(1)}, u32[]{:S(2)}, u32[]{:S(2)}) collective-permute-start(bf16[2,368,128]{2,1,0:T(8,128)(2,1)S(1)} %get-tuple-element.47), channel_id=1, source_target_pairs={{0,12},{4,0},{8,4},{12,8},{1,13},{5,1},{9,5},{13,9},{2,14},{6,2},{... | collective-permute-start | bytes 565256 | tf_op jit(solution)/shard_map/ppermute | solution.py:206
  113.1 11.4 %collective-permute-start.11 = (bf16[2,368,128]{2,1,0:T(8,128)(2,1)S(1)}, bf16[2,368,128]{2,1,0:T(8,128)(2,1)S(1)}, u32[]{:S(2)}, u32[]{:S(2)}) collective-permute-start(bf16[2,368,128]{2,1,0:T(8,128)(2,1)S(1)} %get-tuple-element.48), channel_id=1, source_target_pairs={{0,8},{4,12},{8,0},{12,4},{1,9},{5,13},{9,1},{13,5},{2,10},{6,14},... | collective-permute-start | bytes 565256 | tf_op jit(solution)/shard_map/ppermute | solution.py:206
  124.6 6.5 %collective-permute-start.13 = (bf16[368,128]{1,0:T(8,128)(2,1)S(1)}, bf16[368,128]{1,0:T(8,128)(2,1)S(1)}, u32[]{:S(2)}, u32[]{:S(2)}) collective-permute-start(bf16[368,128]{1,0:T(8,128)(2,1)S(1)} %get-tuple-element.52), channel_id=1, source_target_pairs={{0,0},{2,2},{4,128},{6,130},{8,8},{10,10},{12,136},{14,138},{128,4... | collective-permute-start | bytes 282632 | tf_op jit(solution)/shard_map/ppermute | solution.py:260
  150.1 30.2 %all-to-all-start.3 = ((f32[16,8,128]{2,1,0:T(8,128)}), f32[16,8,128]{2,1,0:T(8,128)S(1)}, u32[]{:S(2)}, u32[]{:S(2)}) async-start(f32[16,8,128]{2,1,0:T(8,128)} %get-tuple-element.32), calls=%async_computation.3 | async-start | bytes 131072 | tf_op jit(solution)/shard_map/all_to_all | solution.py:274
  163.9 16.5 %collective-permute-start.14 = (bf16[368,128]{1,0:T(8,128)(2,1)S(1)}, bf16[368,128]{1,0:T(8,128)(2,1)S(1)}, u32[]{:S(2)}, u32[]{:S(2)}) collective-permute-start(bf16[368,128]{1,0:T(8,128)(2,1)S(1)} %get-tuple-element.51), channel_id=1, source_target_pairs={{0,2},{2,0},{4,130},{6,128},{8,10},{10,8},{12,138},{14,136},{128,6... | collective-permute-start | bytes 282632 | tf_op jit(solution)/shard_map/ppermute | solution.py:261
